TPU v7x, 128 devices: a whole 4x4x4 slice. The times are simulated.
128 devices in a mesh: prow: 8 (over x, core), pcol: 16 (over z, y).
Axes of the slice: x: 4, y: 4, z: 4, core: 2. Of those that a mesh axis runs over, the one named last changes fastest.
Arguments:
- window: float32 [98304, 4096], P('prow', 'pcol'), as said below
- panel_index: int32 [1], replicated, may hold values from 0 to 15
Outputs:
- updated: float32 [98304, 4096], P('prow', 'pcol')
Inputs may be any that keep to these rules, and one draw needn't show every extreme that they name: `window`: entries whose matrix row equals their matrix column lie in 32 to 64; all others are of order one.
All inputs are finite; a program needn't handle non-finite values.
Results may differ from a plain program's by a relative error of at most 0.0027.
Values may be sent and summed in bfloat16 or wider, within the bound.
No kernel may reach another device: no remote copies, remote signals or barrier semaphores. Data moves between devices by JAX's collectives and lax.ppermute only.
A program may use at most 128 MiB of HBM per device.

v0:
```python
import jax
import jax.numpy as jnp
from jax import lax
from jax.sharding import PartitionSpec as P

NB = 128
LOOK = 16


def from_root(block, axis, holder):
    block = jnp.where(lax.axis_index(axis) == holder, block, jnp.zeros_like(block))
    return lax.psum(block, axis)


def body(window, panel_index):
    k = panel_index[0]
    grid_rows = lax.axis_size("prow")
    grid_cols = lax.axis_size("pcol")
    row_place = lax.axis_index("prow")
    col_place = lax.axis_index("pcol")
    rows_dev = window.shape[0]
    col_count = window.shape[1] // NB
    row_tile = jnp.arange(rows_dev) // NB * grid_rows + row_place
    local_panel = lax.dynamic_slice_in_dim(window, k // grid_cols * NB, NB, 1)
    tile = lax.dynamic_slice_in_dim(local_panel, k // grid_rows * NB, NB, 0)
    tile = from_root(tile.astype(jnp.bfloat16), "prow", k % grid_rows).astype(tile.dtype)
    factor = jnp.linalg.cholesky(tile)
    solved = jax.scipy.linalg.solve_triangular(factor, local_panel.T, lower=True).T
    low = solved.astype(jnp.bfloat16)
    placed = lax.dynamic_update_slice(
        jnp.zeros((rows_dev, NB), jnp.float32), factor, (k // grid_rows * NB, jnp.int32(0))
    )
    new_panel = jnp.where(
        (row_tile > k)[:, None], solved, jnp.where((row_tile == k)[:, None], placed, local_panel)
    )
    per_row = LOOK // grid_rows
    first_tile = k + 1 + jnp.remainder(row_place - (k + 1), grid_rows)
    look_start = first_tile // grid_rows * NB
    low = from_root(low, "pcol", k % grid_cols)
    look = lax.all_gather(
        lax.dynamic_slice_in_dim(low, look_start, per_row * NB, 0), "prow", axis=0, tiled=True
    )
    pieces = []
    for column_slot in range(col_count):
        global_col = column_slot * grid_cols + col_place
        owner_row = jnp.remainder(global_col, grid_rows)
        owner_first = k + 1 + jnp.remainder(owner_row - (k + 1), grid_rows)
        position = owner_row * per_row + (global_col - owner_first) // grid_rows
        position = jnp.clip(position, 0, LOOK - 1)
        look_tile = lax.dynamic_slice_in_dim(look, position * NB, NB, 0)
        update = lax.dot_general(
            low, look_tile, (((1,), (1,)), ((), ())), preferred_element_type=jnp.float32
        )
        active = (global_col > k) & (global_col <= k + LOOK)
        mask = active & (row_tile >= global_col)
        column = window[:, column_slot * NB : (column_slot + 1) * NB]
        changed = jnp.where(mask[:, None], column - update, column)
        changed = jnp.where(global_col == k, new_panel, changed)
        pieces.append(changed)
    return jnp.concatenate(pieces, axis=1)


def solution(mesh):
    return jax.shard_map(
        body,
        mesh=mesh,
        in_specs=(P("prow", "pcol"), P()),
        out_specs=P("prow", "pcol"),
        check_vma=False,
    )
```

profile of v0, /device:TPU:1, one launch (start us, length us, event | category | flops | bytes accessed | tf_op | source)
XLA Modules:
  0.0 248.8 jit_solution(13514916261246303500)
XLA Ops:
  7.2 13.6 %fusion.22 = (f32[12288,128]{1,0:T(8,128)}, f32[12288,128]{1,0:T(8,128)}, f32[12288,128]{1,0:T(8,128)}) fusion(f32[12288,256]{1,0:T(8,128)} %param.2, s32[]{:T(128)S(6)} %select_n.136), kind=kLoop, calls=%fused_computation.42 | loop fusion | bytes 37748740 | tf_op jit(solution)/shard_map/slice | solution.py:56
  20.8 1.0 dynamic_slice.16
  21.8 0.1 copy.11
  21.9 23.6 %psum.14 = bf16[128,128]{0,1:T(8,128)(2,1)S(1)} all-reduce(bf16[128,128]{0,1:T(8,128)(2,1)S(1)} %convert_select_fusion.1), channel_id=1, replica_groups=mesh['prow'=8,'pcol'=16] {'prow'}, use_global_device_ids=true, to_apply=%region_0.1 | all-reduce | flops 16384 | bytes 65536 | tf_op jit(solution)/shard_map/psum | solution.py:12
  45.5 0.1 copy.5
  45.7 11.7 %cholesky.16 = f32[128,128]{1,0:T(8,128)S(1)} custom-call(f32[128,128]{1,0:T(8,128)S(1)} %fusion.6), custom_call_target="Cholesky" | custom-call | tf_op jit(solution)/shard_map/jit(cholesky)/cholesky | solution.py:27
  57.4 0.6 compare_reduce_fusion
  58.1 0.7 select_bitcast_fusion
  58.7 0.1 copy.6
  58.8 6.5 %copy.10 = f32[12288,128]{0,1:T(8,128)} copy(f32[12288,128]{1,0:T(8,128)} %get-tuple-element.8) | data formatting | bytes 12582912
  65.4 9.8 %custom-call.7 = f32[1,128,128]{1,2,0:T(8,128)S(1)} custom-call(f32[1,128,128]{2,1,0:T(8,128)S(1)} %get-tuple-element.5), custom_call_target="InvertDiagBlocksLowerTriangular" | custom-call | tf_op jit(solution)/shard_map/jit(_solve_triangular)/triangular_solve | solution.py:28
  75.2 3.4 %broadcast_in_dim.41 = f32[12288,128]{0,1:T(8,128)} broadcast(f32[]{:T(128)} %constant.182.clone.1), dimensions={} | broadcast | bytes 6291460 | tf_op jit(solution)/shard_map/broadcast_in_dim | solution.py:31
  78.6 0.6 constant_dynamic-update-slice_fusion
  79.2 11.9 %select_select_fusion = (f32[12288,128]{0,1:T(8,128)}, bf16[12288,128]{0,1:T(8,128)(2,1)S(1)}) fusion(f32[12288,128]{0,1:T(8,128)} %constant_dynamic-update-slice_fusion, f32[12288,128]{0,1:T(8,128)} %copy.10, pred[12288]{0:T(1024)(128)(4,1)S(1)} %get-tuple-element.12, pred[12288]{0:T(1024)(128)(4,1)S(1)} %get-tuple-element.13, ...), kind=kOutput, calls=%fused_computation.7 | convolution fusion | flops 2420637696 | bytes 28401664 | tf_op jit(solution)/shard_map/jit(_solve_triangular)/triangular_solve | solution.py:28
  91.1 1.9 convert_select_fusion
  93.2 6.6 %copy.13 = f32[12288,128]{0,1:T(8,128)} copy(f32[12288,128]{1,0:T(8,128)} %get-tuple-element.9) | data formatting | bytes 12582912
  99.8 6.9 %copy.12 = f32[12288,128]{0,1:T(8,128)} copy(f32[12288,128]{1,0:T(8,128)} %get-tuple-element.7) | data formatting | bytes 12582912
  106.8 84.6 %all-reduce.2.cloned.1.call-done = bf16[12288,128]{0,1:T(8,128)(2,1)} async-done(((bf16[12288,128]{0,1:T(8,128)(2,1)}), bf16[12288,128]{0,1:T(8,128)(2,1)}) %all-reduce.2.cloned.1.call-update) | async-done | bytes 3145744 | tf_op jit(solution)/shard_map/psum | solution.py:12
  191.4 0.8 constant_dynamic-slice_fusion
  192.3 14.8 %all_gather.3 = bf16[2048,128]{0,1:T(8,128)(2,1)S(1)} all-gather(bf16[256,128]{0,1:T(8,128)(2,1)S(1)} %constant_dynamic-slice_fusion), channel_id=1, replica_groups=mesh['prow'=8,'pcol'=16] {'prow'}, dimensions={0}, use_global_device_ids=true | all-gather | bytes 589824 | tf_op jit(solution)/shard_map/all_gather | solution.py:40
  207.0 7.7 %fusion.3 = f32[12288,128]{0,1:T(8,128)} fusion(f32[12288,128]{0,1:T(8,128)} %get-tuple-element.10, f32[12288,128]{0,1:T(8,128)} %copy.13, bf16[12288,128]{0,1:T(8,128)(2,1)} %all-reduce.2.cloned.1.call-done, pred[12288]{0:T(1024)(128)(4,1)S(1)} %get-tuple-element.15, pred[]{:T(512)S(6)} %eq.32, bf16[2048,128]{0,1:T(8,128)(2,1)S(1)} %all_gather.3, ...), kind=kOutput, calls=%fused_computation.5 | convolution fusion | flops 407371776 | bytes 22065156 | tf_op jit(solution)/shard_map/dot_general | solution.py:51
  214.8 4.1 %fusion.2 = f32[12288,128]{0,1:T(8,128)} fusion(f32[12288,128]{0,1:T(8,128)S(1)} %bitcast.27, f32[12288,128]{0,1:T(8,128)S(1)} %bitcast.29, bf16[12288,128]{0,1:T(8,128)(2,1)S(1)} %copy-done, pred[12288]{0:T(1024)(128)(4,1)S(1)} %get-tuple-element.14, pred[]{:T(512)S(6)} %eq.28, bf16[2048,128]{0,1:T(8,128)(2,1)S(1)} %all_gather.3, s32[]{:T(128)S(6)} %select_n.156), kind=kOutput, calls=%fused_computation.4 | convolution fusion | flops 407371776 | bytes 22065156 | tf_op jit(solution)/shard_map/dot_general | solution.py:51
  218.9 10.5 %pad_maximum_fusion = f32[12288,256]{0,1:T(8,128)} fusion(f32[12288,128]{0,1:T(8,128)} %fusion.3, f32[12288,128]{0,1:T(8,128)} %fusion.2), kind=kLoop, calls=%fused_computation.6 | loop fusion | flops 3145728 | bytes 25165824 | tf_op jit(solution)/shard_map/concatenate | solution.py:60
  229.4 12.6 %copy.9 = f32[12288,256]{1,0:T(8,128)} copy(f32[12288,256]{0,1:T(8,128)} %pad_maximum_fusion) | data formatting | bytes 25165824 | tf_op jit(solution)/shard_map/concatenate | solution.py:60
  (19 shorter events, 0.1 us)
Async XLA Ops:
  6.5 184.9 %all-reduce.2.cloned.1.call-start = ((), (), s32[]{:S(2)}) async-start(), calls=%async_computation | async-start | bytes 6291456 | tf_op jit(solution)/shard_map/psum | solution.py:12
  192.3 22.5 %slice-start = ((s8[6291456]{0:T(1024)(128)(4,1)}), s8[4194304]{0:T(1024)(128)(4,1)S(1)}, s32[]{:S(2)}) async-start(s8[6291456]{0:T(1024)(128)(4,1)} %bitcast.26), calls=%async_computation.1 | async-start | bytes 8388608
  192.3 22.5 %slice-start.2 = ((s8[6291456]{0:T(1024)(128)(4,1)}), s8[4194304]{0:T(1024)(128)(4,1)S(1)}, s32[]{:S(2)}) async-start(s8[6291456]{0:T(1024)(128)(4,1)} %bitcast.28), calls=%async_computation.3 | async-start | bytes 8388608
  207.0 7.7 %slice-start.1 = ((s8[6291456]{0:T(1024)(128)(4,1)}), s8[2097152]{0:T(1024)(128)(4,1)S(1)}, s32[]{:S(2)}) async-start(s8[6291456]{0:T(1024)(128)(4,1)} %bitcast.26), calls=%async_computation.2 | async-start | bytes 4194304
  207.0 7.7 %slice-start.3 = ((s8[6291456]{0:T(1024)(128)(4,1)}), s8[2097152]{0:T(1024)(128)(4,1)S(1)}, s32[]{:S(2)}) async-start(s8[6291456]{0:T(1024)(128)(4,1)} %bitcast.28), calls=%async_computation.4 | async-start | bytes 4194304
  207.0 7.7 %copy-start = (bf16[12288,128]{0,1:T(8,128)(2,1)S(1)}, bf16[12288,128]{0,1:T(8,128)(2,1)}, u32[]{:S(2)}) copy-start(bf16[12288,128]{0,1:T(8,128)(2,1)} %all-reduce.2.cloned.1.call-done) | copy-start | bytes 9437188
Sparse Core Ops, SparseCore 0:
  93.1 98.2 all-reduce.1
where the time goes:
time: 249 us
  waiting for transfers between devices  84.7 us (34%)
  local copies, waits for them, and re-layouts  52.4 us (21%)
  blocking collectives  38.4 us (15%)
  other arithmetic  35.3 us (14%)
  matrix products  23.7 us (10%)
  between operations  14.4 us (6%)
    psum x1, waiting for transfers between devices, from_root(): return lax.psum(block, axis)  84.6 us
    psum x1, blocking collectives, from_root(): return lax.psum(block, axis)  23.6 us
    unnamed x14, local copies, waits for them, and re-layouts  20.2 us
    all_gather x1, blocking collectives, body(): lax.all_gather(lax.dynamic_slice_in_dim(low, look_start, per_row * NB, 0)...  14.8 us
    slice x1, local copies, waits for them, and re-layouts, body(): column = window[:, column_slot * NB:(column_slot + 1) * NB]  13.6 us
    concatenate x1, local copies, waits for them, and re-layouts, body(): return jnp.concatenate(pieces, axis=1)  12.6 us
    another operation x3, other arithmetic, body(): factor = jnp.linalg.cholesky(tile)  12.4 us
    another operation x1, matrix products, body(): jax.scipy.linalg.solve_triangular(factor, local_panel.T, lower=True)  11.9 us
  transfers between devices with their start and end apart: 1, of which 1 were waited for; matrix products, arithmetic and copies ran while one was open for 5% of the time, Pallas kernels for 0%

commit v1 on v0

v1 whole, which is shorter than its diff:
```python
import jax
import jax.numpy as jnp
from jax import lax
from jax.experimental import pallas as pl
from jax.experimental.pallas import tpu as pltpu
from jax.sharding import PartitionSpec as P

NB = 128
LOOK = 16
VMEM_LIMIT = 48 * 1024 * 1024
F32 = jnp.float32
BF16 = jnp.bfloat16
HI = lax.Precision.HIGHEST
ANY = pl.BlockSpec(memory_space=pl.ANY)
PART = 1536
SHIFTS = (2, 1, 3)


def params():
    return pltpu.CompilerParams(vmem_limit_bytes=VMEM_LIMIT)


def z_shift(s):
    return [(z * 4 + y, (z + s) % 4 * 4 + y) for z in range(4) for y in range(4)]


def y_shift(s):
    return [(z * 4 + y, z * 4 + (y + s) % 4) for z in range(4) for y in range(4)]


def x_shift(s):
    return [(x * 2 + c, (x + s) % 4 * 2 + c) for x in range(4) for c in range(2)]


def core_swap():
    return [(i, i ^ 1) for i in range(8)]


def cast_parts(window, z, y):
    step = 512
    per = PART // step

    def body(place_ref, *refs):
        for source, target in zip(refs[:8], refs[8:]):
            target[...] = source[...].astype(BF16)

    def spec(n):
        if n < 4:
            return pl.BlockSpec((step, NB), lambda i, s: (lax.rem(s[0] + n, 4) * per + i, 0))
        return pl.BlockSpec((step, NB), lambda i, s: ((4 + lax.rem(s[1] + n, 4)) * per + i, 0))

    return pl.pallas_call(
        body,
        grid_spec=pltpu.PrefetchScalarGridSpec(
            num_scalar_prefetch=1,
            grid=(per,),
            in_specs=[spec(n) for n in range(8)],
            out_specs=[pl.BlockSpec((step, NB), lambda i, s: (i, 0))] * 8,
        ),
        out_shape=[jax.ShapeDtypeStruct((PART, NB), BF16)] * 8,
        compiler_params=params(),
        name="cast_parts",
    )(jnp.stack([z, y]), *([window] * 8))


def pick_parts(choice, first, second):
    def body(choice_ref, *refs):
        sem = refs[10]
        for half in range(2):
            for s in range(4):

                @pl.when(choice_ref[half] == s)
                def _():
                    copy = pltpu.make_async_copy(refs[4 * half + s], refs[8 + half], sem.at[half])
                    copy.start()

        for half in range(2):
            pltpu.make_async_copy(refs[4 * half], refs[8 + half], sem.at[half]).wait()

    return pl.pallas_call(
        body,
        in_specs=[pl.BlockSpec(memory_space=pltpu.SMEM)] + [ANY] * 8,
        out_specs=[ANY, ANY],
        out_shape=[jax.ShapeDtypeStruct((PART, NB), BF16)] * 2,
        scratch_shapes=[pltpu.SemaphoreType.DMA((2,))],
        compiler_params=params(),
        name="pick_parts",
    )(choice, *first, *second)


def factor(places, tile, rows):
    def body(places_ref, tile_ref, rows_ref, low_ref, inv_ref, weights_ref, work):
        t = tile_ref[...]
        row = lax.broadcasted_iota(jnp.int32, (NB, NB), 0)
        col = lax.broadcasted_iota(jnp.int32, (NB, NB), 1)
        work[:, :NB] = 0.5 * (t + t.T)
        work[:, NB:] = jnp.where(row == col, 1.0, 0.0)
        weights_ref[...] = jnp.zeros_like(weights_ref)
        sub = lax.broadcasted_iota(jnp.int32, (8, 1), 0)
        upper = []
        inverse = []
        for b in range(NB // 8):
            block = work[8 * b : 8 * b + 8, :]
            done = jnp.zeros((8, 2 * NB), F32)
            for s in range(8):
                j = 8 * b + s
                scale = lax.rsqrt(block[s : s + 1, j : j + 1])
                line = block[s : s + 1, :] * scale
                weight = jnp.where(sub > s, block[:, j : j + 1] * scale, 0.0)
                done = jnp.where(sub == s, line, done)
                block = block - weight * line
            upper.append(done[:, :NB])
            inverse.append(done[:, NB:])
            if b < NB // 8 - 1:
                work[...] -= lax.dot_general(
                    done[:, :NB], done, (((0,), (0,)), ((), ())), precision=HI, preferred_element_type=F32
                )
        up = jnp.concatenate(upper, 0)
        low_ref[...] = jnp.where(row >= col, up.T, 0.0)
        inv = jnp.where(row >= col, jnp.concatenate(inverse, 0), 0.0)
        inv_ref[...] = inv
        for n in range(2):
            half = lax.dot_general(
                inv, rows_ref[n * NB : (n + 1) * NB, :], (((1,), (1,)), ((), ())), precision=HI, preferred_element_type=F32
            )
            full = lax.dot_general(inv, half, (((0,), (0,)), ((), ())), precision=HI, preferred_element_type=F32)
            weights_ref[pl.ds(pl.multiple_of(places_ref[n] * NB, NB), NB), :] = full.astype(BF16)

    vmem = pl.BlockSpec(memory_space=pltpu.VMEM)
    return pl.pallas_call(
        body,
        in_specs=[pl.BlockSpec(memory_space=pltpu.SMEM), vmem, vmem],
        out_specs=[vmem] * 3,
        out_shape=[
            jax.ShapeDtypeStruct((NB, NB), F32),
            jax.ShapeDtypeStruct((NB, NB), F32),
            jax.ShapeDtypeStruct((LOOK * NB, NB), BF16),
        ],
        scratch_shapes=[pltpu.VMEM((NB, 2 * NB), F32)],
        compiler_params=params(),
        name="factor",
    )(places, tile, rows)


def keep_column(scalars, window, low, inv):
    step = PART

    def body(s_ref, window_ref, low_ref, inv_ref, out_ref):
        i = pl.program_id(0)
        k, p, is_panel = s_ref[0], s_ref[1], s_ref[2]

        @pl.when(is_panel == 0)
        def _():
            out_ref[...] = window_ref[...]

        @pl.when(is_panel == 1)
        def _():
            out_ref[...] = lax.dot_general(
                window_ref[...].astype(BF16),
                inv_ref[...].astype(BF16),
                (((1,), (1,)), ((), ())),
                preferred_element_type=F32,
            )

            @pl.when(i == 0)
            def _():
                for slot in range(2):
                    tile = slot * 8 + p
                    rows = pl.ds(slot * NB, NB)

                    @pl.when(tile == k)
                    def _():
                        out_ref[rows, :] = low_ref[...]

                    @pl.when(tile < k)
                    def _():
                        out_ref[rows, :] = window_ref[rows, :]

    return pl.pallas_call(
        body,
        grid_spec=pltpu.PrefetchScalarGridSpec(
            num_scalar_prefetch=1,
            grid=(window.shape[0] // step,),
            in_specs=[
                pl.BlockSpec((step, NB), lambda i, s: (i, 1 - s[3])),
                pl.BlockSpec((NB, NB), lambda i, s: (0, 0)),
                pl.BlockSpec((NB, NB), lambda i, s: (0, 0)),
            ],
            out_specs=pl.BlockSpec((step, NB), lambda i, s: (i, 1 - s[3])),
        ),
        out_shape=jax.ShapeDtypeStruct(window.shape, F32),
        compiler_params=params(),
        name="keep_column",
    )(scalars, window, low, inv)


def update(scalars, window, weights, parts, places, out):
    n = len(parts)
    s_all = jnp.concatenate([scalars, jnp.stack(places)])

    def body(s_ref, *refs):
        windows, panels, weight_ref = refs[:n], refs[n : 2 * n], refs[2 * n]
        out_hbm, buffers, sem = refs[2 * n + 2], refs[2 * n + 3], refs[2 * n + 4]
        p, j = s_ref[1], s_ref[4]
        lane = pl.multiple_of(s_ref[3] * NB, NB)
        i = pl.program_id(0)
        slot = lax.rem(i, 2)
        size = windows[0].shape[0]

        def copy_out(m, which, step):
            row = pl.multiple_of(s_ref[5 + m] * PART + step * size, size)
            return pltpu.make_async_copy(
                buffers.at[which, m], out_hbm.at[pl.ds(row, size), pl.ds(lane, NB)], sem.at[which, m]
            )

        for m in range(n):

            @pl.when(i >= 2)
            def _():
                copy_out(m, slot, i - 2).wait()

            row = s_ref[5 + m] * PART + i * size + lax.broadcasted_iota(jnp.int32, (size, NB), 0)
            tile = lax.shift_right_logical(row, 7) * 8 + p
            change = lax.dot_general(
                panels[m][...], weight_ref[...], (((1,), (0,)), ((), ())), preferred_element_type=F32
            )
            buffers[slot, m] = windows[m][...] - jnp.where(tile >= j, change, 0.0)
            copy_out(m, slot, i).start()

        @pl.when(i == pl.num_programs(0) - 1)
        def _():
            for m in range(n):
                copy_out(m, 1 - slot, i - 1).wait()
                copy_out(m, slot, i).wait()

    step = 768

    def window_spec(m):
        return pl.BlockSpec((step, NB), lambda i, s: (s[5 + m] * (PART // step) + i, s[3]))

    return pl.pallas_call(
        body,
        grid_spec=pltpu.PrefetchScalarGridSpec(
            num_scalar_prefetch=1,
            grid=(PART // step,),
            in_specs=[window_spec(m) for m in range(n)]
            + [pl.BlockSpec((step, NB), lambda i, s: (i, 0))] * n
            + [pl.BlockSpec((NB, NB), lambda i, s: (0, 0)), ANY],
            out_specs=ANY,
            scratch_shapes=[pltpu.VMEM((2, n, step, NB), F32), pltpu.SemaphoreType.DMA((2, n))],
        ),
        out_shape=jax.ShapeDtypeStruct(window.shape, F32),
        input_output_aliases={2 * n + 2: 0},
        compiler_params=params(),
        name="update",
    )(s_all, *([window] * n), *parts, weights, out)


def over_prow(block):
    pair = block + lax.ppermute(block, "prow", core_swap())
    others = [lax.ppermute(pair, "prow", x_shift(s)) for s in (2, 1, 3)]
    return pair + others[0] + others[1] + others[2]


def body(window, panel_index):
    k = panel_index[0]
    p = lax.axis_index("prow")
    q = lax.axis_index("pcol")
    z, y = q // 4, q % 4
    z0, y0 = k // 4, k % 4
    dz, dy = (z - z0) % 4, (y - y0) % 4
    slot = jnp.where(q <= k, 1, 0)
    j = slot * 16 + q
    scalars = jnp.stack([k, p, jnp.where(q == k, 1, 0), slot, j]).astype(jnp.int32)

    parts = cast_parts(window, z, y)

    got = {}
    for s in SHIFTS:
        got["z", s] = lax.ppermute(parts[s], "pcol", z_shift(s))
        got["y", s] = lax.ppermute(parts[4 + s], "pcol", y_shift(s))
    first, second = pick_parts(
        jnp.stack([dz, dy]),
        [parts[0], got["z", 1], got["z", 2], got["z", 3]],
        [parts[4], got["y", 1], got["y", 2], got["y", 3]],
    )

    tile = lax.dynamic_slice(window, (k // 8 * NB, 0), (NB, NB))
    tile = over_prow(jnp.where(p == k % 8, tile, 0.0))
    j_first = k + 1 + (p - (k + 1)) % 8
    look_rows = lax.dynamic_slice(window, (j_first // 8 * NB, 0), (2 * NB, NB))
    low, inv, weights = factor(jnp.stack([j_first % 16, (j_first + 8) % 16]), tile, look_rows)

    for s in SHIFTS:
        got["y", s] = lax.ppermute(first, "pcol", y_shift(s))
        got["z", s] = lax.ppermute(second, "pcol", z_shift(s))
    first, second = pick_parts(
        jnp.stack([dy, dz]),
        [first, got["y", 1], got["y", 2], got["y", 3]],
        [second, got["z", 1], got["z", 2], got["z", 3]],
    )

    weights = lax.all_to_all(weights, "pcol", 0, 0, tiled=True)
    weights = over_prow(lax.dynamic_slice(weights, (k * NB, 0), (NB, NB)))

    out = keep_column(scalars, window, low, inv)

    for s in SHIFTS:
        got["z", s] = lax.ppermute(first, "pcol", z_shift(s))
        got["y", s] = lax.ppermute(second, "pcol", y_shift(s))
    out = update(scalars, window, weights, [first, second], [z, 4 + y], out)
    for s in SHIFTS:
        out = update(
            scalars, window, weights, [got["z", s], got["y", s]], [(z - s) % 4, 4 + (y - s) % 4], out
        )
    return out


def solution(mesh):
    return jax.shard_map(
        body,
        mesh=mesh,
        in_specs=(P("prow", "pcol"), P()),
        out_specs=P("prow", "pcol"),
        check_vma=False,
    )
```

time: 249 us -> 135 us (0.54)
  waiting for transfers between devices: 84.7 us -> 24.4 us
  starting transfers between devices: 0.01 us -> 52.2 us
  Pallas kernels: 0 us -> 47.3 us
  local copies, waits for them, and re-layouts: 52.4 us -> 5.65 us
  blocking collectives: 38.4 us -> 0 us
  other arithmetic: 35.3 us -> 2.83 us
  matrix products: 23.7 us -> 0 us
  between operations: 14.4 us -> 1.01 us
    psum x1 -> x0, waiting for transfers between devices: 84.6 us -> none  [from_root(): return lax.psum(block, axis)]
    pallas_call x0 -> x9, Pallas kernels: none -> 47.3 us  [the longest x1 17.6 us: factor(): pl.pallas_call(body, in_specs=[pl.BlockSpec(memory_space=pltpu.SMEM), vme...]
    ppermute x0 -> x26, starting transfers between devices: none -> 45.3 us  [the longest x6 10.9 us: over_prow(): others = [lax.ppermute(pair, 'prow', x_shift(s)) for s in (2, 1, 3)]]
    ppermute x0 -> x26, waiting for transfers between devices: none -> 24.4 us  [the longest x3 8.57 us: body(): got['z', s] = lax.ppermute(second, 'pcol', z_shift(s))]
    psum x1 -> x0, blocking collectives: 23.6 us -> none  [from_root(): return lax.psum(block, axis)]
    another operation x5 -> x4, other arithmetic: 22.9 us -> 0.3 us  [the longest x1 0.07 us: cast_parts(): jnp.stack([z, y])]
    unnamed x14 -> x10, local copies, waits for them, and re-layouts: 20.2 us -> 3.55 us
    all_gather x1 -> x0, blocking collectives: 14.8 us -> none  [body(): lax.all_gather(lax.dynamic_slice_in_dim(low, look_start, per_row * NB, 0)...]
  transfers between devices with their start and end apart: 1 -> 27, of which waited for: 1 -> 6; matrix products, arithmetic and copies ran while one was open for 5% -> 4% of each run, Pallas kernels for 0% -> 29%
where the time goes in v1:
time: 135 us; the launch traced here: 133 us
  starting transfers between devices  52.2 us (39%)
  Pallas kernels  47.3 us (35%)
  waiting for transfers between devices  24.4 us (18%)
  local copies, waits for them, and re-layouts  5.65 us (4%)
  other arithmetic  2.83 us (2%)
    pallas_call x1, Pallas kernels, factor(): pl.pallas_call(body, in_specs=[pl.BlockSpec(memory_space=pltpu.SMEM), vme...  17.6 us
    pallas_call x4, Pallas kernels, update(): pl.pallas_call(body, grid_spec=pltpu.PrefetchScalarGridSpec(num_scalar_pr...  13.7 us
    ppermute x6, starting transfers between devices, over_prow(): others = [lax.ppermute(pair, 'prow', x_shift(s)) for s in (2, 1, 3)]  10.9 us
    ppermute x3, waiting for transfers between devices, body(): got['z', s] = lax.ppermute(second, 'pcol', z_shift(s))  8.57 us
    pallas_call x1, Pallas kernels, keep_column(): pl.pallas_call(body, grid_spec=pltpu.PrefetchScalarGridSpec(num_scalar_pr...  8.4 us
    ppermute x3, waiting for transfers between devices, body(): got['y', s] = lax.ppermute(first, 'pcol', y_shift(s))  8.26 us
    all_to_all x1, starting transfers between devices, body(): weights = lax.all_to_all(weights, 'pcol', 0, 0, tiled=True)  6.89 us
    ppermute x3, starting transfers between devices, body(): got['z', s] = lax.ppermute(parts[s], 'pcol', z_shift(s))  6.58 us
  transfers between devices with their start and end apart: 27, of which 6 were waited for; matrix products, arithmetic and copies ran while one was open for 4% of the time, Pallas kernels for 29%

profile of v1, /device:TPU:1, one launch (start us, length us, event | category | flops | bytes accessed | tf_op | source)
XLA Modules:
  0.0 133.4 jit_solution(3000358284122669497)
XLA Ops:
  0.1 5.0 %cast_parts.1 = (bf16[1536,128]{1,0:T(8,128)(2,1)S(1)}, bf16[1536,128]{1,0:T(8,128)(2,1)S(1)}, bf16[1536,128]{1,0:T(8,128)(2,1)}, bf16[1536,128]{1,0:T(8,128)(2,...) custom-call(s32[2]{0:T(128)S(1)} %pad_add_fusion.2.place_ref, ...), custom_call_target="tpu_custom_call" | custom-call | tf_op jit(solution)/shard_map/cast_parts/pallas_call | solution.py:52
  5.1 2.5 %collective-permute-start = (bf16[1536,128]{1,0:T(8,128)(2,1)S(1)}, bf16[1536,128]{1,0:T(8,128)(2,1)S(1)}, u32[]{:S(2)}, u32[]{:S(2)}) collective-permute-start(bf16[1536,128]{1,0:T(8,128)(2,1)S(1)} %get-tuple-element.21), channel_id=1, source_target_pairs={{0,4},{1,5},{2,6},{3,7},{4,8},{5,9},{6,10},{7,11},{8,12},{9,13},{1... | collective-permute-start | bytes 1179656 | tf_op jit(solution)/shard_map/ppermute | solution.py:280
  10.1 3.3 %collective-permute-start.1 = (bf16[1536,128]{1,0:T(8,128)(2,1)}, bf16[1536,128]{1,0:T(8,128)(2,1)S(1)}, u32[]{:S(2)}, u32[]{:S(2)}) collective-permute-start(bf16[1536,128]{1,0:T(8,128)(2,1)} %get-tuple-element.22), channel_id=1, source_target_pairs={{0,8},{1,9},{2,10},{3,11},{4,12},{5,13},{6,14},{7,15},{8,0},{9,1},... | collective-permute-start | bytes 1179656 | tf_op jit(solution)/shard_map/ppermute | solution.py:280
  16.1 2.6 %collective-permute-start.4 = (bf16[1536,128]{1,0:T(8,128)(2,1)}, bf16[1536,128]{1,0:T(8,128)(2,1)S(1)}, u32[]{:S(2)}, u32[]{:S(2)}) collective-permute-start(bf16[1536,128]{1,0:T(8,128)(2,1)} %get-tuple-element.26), channel_id=1, source_target_pairs={{0,2},{1,3},{2,0},{3,1},{4,6},{5,7},{6,4},{7,5},{8,10},{9,11},{10,... | collective-permute-start | bytes 1179656 | tf_op jit(solution)/shard_map/ppermute | solution.py:281
  18.7 2.6 %collective-permute-start.5 = (bf16[1536,128]{1,0:T(8,128)(2,1)S(1)}, bf16[1536,128]{1,0:T(8,128)(2,1)S(1)}, u32[]{:S(2)}, u32[]{:S(2)}) collective-permute-start(bf16[1536,128]{1,0:T(8,128)(2,1)S(1)} %get-tuple-element.27), channel_id=1, source_target_pairs={{0,3},{1,0},{2,1},{3,2},{4,7},{5,4},{6,5},{7,6},{8,11},{9,8},{10,9... | collective-permute-start | bytes 1179656 | tf_op jit(solution)/shard_map/ppermute | solution.py:281
  23.2 4.7 %collective-permute-done.1.refs_2_ = bf16[1536,128]{1,0:T(8,128)(2,1)S(1)} collective-permute-done((bf16[1536,128]{1,0:T(8,128)(2,1)}, bf16[1536,128]{1,0:T(8,128)(2,1)S(1)}, u32[]{:S(2)}, u32[]{:S(2)}) %collective-permute-start.1) | collective-permute-done | bytes 393248 | tf_op jit(solution)/shard_map/ppermute | solution.py:280
  27.9 2.7 %collective-permute-start.15 = (f32[128,128]{1,0:T(8,128)S(1)}, f32[128,128]{1,0:T(8,128)S(1)}, u32[]{:S(2)}, u32[]{:S(2)}) collective-permute-start(f32[128,128]{1,0:T(8,128)S(1)} %fusion.1), channel_id=1, source_target_pairs={{0,64},{16,80},{32,96},{48,112},{64,0},{80,16},{96,32},{112,48},{1... | collective-permute-start | bytes 196616 | tf_op jit(solution)/shard_map/ppermute | solution.py:261
  33.3 2.0 %collective-permute-done.4.refs_6_ = bf16[1536,128]{1,0:T(8,128)(2,1)S(1)} collective-permute-done((bf16[1536,128]{1,0:T(8,128)(2,1)}, bf16[1536,128]{1,0:T(8,128)(2,1)S(1)}, u32[]{:S(2)}, u32[]{:S(2)}) %collective-permute-start.4) | collective-permute-done | bytes 393248 | tf_op jit(solution)/shard_map/ppermute | solution.py:281
  37.7 17.6 %factor.1 = (f32[128,128]{1,0:T(8,128)S(1)}, f32[128,128]{1,0:T(8,128)S(1)}, bf16[2048,128]{1,0:T(8,128)(2,1)}) custom-call(s32[2]{0:T(128)S(1)} %pad_add_fusion.3.places_ref, f32[128,128]{1,0:T(8,128)S(1)} %add_add_fusion.tile_ref, f32[256,128]{1,0:T(8,128)S(1)} %constant_dynamic-slice_fusion.1.rows_ref), custom_call_target="tpu_custom_call" | custom-call | tf_op jit(solution)/shard_map/factor/pallas_call | solution.py:130
  56.6 6.9 %all-to-all-start = ((bf16[16,128,128]{2,1,0:T(8,128)(2,1)}), bf16[16,128,128]{2,1,0:T(8,128)(2,1)}, u32[]{:S(2)}, u32[]{:S(2)}) async-start(bf16[16,128,128]{2,1,0:T(8,128)(2,1)} %bitcast.13), calls=%async_computation | async-start | bytes 1048576 | tf_op jit(solution)/shard_map/all_to_all | solution.py:303
  63.5 2.5 %collective-permute-start.11 = (bf16[1536,128]{1,0:T(8,128)(2,1)}, bf16[1536,128]{1,0:T(8,128)(2,1)S(1)}, u32[]{:S(2)}, u32[]{:S(2)}) collective-permute-start(bf16[1536,128]{1,0:T(8,128)(2,1)} %get-tuple-element.29.refs_4_), channel_id=1, source_target_pairs={{0,12},{1,13},{2,14},{3,15},{4,0},{5,1},{6,2},{7,3},{8,4},{9,5},{1... | collective-permute-start | bytes 1179656 | tf_op jit(solution)/shard_map/ppermute | solution.py:296
  67.2 2.4 %collective-permute-start.7 = (bf16[1536,128]{1,0:T(8,128)(2,1)S(1)}, bf16[1536,128]{1,0:T(8,128)(2,1)S(1)}, u32[]{:S(2)}, u32[]{:S(2)}) collective-permute-start(bf16[1536,128]{1,0:T(8,128)(2,1)S(1)} %get-tuple-element.28.refs_0_), channel_id=1, source_target_pairs={{0,2},{1,3},{2,0},{3,1},{4,6},{5,7},{6,4},{7,5},{8,10},{9,11},{10,... | collective-permute-start | bytes 1179656 | tf_op jit(solution)/shard_map/ppermute | solution.py:295
  70.8 8.6 %collective-permute-done.11.refs_7_ = bf16[1536,128]{1,0:T(8,128)(2,1)S(1)} collective-permute-done((bf16[1536,128]{1,0:T(8,128)(2,1)}, bf16[1536,128]{1,0:T(8,128)(2,1)S(1)}, u32[]{:S(2)}, u32[]{:S(2)}) %collective-permute-start.11) | collective-permute-done | bytes 393248 | tf_op jit(solution)/shard_map/ppermute | solution.py:296
  80.4 7.2 %collective-permute-done.7.refs_2_ = bf16[1536,128]{1,0:T(8,128)(2,1)S(1)} collective-permute-done((bf16[1536,128]{1,0:T(8,128)(2,1)S(1)}, bf16[1536,128]{1,0:T(8,128)(2,1)S(1)}, u32[]{:S(2)}, u32[]{:S(2)}) %collective-permute-start.7) | collective-permute-done | bytes 393248 | tf_op jit(solution)/shard_map/ppermute | solution.py:295
  88.7 2.4 %collective-permute-start.24 = (bf16[1536,128]{1,0:T(8,128)(2,1)S(1)}, bf16[1536,128]{1,0:T(8,128)(2,1)S(1)}, u32[]{:S(2)}, u32[]{:S(2)}) collective-permute-start(bf16[1536,128]{1,0:T(8,128)(2,1)S(1)} %get-tuple-element.30.refs_2_), channel_id=1, source_target_pairs={{0,8},{1,9},{2,10},{3,11},{4,12},{5,13},{6,14},{7,15},{8,0},{9,1},... | collective-permute-start | bytes 1179656 | tf_op jit(solution)/shard_map/ppermute | solution.py:309
  91.9 3.6 %collective-permute-start.18 = (bf16[128,128]{1,0:T(8,128)(2,1)S(1)}, bf16[128,128]{1,0:T(8,128)(2,1)S(1)}, u32[]{:S(2)}, u32[]{:S(2)}) collective-permute-start(bf16[128,128]{1,0:T(8,128)(2,1)S(1)} %constant_dynamic-slice_fusion), channel_id=1, source_target_pairs={{0,16},{16,0},{32,48},{48,32},{64,80},{80,64},{96,112},{112,96},{1... | collective-permute-start | bytes 98312 | tf_op jit(solution)/shard_map/ppermute | solution.py:260
  97.1 2.8 %collective-permute-start.19 = (bf16[128,128]{1,0:T(8,128)(2,1)S(1)}, bf16[128,128]{1,0:T(8,128)(2,1)S(1)}, u32[]{:S(2)}, u32[]{:S(2)}) collective-permute-start(bf16[128,128]{1,0:T(8,128)(2,1)S(1)} %fusion), channel_id=1, source_target_pairs={{0,64},{16,80},{32,96},{48,112},{64,0},{80,16},{96,32},{112,48},{1... | collective-permute-start | bytes 98312 | tf_op jit(solution)/shard_map/ppermute | solution.py:261
  100.2 2.4 %collective-permute-start.21 = (bf16[128,128]{1,0:T(8,128)(2,1)S(1)}, bf16[128,128]{1,0:T(8,128)(2,1)S(1)}, u32[]{:S(2)}, u32[]{:S(2)}) collective-permute-start(bf16[128,128]{1,0:T(8,128)(2,1)S(1)} %fusion), channel_id=1, source_target_pairs={{0,96},{16,112},{32,0},{48,16},{64,32},{80,48},{96,64},{112,80},{1... | collective-permute-start | bytes 98312 | tf_op jit(solution)/shard_map/ppermute | solution.py:261
  106.3 2.6 %collective-permute-start.13 = (bf16[1536,128]{1,0:T(8,128)(2,1)S(1)}, bf16[1536,128]{1,0:T(8,128)(2,1)S(1)}, u32[]{:S(2)}, u32[]{:S(2)}) collective-permute-start(bf16[1536,128]{1,0:T(8,128)(2,1)S(1)} %get-tuple-element.31.refs_3_), channel_id=1, source_target_pairs={{0,3},{1,0},{2,1},{3,2},{4,7},{5,4},{6,5},{7,6},{8,11},{9,8},{10,9... | collective-permute-start | bytes 1179656 | tf_op jit(solution)/shard_map/ppermute | solution.py:310
  111.0 8.4 %keep_column.1.refs_5_ = f32[12288,256]{1,0:T(8,128)} custom-call(s32[5]{0:T(128)S(1)} %stack.90.s_ref, f32[12288,256]{1,0:T(8,128)} %refs_1_.9, f32[128,128]{1,0:T(8,128)S(1)} %copy-done.1, f32[128,128]{1,0:T(8,128)S(1)} %copy-done.3), custom_call_target="tpu_custom_call" | custom-call | tf_op jit(solution)/shard_map/keep_column/pallas_call | solution.py:179
  119.4 3.4 %update.4.refs_5_ = f32[12288,256]{1,0:T(8,128)} custom-call(s32[7]{0:T(128)S(1)} %concatenate.19.s_ref, f32[12288,256]{1,0:T(8,128)} %refs_1_.9, f32[12288,256]{1,0:T(8,128)} %refs_1_.9, bf16[1536,128]{1,0:T(8,128)(2,1)S(1)} %get-tuple-element.30.refs_2_, bf16[1536,128]{1,0:T(8,128)(2,1)S(1)} %get-tuple-element.31.refs_3_, ...), custom_call_target="tpu_custom_call", output_to_operand_aliasing={{}: (6, {})} | custom-call | tf_op jit(solution)/shard_map/update/pallas_call | solution.py:241
  122.9 3.4 %update.5.refs_5_ = f32[12288,256]{1,0:T(8,128)} custom-call(s32[7]{0:T(128)S(1)} %concatenate.18.s_ref, f32[12288,256]{1,0:T(8,128)} %refs_1_.9, f32[12288,256]{1,0:T(8,128)} %refs_1_.9, bf16[1536,128]{1,0:T(8,128)(2,1)S(1)} %collective-permute-done.24.refs_2_, ...), custom_call_target="tpu_custom_call", output_to_operand_aliasing={{}: (6, {})} | custom-call | tf_op jit(solution)/shard_map/update/pallas_call | solution.py:241
  126.3 3.4 %update.6.refs_5_ = f32[12288,256]{1,0:T(8,128)} custom-call(s32[7]{0:T(128)S(1)} %concatenate.17.s_ref, f32[12288,256]{1,0:T(8,128)} %refs_1_.9, f32[12288,256]{1,0:T(8,128)} %refs_1_.9, bf16[1536,128]{1,0:T(8,128)(2,1)S(1)} %collective-permute-done.22.refs_2_, ...), custom_call_target="tpu_custom_call", output_to_operand_aliasing={{}: (6, {})} | custom-call | tf_op jit(solution)/shard_map/update/pallas_call | solution.py:241
  129.8 3.4 %update.7 = f32[12288,256]{1,0:T(8,128)} custom-call(s32[7]{0:T(128)S(1)} %concatenate.16.s_ref, f32[12288,256]{1,0:T(8,128)} %refs_1_.9, f32[12288,256]{1,0:T(8,128)} %refs_1_.9, bf16[1536,128]{1,0:T(8,128)(2,1)S(1)} %collective-permute-done.12.refs_2_, bf16[1536,128]{1,0:T(8,128)(2,1)S(1)} %collective-permute-done.13.refs_3_, ...), custom_call_target="tpu_custom_call", output_to_operand_aliasing={{}: (6, {})} | custom-call | tf_op jit(solution)/shard_map/update/pallas_call | solution.py:241
  (65 shorter events, 25.7 us)
Async XLA Ops:
  5.1 13.6 %collective-permute-start = (bf16[1536,128]{1,0:T(8,128)(2,1)S(1)}, bf16[1536,128]{1,0:T(8,128)(2,1)S(1)}, u32[]{:S(2)}, u32[]{:S(2)}) collective-permute-start(bf16[1536,128]{1,0:T(8,128)(2,1)S(1)} %get-tuple-element.21), channel_id=1, source_target_pairs={{0,4},{1,5},{2,6},{3,7},{4,8},{5,9},{6,10},{7,11},{8,12},{9,13},{1... | collective-permute-start | bytes 1179656 | tf_op jit(solution)/shard_map/ppermute | solution.py:280
  9.2 6.3 %collective-permute-start.14 = (f32[128,128]{1,0:T(8,128)S(1)}, f32[128,128]{1,0:T(8,128)S(1)}, u32[]{:S(2)}, u32[]{:S(2)}) collective-permute-start(f32[128,128]{1,0:T(8,128)S(1)} %dynamic-slice_select_fusion), channel_id=1, source_target_pairs={{0,16},{16,0},{32,48},{48,32},{64,80},{80,64},{96,112},{112,96},{1... | collective-permute-start | bytes 196616 | tf_op jit(solution)/shard_map/ppermute | solution.py:260
  10.1 17.7 %collective-permute-start.1 = (bf16[1536,128]{1,0:T(8,128)(2,1)}, bf16[1536,128]{1,0:T(8,128)(2,1)S(1)}, u32[]{:S(2)}, u32[]{:S(2)}) collective-permute-start(bf16[1536,128]{1,0:T(8,128)(2,1)} %get-tuple-element.22), channel_id=1, source_target_pairs={{0,8},{1,9},{2,10},{3,11},{4,12},{5,13},{6,14},{7,15},{8,0},{9,1},... | collective-permute-start | bytes 1179656 | tf_op jit(solution)/shard_map/ppermute | solution.py:280
  13.5 17.2 %collective-permute-start.2 = (bf16[1536,128]{1,0:T(8,128)(2,1)}, bf16[1536,128]{1,0:T(8,128)(2,1)S(1)}, u32[]{:S(2)}, u32[]{:S(2)}) collective-permute-start(bf16[1536,128]{1,0:T(8,128)(2,1)} %get-tuple-element.23), channel_id=1, source_target_pairs={{0,12},{1,13},{2,14},{3,15},{4,0},{5,1},{6,2},{7,3},{8,4},{9,5},{1... | collective-permute-start | bytes 1179656 | tf_op jit(solution)/shard_map/ppermute | solution.py:280
  14.2 17.5 %collective-permute-start.3 = (bf16[1536,128]{1,0:T(8,128)(2,1)}, bf16[1536,128]{1,0:T(8,128)(2,1)S(1)}, u32[]{:S(2)}, u32[]{:S(2)}) collective-permute-start(bf16[1536,128]{1,0:T(8,128)(2,1)} %get-tuple-element.25), channel_id=1, source_target_pairs={{0,1},{1,2},{2,3},{3,0},{4,5},{5,6},{6,7},{7,4},{8,9},{9,10},{10,1... | collective-permute-start | bytes 1179656 | tf_op jit(solution)/shard_map/ppermute | solution.py:281
  16.1 19.2 %collective-permute-start.4 = (bf16[1536,128]{1,0:T(8,128)(2,1)}, bf16[1536,128]{1,0:T(8,128)(2,1)S(1)}, u32[]{:S(2)}, u32[]{:S(2)}) collective-permute-start(bf16[1536,128]{1,0:T(8,128)(2,1)} %get-tuple-element.26), channel_id=1, source_target_pairs={{0,2},{1,3},{2,0},{3,1},{4,6},{5,7},{6,4},{7,5},{8,10},{9,11},{10,... | collective-permute-start | bytes 1179656 | tf_op jit(solution)/shard_map/ppermute | solution.py:281
  18.7 16.6 %collective-permute-start.5 = (bf16[1536,128]{1,0:T(8,128)(2,1)S(1)}, bf16[1536,128]{1,0:T(8,128)(2,1)S(1)}, u32[]{:S(2)}, u32[]{:S(2)}) collective-permute-start(bf16[1536,128]{1,0:T(8,128)(2,1)S(1)} %get-tuple-element.27), channel_id=1, source_target_pairs={{0,3},{1,0},{2,1},{3,2},{4,7},{5,4},{6,5},{7,6},{8,11},{9,8},{10,9... | collective-permute-start | bytes 1179656 | tf_op jit(solution)/shard_map/ppermute | solution.py:281
  27.9 9.8 %collective-permute-start.15 = (f32[128,128]{1,0:T(8,128)S(1)}, f32[128,128]{1,0:T(8,128)S(1)}, u32[]{:S(2)}, u32[]{:S(2)}) collective-permute-start(f32[128,128]{1,0:T(8,128)S(1)} %fusion.1), channel_id=1, source_target_pairs={{0,64},{16,80},{32,96},{48,112},{64,0},{80,16},{96,32},{112,48},{1... | collective-permute-start | bytes 196616 | tf_op jit(solution)/shard_map/ppermute | solution.py:261
  30.6 7.0 %collective-permute-start.16 = (f32[128,128]{1,0:T(8,128)S(1)}, f32[128,128]{1,0:T(8,128)S(1)}, u32[]{:S(2)}, u32[]{:S(2)}) collective-permute-start(f32[128,128]{1,0:T(8,128)S(1)} %fusion.1), channel_id=1, source_target_pairs={{0,32},{16,48},{32,64},{48,80},{64,96},{80,112},{96,0},{112,16},{1... | collective-permute-start | bytes 196616 | tf_op jit(solution)/shard_map/ppermute | solution.py:261
  31.7 6.0 %collective-permute-start.17 = (f32[128,128]{1,0:T(8,128)S(1)}, f32[128,128]{1,0:T(8,128)S(1)}, u32[]{:S(2)}, u32[]{:S(2)}) collective-permute-start(f32[128,128]{1,0:T(8,128)S(1)} %fusion.1), channel_id=1, source_target_pairs={{0,96},{16,112},{32,0},{48,16},{64,32},{80,48},{96,64},{112,80},{1... | collective-permute-start | bytes 196616 | tf_op jit(solution)/shard_map/ppermute | solution.py:261
  36.9 33.9 %collective-permute-start.10 = (bf16[1536,128]{1,0:T(8,128)(2,1)}, bf16[1536,128]{1,0:T(8,128)(2,1)S(1)}, u32[]{:S(2)}, u32[]{:S(2)}) collective-permute-start(bf16[1536,128]{1,0:T(8,128)(2,1)} %get-tuple-element.29.refs_4_), channel_id=1, source_target_pairs={{0,8},{1,9},{2,10},{3,11},{4,12},{5,13},{6,14},{7,15},{8,0},{9,1},... | collective-permute-start | bytes 1179656 | tf_op jit(solution)/shard_map/ppermute | solution.py:296
  56.6 34.5 %all-to-all-start = ((bf16[16,128,128]{2,1,0:T(8,128)(2,1)}), bf16[16,128,128]{2,1,0:T(8,128)(2,1)}, u32[]{:S(2)}, u32[]{:S(2)}) async-start(bf16[16,128,128]{2,1,0:T(8,128)(2,1)} %bitcast.13), calls=%async_computation | async-start | bytes 1048576 | tf_op jit(solution)/shard_map/all_to_all | solution.py:303
  63.5 15.9 %collective-permute-start.11 = (bf16[1536,128]{1,0:T(8,128)(2,1)}, bf16[1536,128]{1,0:T(8,128)(2,1)S(1)}, u32[]{:S(2)}, u32[]{:S(2)}) collective-permute-start(bf16[1536,128]{1,0:T(8,128)(2,1)} %get-tuple-element.29.refs_4_), channel_id=1, source_target_pairs={{0,12},{1,13},{2,14},{3,15},{4,0},{5,1},{6,2},{7,3},{8,4},{9,5},{1... | collective-permute-start | bytes 1179656 | tf_op jit(solution)/shard_map/ppermute | solution.py:296
  66.0 14.4 %collective-permute-start.6 = (bf16[1536,128]{1,0:T(8,128)(2,1)S(1)}, bf16[1536,128]{1,0:T(8,128)(2,1)S(1)}, u32[]{:S(2)}, u32[]{:S(2)}) collective-permute-start(bf16[1536,128]{1,0:T(8,128)(2,1)S(1)} %get-tuple-element.28.refs_0_), channel_id=1, source_target_pairs={{0,1},{1,2},{2,3},{3,0},{4,5},{5,6},{6,7},{7,4},{8,9},{9,10},{10,1... | collective-permute-start | bytes 1179656 | tf_op jit(solution)/shard_map/ppermute | solution.py:295
  67.2 20.5 %collective-permute-start.7 = (bf16[1536,128]{1,0:T(8,128)(2,1)S(1)}, bf16[1536,128]{1,0:T(8,128)(2,1)S(1)}, u32[]{:S(2)}, u32[]{:S(2)}) collective-permute-start(bf16[1536,128]{1,0:T(8,128)(2,1)S(1)} %get-tuple-element.28.refs_0_), channel_id=1, source_target_pairs={{0,2},{1,3},{2,0},{3,1},{4,6},{5,7},{6,4},{7,5},{8,10},{9,11},{10,... | collective-permute-start | bytes 1179656 | tf_op jit(solution)/shard_map/ppermute | solution.py:295
  69.6 18.1 %collective-permute-start.8 = (bf16[1536,128]{1,0:T(8,128)(2,1)S(1)}, bf16[1536,128]{1,0:T(8,128)(2,1)S(1)}, u32[]{:S(2)}, u32[]{:S(2)}) collective-permute-start(bf16[1536,128]{1,0:T(8,128)(2,1)S(1)} %get-tuple-element.28.refs_0_), channel_id=1, source_target_pairs={{0,3},{1,0},{2,1},{3,2},{4,7},{5,4},{6,5},{7,6},{8,11},{9,8},{10,9... | collective-permute-start | bytes 1179656 | tf_op jit(solution)/shard_map/ppermute | solution.py:295
  70.8 16.9 %collective-permute-start.9 = (bf16[1536,128]{1,0:T(8,128)(2,1)}, bf16[1536,128]{1,0:T(8,128)(2,1)S(1)}, u32[]{:S(2)}, u32[]{:S(2)}) collective-permute-start(bf16[1536,128]{1,0:T(8,128)(2,1)} %get-tuple-element.29.refs_4_), channel_id=1, source_target_pairs={{0,4},{1,5},{2,6},{3,7},{4,8},{5,9},{6,10},{7,11},{8,12},{9,13},{1... | collective-permute-start | bytes 1179656 | tf_op jit(solution)/shard_map/ppermute | solution.py:296
  88.7 17.6 %collective-permute-start.24 = (bf16[1536,128]{1,0:T(8,128)(2,1)S(1)}, bf16[1536,128]{1,0:T(8,128)(2,1)S(1)}, u32[]{:S(2)}, u32[]{:S(2)}) collective-permute-start(bf16[1536,128]{1,0:T(8,128)(2,1)S(1)} %get-tuple-element.30.refs_2_), channel_id=1, source_target_pairs={{0,8},{1,9},{2,10},{3,11},{4,12},{5,13},{6,14},{7,15},{8,0},{9,1},... | collective-permute-start | bytes 1179656 | tf_op jit(solution)/shard_map/ppermute | solution.py:309
  97.1 6.6 %collective-permute-start.19 = (bf16[128,128]{1,0:T(8,128)(2,1)S(1)}, bf16[128,128]{1,0:T(8,128)(2,1)S(1)}, u32[]{:S(2)}, u32[]{:S(2)}) collective-permute-start(bf16[128,128]{1,0:T(8,128)(2,1)S(1)} %fusion), channel_id=1, source_target_pairs={{0,64},{16,80},{32,96},{48,112},{64,0},{80,16},{96,32},{112,48},{1... | collective-permute-start | bytes 98312 | tf_op jit(solution)/shard_map/ppermute | solution.py:261
  102.6 23.7 %collective-permute-start.22 = (bf16[1536,128]{1,0:T(8,128)(2,1)S(1)}, bf16[1536,128]{1,0:T(8,128)(2,1)S(1)}, u32[]{:S(2)}, u32[]{:S(2)}) collective-permute-start(bf16[1536,128]{1,0:T(8,128)(2,1)S(1)} %get-tuple-element.30.refs_2_), channel_id=1, source_target_pairs={{0,4},{1,5},{2,6},{3,7},{4,8},{5,9},{6,10},{7,11},{8,12},{9,13},{1... | collective-permute-start | bytes 1179656 | tf_op jit(solution)/shard_map/ppermute | solution.py:309
  103.7 19.2 %collective-permute-start.25 = (bf16[1536,128]{1,0:T(8,128)(2,1)S(1)}, bf16[1536,128]{1,0:T(8,128)(2,1)S(1)}, u32[]{:S(2)}, u32[]{:S(2)}) collective-permute-start(bf16[1536,128]{1,0:T(8,128)(2,1)S(1)} %get-tuple-element.31.refs_3_), channel_id=1, source_target_pairs={{0,2},{1,3},{2,0},{3,1},{4,6},{5,7},{6,4},{7,5},{8,10},{9,11},{10,... | collective-permute-start | bytes 1179656 | tf_op jit(solution)/shard_map/ppermute | solution.py:310
  104.6 21.7 %collective-permute-start.23 = (bf16[1536,128]{1,0:T(8,128)(2,1)S(1)}, bf16[1536,128]{1,0:T(8,128)(2,1)S(1)}, u32[]{:S(2)}, u32[]{:S(2)}) collective-permute-start(bf16[1536,128]{1,0:T(8,128)(2,1)S(1)} %get-tuple-element.31.refs_3_), channel_id=1, source_target_pairs={{0,1},{1,2},{2,3},{3,0},{4,5},{5,6},{6,7},{7,4},{8,9},{9,10},{10,1... | collective-permute-start | bytes 1179656 | tf_op jit(solution)/shard_map/ppermute | solution.py:310
  104.6 25.2 %collective-permute-start.12 = (bf16[1536,128]{1,0:T(8,128)(2,1)S(1)}, bf16[1536,128]{1,0:T(8,128)(2,1)S(1)}, u32[]{:S(2)}, u32[]{:S(2)}) collective-permute-start(bf16[1536,128]{1,0:T(8,128)(2,1)S(1)} %get-tuple-element.30.refs_2_), channel_id=1, source_target_pairs={{0,12},{1,13},{2,14},{3,15},{4,0},{5,1},{6,2},{7,3},{8,4},{9,5},{1... | collective-permute-start | bytes 1179656 | tf_op jit(solution)/shard_map/ppermute | solution.py:309
  106.3 23.5 %collective-permute-start.13 = (bf16[1536,128]{1,0:T(8,128)(2,1)S(1)}, bf16[1536,128]{1,0:T(8,128)(2,1)S(1)}, u32[]{:S(2)}, u32[]{:S(2)}) collective-permute-start(bf16[1536,128]{1,0:T(8,128)(2,1)S(1)} %get-tuple-element.31.refs_3_), channel_id=1, source_target_pairs={{0,3},{1,0},{2,1},{3,2},{4,7},{5,4},{6,5},{7,6},{8,11},{9,8},{10,9... | collective-permute-start | bytes 1179656 | tf_op jit(solution)/shard_map/ppermute | solution.py:310
  (8 other events, 17.1 us)

commit v2 on v0

v2 whole, which is shorter than its diff:
```python
import jax
import jax.numpy as jnp
from jax import lax
from jax.experimental import pallas as pl
from jax.experimental.pallas import tpu as pltpu
from jax.sharding import PartitionSpec as P

NB = 128
LOOK = 16
VMEM_LIMIT = 48 * 1024 * 1024
F32 = jnp.float32
BF16 = jnp.bfloat16
HI = lax.Precision.HIGHEST
ANY = pl.BlockSpec(memory_space=pl.ANY)
HBM = pl.BlockSpec(memory_space=pltpu.HBM)
SMEM = pl.BlockSpec(memory_space=pltpu.SMEM)
VMEM = pl.BlockSpec(memory_space=pltpu.VMEM)
SHARE = 16
PART = 1536
SHIFTS = (1, 3, 2)
BOTH = ("prow", "pcol")


def params():
    return pltpu.CompilerParams(vmem_limit_bytes=VMEM_LIMIT)


def z_shift(s):
    return [(z * 4 + y, (z + s) % 4 * 4 + y) for z in range(4) for y in range(4)]


def y_shift(s):
    return [(z * 4 + y, z * 4 + (y + s) % 4) for z in range(4) for y in range(4)]


def x_shift(s):
    return [(x * 2 + c, (x + s) % 4 * 2 + c) for x in range(4) for c in range(2)]


def split_shift(s, axis):
    pairs = []
    for p in range(8):
        along = z_shift(s) if (p + axis) % 2 == 0 else y_shift(s)
        pairs += [(p * 16 + a, p * 16 + b) for a, b in along]
    return pairs


def core_swap():
    return [(i, i ^ 1) for i in range(8)]


def cost(us):
    return pl.CostEstimate(flops=0, transcendentals=0, bytes_accessed=int(us * 3.5e6))


def read_half(place_ref, window_ref, buffer, sem):
    copies = []
    for n in range(4):
        part = place_ref[0] * 4 + lax.rem(place_ref[1] + n, 4)
        rows = pl.ds(pl.multiple_of(part * PART, PART), PART)
        copies.append(pltpu.make_async_copy(window_ref.at[rows, pl.ds(0, NB)], buffer.at[n], sem.at[n]))
    return copies


def cast_half(window, half, first):
    def body(place_ref, window_ref, out_ref, buffer, sem):
        copies = read_half(place_ref, window_ref, buffer, sem)
        for copy in copies:
            copy.start()
        for n in range(4):
            copies[n].wait()
            out_ref[n * PART : (n + 1) * PART, :] = buffer[n].astype(BF16)

    return pl.pallas_call(
        body,
        in_specs=[SMEM, HBM],
        out_specs=VMEM,
        out_shape=jax.ShapeDtypeStruct((4 * PART, NB), BF16),
        scratch_shapes=[pltpu.VMEM((4, PART, NB), F32), pltpu.SemaphoreType.DMA((4,))],
        compiler_params=params(),
        cost_estimate=cost(2.0),
        name="cast_half",
    )(jnp.stack([half, first]).astype(jnp.int32), window)


def pair_up(window, half, first, partners):
    def body(place_ref, window_ref, partners_ref, *refs):
        outs, buffer, sem = refs[:4], refs[4], refs[5]
        copies = read_half(place_ref, window_ref, buffer, sem)
        for copy in copies:
            copy.start()
        for n in range(4):
            outs[n][PART:, :] = partners_ref[n * PART : (n + 1) * PART, :]
        for n in range(4):
            copies[n].wait()
            outs[n][:PART, :] = buffer[n].astype(BF16)

    return pl.pallas_call(
        body,
        in_specs=[SMEM, HBM, VMEM],
        out_specs=[VMEM] * 4,
        out_shape=[jax.ShapeDtypeStruct((2 * PART, NB), BF16)] * 4,
        scratch_shapes=[pltpu.VMEM((4, PART, NB), F32), pltpu.SemaphoreType.DMA((4,))],
        compiler_params=params(),
        cost_estimate=cost(2.5),
        name="pair_up",
    )(jnp.stack([half, first]).astype(jnp.int32), window, partners)


def cut_shares(places, tiles):
    def body(places_ref, *refs):
        out_ref, stack = refs[4], refs[5]
        for n in range(4):
            stack[n * 6 * NB : (n + 1) * 6 * NB, :] = refs[n][...]

        def share(n):
            row = places_ref[n] * NB + places_ref[LOOK + 1] * SHARE
            return stack[pl.ds(pl.multiple_of(row, SHARE), SHARE), :]

        for n in range(LOOK):
            out_ref[2 * n * SHARE : (2 * n + 1) * SHARE, :] = share(0)
            out_ref[(2 * n + 1) * SHARE : (2 * n + 2) * SHARE, :] = share(n + 1)

    return pl.pallas_call(
        body,
        in_specs=[SMEM] + [VMEM] * 4,
        out_specs=VMEM,
        out_shape=jax.ShapeDtypeStruct((2 * LOOK * SHARE, NB), BF16),
        scratch_shapes=[pltpu.VMEM((24 * NB, NB), BF16)],
        compiler_params=params(),
        cost_estimate=cost(1.0),
        name="cut_shares",
    )(places, *tiles)


def pick(choice, arrays):
    return jnp.where(
        choice < 2, jnp.where(choice == 0, arrays[0], arrays[1]), jnp.where(choice == 2, arrays[2], arrays[3])
    )


def factor(places, shares):
    block_rows = 16

    def body(places_ref, *refs):
        low_ref, inv_ref, weights_ref, work, stack = refs[4:]
        for n in range(4):
            stack[n * 4 * SHARE : (n + 1) * 4 * SHARE, :] = refs[n][...]

        def tile_at(n):
            shares = []
            for p in range(8):
                row = lax.rem(places_ref[0] - p // 2 + 4, 4) * 4 * SHARE + (p % 2 * 2 + n) * SHARE
                shares.append(stack[pl.ds(pl.multiple_of(row, SHARE), SHARE), :])
            return jnp.concatenate(shares, 0)

        t = tile_at(0).astype(F32)
        row = lax.broadcasted_iota(jnp.int32, (NB, NB), 0)
        col = lax.broadcasted_iota(jnp.int32, (NB, NB), 1)
        work[:, :NB] = 0.5 * (t + t.T)
        work[:, NB:] = jnp.where(row == col, 1.0, 0.0)
        sub = lax.broadcasted_iota(jnp.int32, (block_rows, NB), 0)
        upper = []
        inverse = []
        for b in range(NB // block_rows):
            base = block_rows * b
            left = work[base : base + block_rows, :NB]
            right = work[base : base + block_rows, NB:]
            columns = [
                jnp.broadcast_to(left[:, base + s : base + s + 1], (block_rows, NB)) for s in range(block_rows)
            ]
            done_left = left
            done_right = right
            for s in range(block_rows):
                scale = lax.rsqrt(columns[s][s : s + 1, :])
                weight = columns[s] * scale
                for r in range(s + 1, block_rows):
                    columns[r] = columns[r] - weight * weight[r : r + 1, :]
                below = jnp.where(sub > s, weight, 0.0)
                line_left = left[s : s + 1, :] * scale
                line_right = right[s : s + 1, :] * scale
                done_left = jnp.where(sub == s, line_left, done_left)
                done_right = jnp.where(sub == s, line_right, done_right)
                left = left - below * line_left
                right = right - below * line_right
            upper.append(done_left)
            inverse.append(done_right)
            if base + block_rows < NB:
                work[...] -= lax.dot_general(
                    done_left,
                    jnp.concatenate([done_left, done_right], 1),
                    (((0,), (0,)), ((), ())),
                    precision=HI,
                    preferred_element_type=F32,
                )
        up = jnp.concatenate(upper, 0)
        low_ref[...] = jnp.where(row >= col, up.T, 0.0)
        inv = jnp.where(row >= col, jnp.concatenate(inverse, 0), 0.0)
        inv_ref[...] = inv
        tile = tile_at(1).astype(F32)
        half = lax.dot_general(inv, tile, (((1,), (1,)), ((), ())), precision=HI, preferred_element_type=F32)
        full = lax.dot_general(inv, half, (((0,), (0,)), ((), ())), precision=HI, preferred_element_type=F32)
        weights_ref[...] = full.astype(BF16)

    return pl.pallas_call(
        body,
        in_specs=[SMEM] + [VMEM] * 4,
        out_specs=[VMEM] * 3,
        out_shape=[
            jax.ShapeDtypeStruct((NB, NB), F32),
            jax.ShapeDtypeStruct((NB, NB), F32),
            jax.ShapeDtypeStruct((NB, NB), BF16),
        ],
        scratch_shapes=[pltpu.VMEM((NB, 2 * NB), F32), pltpu.VMEM((16 * SHARE, NB), BF16)],
        compiler_params=params(),
        cost_estimate=cost(10.0),
        name="factor",
    )(places, *shares)


def column_copies(source, buffer, target, lane, sem, count):
    size = buffer.shape[0] // count
    lanes = pl.ds(pl.multiple_of(lane * NB, NB), NB)
    into, out = [], []
    for n in range(count):
        rows = pl.ds(n * size, size)
        into.append(pltpu.make_async_copy(source.at[rows, lanes], buffer.at[rows], sem.at[0, n]))
        out.append(pltpu.make_async_copy(buffer.at[rows], target.at[rows, lanes], sem.at[1, n]))
    return into, out


def keep_column(scalars, window):
    def body(s_ref, window_ref, out_ref, buffer, sem):
        @pl.when(s_ref[2] == 0)
        def _():
            into, out = column_copies(window_ref, buffer, out_ref, 1 - s_ref[3], sem, 4)
            for copy in into:
                copy.start()
            for first, second in zip(into, out):
                first.wait()
                second.start()
            for copy in out:
                copy.wait()

    return pl.pallas_call(
        body,
        in_specs=[SMEM, HBM],
        out_specs=HBM,
        out_shape=jax.ShapeDtypeStruct(window.shape, F32),
        scratch_shapes=[pltpu.VMEM((window.shape[0], NB), F32), pltpu.SemaphoreType.DMA((2, 4))],
        compiler_params=params(),
        cost_estimate=cost(5.5),
        name="keep_column",
    )(scalars, window)


def write_panel(scalars, window, low, inv, out):
    count = 4
    size = window.shape[0] // count

    def body(s_ref, window_ref, low_ref, inv_ref, _, out_ref, buffer, sem):
        k, p = s_ref[0], s_ref[1]

        @pl.when(s_ref[2] == 1)
        def _():
            into, out = column_copies(window_ref, buffer, out_ref, 0, sem, count)
            for copy in into:
                copy.start()
            high = inv_ref[...].astype(BF16)
            for n in range(count):
                into[n].wait()
                if n == 0:
                    head = buffer[0 : 2 * NB, :]
                for t in range(size // 256):
                    rows = slice(n * size + t * 256, n * size + (t + 1) * 256)
                    buffer[rows, :] = lax.dot_general(
                        buffer[rows, :].astype(BF16), high, (((1,), (1,)), ((), ())), preferred_element_type=F32
                    )
                if n == 0:
                    for slot in range(2):
                        tile = slot * 8 + p
                        rows = pl.ds(slot * NB, NB)

                        @pl.when(tile == k)
                        def _():
                            buffer[rows, :] = low_ref[...]

                        @pl.when(tile < k)
                        def _():
                            buffer[rows, :] = head[slot * NB : (slot + 1) * NB, :]

                out[n].start()
            for copy in out:
                copy.wait()

    return pl.pallas_call(
        body,
        in_specs=[SMEM, HBM, VMEM, VMEM, HBM],
        out_specs=HBM,
        out_shape=jax.ShapeDtypeStruct(window.shape, F32),
        scratch_shapes=[pltpu.VMEM((window.shape[0], NB), F32), pltpu.SemaphoreType.DMA((2, count))],
        input_output_aliases={4: 0},
        compiler_params=params(),
        cost_estimate=cost(1.0),
        name="write_panel",
    )(scalars, window, low, inv, out)


def hold(scalars, window, places):
    n = len(places)

    def body(s_ref, window_ref, out_ref, sem):
        lanes = pl.ds(pl.multiple_of(s_ref[3] * NB, NB), NB)
        copies = [
            pltpu.make_async_copy(
                window_ref.at[pl.ds(pl.multiple_of(s_ref[5 + m] * PART, PART), PART), lanes], out_ref.at[m], sem.at[m]
            )
            for m in range(n)
        ]
        for copy in copies:
            copy.start()
        for copy in copies:
            copy.wait()

    return pl.pallas_call(
        body,
        in_specs=[SMEM, HBM],
        out_specs=VMEM,
        out_shape=jax.ShapeDtypeStruct((n, PART, NB), F32),
        scratch_shapes=[pltpu.SemaphoreType.DMA((n,))],
        compiler_params=params(),
        cost_estimate=cost(1.5),
        name="hold",
    )(jnp.concatenate([scalars, jnp.stack(places).astype(jnp.int32)]), window)


def update(scalars, window, weights, parts, places, out, held=None):
    n = len(parts)
    size = PART // 2
    blocks = [(m, i) for m in range(n) for i in range(2)]
    s_all = jnp.concatenate([scalars, jnp.stack(places).astype(jnp.int32)])
    source = window if held is None else held[0]

    def body(s_ref, source_ref, weight_ref, *refs):
        panels, out_ref = refs[:n], refs[n + 1]
        buffer, sem = refs[n + 2 :]
        p, j = s_ref[1], s_ref[4]
        lanes = pl.ds(pl.multiple_of(s_ref[3] * NB, NB), NB)

        def rows(m, i):
            return pl.ds(pl.multiple_of(s_ref[5 + m] * PART + i * size, size), size)

        def read(m, i):
            return pltpu.make_async_copy(source_ref.at[rows(m, i), lanes], buffer.at[m, i], sem.at[0, m, i])

        def write(m, i):
            return pltpu.make_async_copy(buffer.at[m, i], out_ref.at[rows(m, i), lanes], sem.at[1, m, i])

        if held is None:
            for m, i in blocks:
                read(m, i).start()
        for m, i in blocks:
            first = parts[m][1] * PART + i * size
            if held is None:
                read(m, i).wait()
            for t in range(size // 256):
                change = lax.dot_general(
                    panels[m][first + t * 256 : first + (t + 1) * 256, :],
                    weight_ref[...],
                    (((1,), (0,)), ((), ())),
                    preferred_element_type=F32,
                )
                for u in range(2):
                    at = t * 256 + u * NB
                    tile = (s_ref[5 + m] * (PART // NB) + (i * size + at) // NB) * 8 + p
                    if held is None:
                        old = buffer[m, i, at : at + NB, :]
                    else:
                        old = source_ref[held[1] + m, i * size + at : i * size + at + NB, :]
                    buffer[m, i, at : at + NB, :] = old - jnp.where(tile >= j, change[u * NB : (u + 1) * NB, :], 0.0)
            write(m, i).start()
        for m, i in blocks:
            write(m, i).wait()

    return pl.pallas_call(
        body,
        in_specs=[SMEM, HBM if held is None else VMEM, VMEM] + [VMEM] * n + [HBM],
        out_specs=HBM,
        out_shape=jax.ShapeDtypeStruct(window.shape, F32),
        scratch_shapes=[
            pltpu.VMEM((n, 2, size, NB), F32),
            pltpu.SemaphoreType.DMA((2, n, 2)),
        ],
        input_output_aliases={3 + n: 0},
        compiler_params=params(),
        cost_estimate=cost(1.0 + 0.8 * n),
        name="update",
    )(s_all, source, weights, *[part[0] for part in parts], out)


def turn(s):
    return [(n * 2 + c, (n + (s if c == 0 else -s)) % 4 * 2 + c) for n in range(4) for c in range(2)]


def pair_of(block, c):
    partner = lax.ppermute(block, "prow", core_swap())
    return jnp.where(c == 0, jnp.concatenate([block, partner]), jnp.concatenate([partner, block]))


def over_rows(block, pair, c):
    n = block.shape[0]
    beside = lax.ppermute(pair, "prow", turn(1))
    across = lax.ppermute(block, "prow", x_shift(2))
    got = jnp.concatenate([beside, across])
    other = lax.ppermute(got, "prow", core_swap())
    far = jnp.where(
        c == 0, jnp.concatenate([across, other[2 * n :]]), jnp.concatenate([other[2 * n :], across])
    )
    one = jnp.where(c == 0, beside, other[: 2 * n])
    three = jnp.where(c == 0, other[: 2 * n], beside)
    return [pair, one, far, three]


def body(window, panel_index):
    k = panel_index[0]
    p = lax.axis_index("prow")
    q = lax.axis_index("pcol")
    z, y = q // 4, q % 4
    x, c = p // 2, p % 2
    z0, y0 = k // 4, k % 4
    dz, dy = (z - z0) % 4, (y - y0) % 4
    slot = jnp.where(q <= k, 1, 0)
    j = slot * 16 + q
    scalars = jnp.stack([k, p, jnp.where(q == k, 1, 0), slot, j]).astype(jnp.int32)

    along, across = jnp.where(c == 0, z, y), jnp.where(c == 0, y, z)
    d_along, d_across = jnp.where(c == 0, dz, dy), jnp.where(c == 0, dy, dz)
    others = lax.ppermute(cast_half(window, 1 - c, across), "prow", core_swap())
    own = lax.dynamic_slice(window, (k // 8 * NB, 0), (3 * NB, NB)).astype(BF16)
    pair = pair_of(own, c)
    pair, others = lax.optimization_barrier((pair, others))
    messages = pair_up(window, c, along, others)
    messages, own, pair = lax.optimization_barrier((messages, own, pair))

    moved = [messages[0]] + [lax.ppermute(messages[s], BOTH, split_shift(s, 0)) for s in (1, 2, 3)]

    tiles = over_rows(own, pair, c)
    column = jnp.arange(LOOK)
    look = jnp.concatenate([jnp.reshape(k, (1,)), column + jnp.where(column <= k, 16, 0)])
    at = (x - look % 8 // 2) % 4 * 6 + look % 2 * 3 + look // 8 - k // 8
    shares = cut_shares(jnp.concatenate([at, jnp.reshape(p, (1,))]).astype(jnp.int32), tiles)
    shares = lax.all_to_all(shares, "pcol", 0, 0, tiled=True)
    moved, shares = lax.optimization_barrier((moved, shares))
    message = pick(d_along, moved)

    moved = [message] + [lax.ppermute(message, BOTH, split_shift(s, 1)) for s in (1, 2, 3)]
    share = lax.dynamic_slice(shares, (k * 2 * SHARE, 0), (2 * SHARE, NB))
    low, inv, weights = factor(jnp.reshape(x, (1,)).astype(jnp.int32), over_rows(share, pair_of(share, c), c))
    out = keep_column(scalars, window)
    out = write_panel(scalars, window, low, inv, out)
    moved, out, weights = lax.optimization_barrier((moved, out, weights))
    message = pick(d_across, moved)

    gathered = [message] + [lax.ppermute(message, BOTH, split_shift(s, 0)) for s in (1, 2, 3)]

    def places_of(s):
        return [4 * c + (along - s) % 4, 4 * (1 - c) + (across - s) % 4]

    def swapped(block):
        return lax.ppermute(block, "prow", core_swap())

    out = update(scalars, window, weights, [(gathered[0], 0), (swapped(gathered[0]), 1)], places_of(0), out)
    gathered, out = lax.optimization_barrier((gathered, out))
    others = [swapped(gathered[s]) for s in SHIFTS]
    out = update(
        scalars, window, weights, [(gathered[s], 0) for s in SHIFTS], [places_of(s)[0] for s in SHIFTS], out
    )
    others, out = lax.optimization_barrier((others, out))
    return update(
        scalars, window, weights, [(other, 1) for other in others], [places_of(s)[1] for s in SHIFTS], out
    )


def solution(mesh):
    return jax.shard_map(
        body,
        mesh=mesh,
        in_specs=(P("prow", "pcol"), P()),
        out_specs=P("prow", "pcol"),
        check_vma=False,
    )
```

time: 249 us -> 103 us (0.41)
  waiting for transfers between devices: 84.7 us -> 31.8 us
  local copies, waits for them, and re-layouts: 52.4 us -> 3.99 us
  blocking collectives: 38.4 us -> 0 us
  starting transfers between devices: 0.01 us -> 31.8 us
  other arithmetic: 35.3 us -> 3.85 us
  Pallas kernels: 0 us -> 29.1 us
  matrix products: 23.7 us -> 0 us
  between operations: 14.4 us -> 1.13 us
    psum x1 -> x0, waiting for transfers between devices: 84.6 us -> none  [from_root(): return lax.psum(block, axis)]
    pallas_call x0 -> x9, Pallas kernels: none -> 29.1 us  [the longest x3 12 us: update(): pl.pallas_call(body, in_specs=[SMEM, HBM if held is None else VMEM, VMEM]...]
    ppermute x0 -> x22, waiting for transfers between devices: none -> 25.1 us  [the longest x3 16.2 us: body(): lax.ppermute(message, BOTH, split_shift(s, 0))]
    ppermute x0 -> x22, starting transfers between devices: none -> 24.7 us  [the longest x3 4.99 us: body(): lax.ppermute(messages[s], BOTH, split_shift(s, 0))]
    psum x1 -> x0, blocking collectives: 23.6 us -> none  [from_root(): return lax.psum(block, axis)]
    another operation x5 -> x2, other arithmetic: 22.9 us -> 0.15 us  [the longest x1 0.08 us: pair_up(): jnp.stack([half, first]).astype(jnp.int32)]
    unnamed x14 -> x8, local copies, waits for them, and re-layouts: 20.2 us -> 2.7 us
    all_gather x1 -> x0, blocking collectives: 14.8 us -> none  [body(): lax.all_gather(lax.dynamic_slice_in_dim(low, look_start, per_row * NB, 0)...]
  transfers between devices with their start and end apart: 1 -> 23, of which waited for: 1 -> 9; matrix products, arithmetic and copies ran while one was open for 5% -> 4% of each run, Pallas kernels for 0% -> 19%
where the time goes in v2:
time: 103 us; the launch traced here: 102 us
  starting transfers between devices  31.8 us (31%)
  waiting for transfers between devices  31.8 us (31%)
  Pallas kernels  29.1 us (28%)
  local copies, waits for them, and re-layouts  3.99 us (4%)
  other arithmetic  3.85 us (4%)
  between operations  1.13 us (1%)
    ppermute x3, waiting for transfers between devices, body(): lax.ppermute(message, BOTH, split_shift(s, 0))  16.2 us
    pallas_call x3, Pallas kernels, update(): pl.pallas_call(body, in_specs=[SMEM, HBM if held is None else VMEM, VMEM]...  12 us
    all_to_all x1, starting transfers between devices, body(): shares = lax.all_to_all(shares, 'pcol', 0, 0, tiled=True)  7.11 us
    all_to_all x1, waiting for transfers between devices, body(): shares = lax.all_to_all(shares, 'pcol', 0, 0, tiled=True)  6.76 us
    ppermute x2, waiting for transfers between devices, over_rows(): across = lax.ppermute(block, 'prow', x_shift(2))  5.34 us
    pallas_call x1, Pallas kernels, write_panel(): pl.pallas_call(body, in_specs=[SMEM, HBM, VMEM, VMEM, HBM], out_specs=HBM...  5.15 us
    pallas_call x1, Pallas kernels, factor(): pl.pallas_call(body, in_specs=[SMEM] + [VMEM] * 4, out_specs=[VMEM] * 3,...  5.09 us
    ppermute x3, starting transfers between devices, body(): lax.ppermute(messages[s], BOTH, split_shift(s, 0))  4.99 us
  transfers between devices with their start and end apart: 23, of which 9 were waited for; matrix products, arithmetic and copies ran while one was open for 4% of the time, Pallas kernels for 19%

profile of v2, /device:TPU:1, one launch (start us, length us, event | category | flops | bytes accessed | tf_op | source)
XLA Modules:
  0.0 101.7 jit_solution(16383057177971284488)
XLA Ops:
  0.1 2.5 %cast_half.1 = bf16[6144,128]{1,0:T(8,128)(2,1)S(1)} custom-call(s32[2]{0:T(128)S(1)} %pad_add_fusion.1.place_ref, f32[12288,256]{1,0:T(8,128)} %source_ref.5), custom_call_target="tpu_custom_call" | custom-call | bytes 7000000 | tf_op jit(solution)/shard_map/cast_half/pallas_call | solution.py:74
  2.6 1.5 %collective-permute-start.1 = (bf16[6144,128]{1,0:T(8,128)(2,1)S(1)}, bf16[6144,128]{1,0:T(8,128)(2,1)S(1)}, u32[]{:S(2)}, u32[]{:S(2)}) collective-permute-start(bf16[6144,128]{1,0:T(8,128)(2,1)S(1)} %cast_half.1), channel_id=1, source_target_pairs={{0,16},{16,0},{32,48},{48,32},{64,80},{80,64},{96,112},{112,96},{1... | collective-permute-start | bytes 4718600 | tf_op jit(solution)/shard_map/ppermute | solution.py:438
  5.9 1.4 %collective-permute-done = bf16[384,128]{1,0:T(8,128)(2,1)S(1)} collective-permute-done((bf16[384,128]{1,0:T(8,128)(2,1)S(1)}, bf16[384,128]{1,0:T(8,128)(2,1)S(1)}, u32[]{:S(2)}, u32[]{:S(2)}) %collective-permute-start) | collective-permute-done | bytes 98336 | tf_op jit(solution)/shard_map/ppermute | solution.py:406
  7.3 2.5 %pair_up.1 = (bf16[3072,128]{1,0:T(8,128)(2,1)S(1)}, bf16[3072,128]{1,0:T(8,128)(2,1)S(1)}, bf16[3072,128]{1,0:T(8,128)(2,1)S(1)}, bf16[3072,128]{1,0:T(8,128)(2,1)S(1)}) custom-call(s32[2]{0:T(128)S(1)} %pad_add_fusion.place_ref, f32[12288,256]{1,0:T(8,128)} %source_ref.5, bf16[6144,128]{1,0:T(8,128)(2,1)S(1)} %collective-permute-done.1.partners_ref), custom_call_target="tpu_custom_call" | custom-call | bytes 8750000 | tf_op jit(solution)/shard_map/pair_up/pallas_call | solution.py:98
  11.6 2.6 %collective-permute-start.5 = (bf16[768,128]{1,0:T(8,128)(2,1)S(1)}, bf16[768,128]{1,0:T(8,128)(2,1)S(1)}, u32[]{:S(2)}, u32[]{:S(2)}) collective-permute-start(bf16[768,128]{1,0:T(8,128)(2,1)S(1)} %maximum_select_fusion.refs_0_), channel_id=1, source_target_pairs={{0,32},{16,112},{32,64},{48,16},{64,96},{80,48},{96,0},{112,80},{1... | collective-permute-start | bytes 589832 | tf_op jit(solution)/shard_map/ppermute | solution.py:412
  14.6 1.3 %collective-permute-start.2 = (bf16[3072,128]{1,0:T(8,128)(2,1)}, bf16[3072,128]{1,0:T(8,128)(2,1)S(1)}, u32[]{:S(2)}, u32[]{:S(2)}) collective-permute-start(bf16[3072,128]{1,0:T(8,128)(2,1)} %copy-done.1), channel_id=1, source_target_pairs={{0,4},{1,5},{2,6},{3,7},{4,8},{5,9},{6,10},{7,11},{8,12},{9,13},{1... | collective-permute-start | bytes 2359304 | tf_op jit(solution)/shard_map/ppermute | solution.py:445
  15.9 2.6 %collective-permute-start.3 = (bf16[3072,128]{1,0:T(8,128)(2,1)}, bf16[3072,128]{1,0:T(8,128)(2,1)S(1)}, u32[]{:S(2)}, u32[]{:S(2)}) collective-permute-start(bf16[3072,128]{1,0:T(8,128)(2,1)} %copy-done), channel_id=1, source_target_pairs={{0,8},{1,9},{2,10},{3,11},{4,12},{5,13},{6,14},{7,15},{8,0},{9,1},... | collective-permute-start | bytes 2359304 | tf_op jit(solution)/shard_map/ppermute | solution.py:445
  21.7 2.1 %collective-permute-start.7 = (bf16[1152,128]{1,0:T(8,128)(2,1)S(1)}, bf16[1152,128]{1,0:T(8,128)(2,1)S(1)}, u32[]{:S(2)}, u32[]{:S(2)}) collective-permute-start(bf16[1152,128]{1,0:T(8,128)(2,1)S(1)} %pad_maximum_fusion), channel_id=1, source_target_pairs={{0,16},{16,0},{32,48},{48,32},{64,80},{80,64},{96,112},{112,96},{1... | collective-permute-start | bytes 884744 | tf_op jit(solution)/shard_map/ppermute | solution.py:415
  26.1 1.3 %cut_shares.1 = bf16[512,128]{1,0:T(8,128)(2,1)} custom-call(s32[18]{0:T(128)S(1)} %pad_add_fusion.3.places_ref, bf16[768,128]{1,0:T(8,128)(2,1)S(1)} %maximum_select_fusion.refs_0_, bf16[768,128]{1,0:T(8,128)(2,1)S(1)} %get-tuple-element.74.refs_1_, bf16[768,128]{1,0:T(8,128)(2,1)S(1)} %get-tuple-element.77.refs_2_, ...), custom_call_target="tpu_custom_call" | custom-call | bytes 3500000 | tf_op jit(solution)/shard_map/cut_shares/pallas_call | solution.py:124
  27.3 7.1 %all-to-all-start = ((bf16[16,32,128]{2,1,0:T(8,128)(2,1)}), bf16[16,32,128]{2,1,0:T(8,128)(2,1)S(1)}, u32[]{:S(2)}, u32[]{:S(2)}) async-start(bf16[16,32,128]{2,1,0:T(8,128)(2,1)} %bitcast.12), calls=%async_computation | async-start | bytes 262144 | tf_op jit(solution)/shard_map/all_to_all | solution.py:452
  34.5 6.8 %all-to-all-done = bf16[16,32,128]{2,1,0:T(8,128)(2,1)S(1)} async-done(((bf16[16,32,128]{2,1,0:T(8,128)(2,1)}), bf16[16,32,128]{2,1,0:T(8,128)(2,1)S(1)}, u32[]{:S(2)}, u32[]{:S(2)}) %all-to-all-start) | async-done | bytes 131104 | tf_op jit(solution)/shard_map/all_to_all | solution.py:452
  41.3 1.3 %select_select_fusion.1 = bf16[3072,128]{1,0:T(8,128)(2,1)S(1)} fusion(bf16[3072,128]{1,0:T(8,128)(2,1)S(1)} %collective-permute-done.3, bf16[3072,128]{1,0:T(8,128)(2,1)} %collective-permute-done.4, bf16[3072,128]{1,0:T(8,128)(2,1)S(1)} %get-tuple-element.51, bf16[3072,128]{1,0:T(8,128)(2,1)S(1)} %collective-permute-done.2, pred[]{:T(512)S(6)} %eq.50, ...), kind=kLoop, calls=%fused_computation.1 | loop fusion | flops 1179648 | bytes 3932163 | tf_op jit(solution)/shard_map/jit(_where)/select_n | solution.py:137
  44.6 3.2 %collective-permute-start.11 = (bf16[32,128]{1,0:T(8,128)(2,1)S(1)}, bf16[32,128]{1,0:T(8,128)(2,1)S(1)}, u32[]{:S(2)}, u32[]{:S(2)}) collective-permute-start(bf16[32,128]{1,0:T(8,128)(2,1)S(1)} %constant_dynamic-slice_fusion), channel_id=1, source_target_pairs={{0,16},{16,0},{32,48},{48,32},{64,80},{80,64},{96,112},{112,96},{1... | collective-permute-start | bytes 24584 | tf_op jit(solution)/shard_map/ppermute | solution.py:406
  48.6 1.2 %collective-permute-start.12 = (bf16[64,128]{1,0:T(8,128)(2,1)S(1)}, bf16[64,128]{1,0:T(8,128)(2,1)S(1)}, u32[]{:S(2)}, u32[]{:S(2)}) collective-permute-start(bf16[64,128]{1,0:T(8,128)(2,1)S(1)} %maximum_select_fusion.2.refs_0_), channel_id=1, source_target_pairs={{0,32},{16,112},{32,64},{48,16},{64,96},{80,48},{96,0},{112,80},{1... | collective-permute-start | bytes 49160 | tf_op jit(solution)/shard_map/ppermute | solution.py:412
  49.8 4.2 %collective-permute-done.13 = bf16[32,128]{1,0:T(8,128)(2,1)S(1)} collective-permute-done((bf16[32,128]{1,0:T(8,128)(2,1)S(1)}, bf16[32,128]{1,0:T(8,128)(2,1)S(1)}, u32[]{:S(2)}, u32[]{:S(2)}) %collective-permute-start.13) | collective-permute-done | bytes 8224 | tf_op jit(solution)/shard_map/ppermute | solution.py:413
  55.3 5.1 %factor.1 = (f32[128,128]{1,0:T(8,128)S(1)}, f32[128,128]{1,0:T(8,128)S(1)}, bf16[128,128]{1,0:T(8,128)(2,1)S(1)}) custom-call(s32[1]{0:T(128)} %bitcast.14.places_ref, bf16[64,128]{1,0:T(8,128)(2,1)S(1)} %maximum_select_fusion.2.refs_0_, bf16[64,128]{1,0:T(8,128)(2,1)S(1)} %get-tuple-element.76.refs_1_, bf16[64,128]{1,0:T(8,128)(2,1)S(1)} %maximum_select_fusion.3.refs_2_, ...), custom_call_target="tpu_custom_call" | custom-call | bytes 35000000 | tf_op jit(solution)/shard_map/factor/pallas_call | solution.py:205
  60.4 5.2 %write_panel.1.refs_2_ = f32[12288,256]{1,0:T(8,128)} custom-call(s32[5]{0:T(128)S(1)} %stack.70.s_ref, f32[12288,256]{1,0:T(8,128)} %source_ref.5, f32[128,128]{1,0:T(8,128)S(1)} %get-tuple-element.56.low_ref, f32[128,128]{1,0:T(8,128)S(1)} %get-tuple-element.57.inv_ref, f32[12288,256]{1,0:T(8,128)} %keep_column.1._), custom_call_target="tpu_custom_call", output_to_operand_aliasing={{}: (4, {})} | custom-call | bytes 3500000 | tf_op jit(solution)/shard_map/write_panel/pallas_call | solution.py:296
  66.6 1.8 %collective-permute-start.18 = (bf16[3072,128]{1,0:T(8,128)(2,1)S(1)}, bf16[3072,128]{1,0:T(8,128)(2,1)}, u32[]{:S(2)}, u32[]{:S(2)}) collective-permute-start(bf16[3072,128]{1,0:T(8,128)(2,1)S(1)} %select_select_fusion.refs_0_), channel_id=1, source_target_pairs={{0,16},{16,0},{32,48},{48,32},{64,80},{80,64},{96,112},{112,96},{1... | collective-permute-start | bytes 2359304 | tf_op jit(solution)/shard_map/ppermute | solution.py:470
  68.4 2.5 %collective-permute-start.17 = (bf16[3072,128]{1,0:T(8,128)(2,1)S(1)}, bf16[3072,128]{1,0:T(8,128)(2,1)S(1)}, u32[]{:S(2)}, u32[]{:S(2)}) collective-permute-start(bf16[3072,128]{1,0:T(8,128)(2,1)S(1)} %select_select_fusion.refs_0_), channel_id=1, source_target_pairs={{0,12},{1,13},{2,14},{3,15},{4,0},{5,1},{6,2},{7,3},{8,4},{9,5},{1... | collective-permute-start | bytes 2359304 | tf_op jit(solution)/shard_map/ppermute | solution.py:464
  72.0 3.8 %update.3.refs_3_ = f32[12288,256]{1,0:T(8,128)} custom-call(s32[7]{0:T(128)S(1)} %concatenate.61.s_ref, f32[12288,256]{1,0:T(8,128)} %source_ref.5, bf16[128,128]{1,0:T(8,128)(2,1)S(1)} %get-tuple-element.59.weight_ref, bf16[3072,128]{1,0:T(8,128)(2,1)S(1)} %select_select_fusion.refs_0_, ...), custom_call_target="tpu_custom_call", output_to_operand_aliasing={{}: (5, {})} | custom-call | bytes 9100000 | tf_op jit(solution)/shard_map/update/pallas_call | solution.py:385
  75.8 12.5 %collective-permute-done.17.refs_1_ = bf16[3072,128]{1,0:T(8,128)(2,1)S(1)} collective-permute-done((bf16[3072,128]{1,0:T(8,128)(2,1)S(1)}, bf16[3072,128]{1,0:T(8,128)(2,1)S(1)}, u32[]{:S(2)}, u32[]{:S(2)}) %collective-permute-start.17) | collective-permute-done | bytes 786464 | tf_op jit(solution)/shard_map/ppermute | solution.py:464
  88.3 3.7 %collective-permute-done.15.refs_0_ = bf16[3072,128]{1,0:T(8,128)(2,1)S(1)} collective-permute-done((bf16[3072,128]{1,0:T(8,128)(2,1)S(1)}, bf16[3072,128]{1,0:T(8,128)(2,1)S(1)}, u32[]{:S(2)}, u32[]{:S(2)}) %collective-permute-start.15) | collective-permute-done | bytes 786464 | tf_op jit(solution)/shard_map/ppermute | solution.py:464
  93.3 3.7 %update.4.refs_3_ = f32[12288,256]{1,0:T(8,128)} custom-call(s32[8]{0:T(128)S(1)} %concatenate.62.s_ref, f32[12288,256]{1,0:T(8,128)} %source_ref.5, bf16[128,128]{1,0:T(8,128)(2,1)S(1)} %get-tuple-element.59.weight_ref, bf16[3072,128]{1,0:T(8,128)(2,1)S(1)} %collective-permute-done.15.refs_0_, ...), custom_call_target="tpu_custom_call", output_to_operand_aliasing={{}: (6, {})} | custom-call | bytes 11900000 | tf_op jit(solution)/shard_map/update/pallas_call | solution.py:385
  97.0 4.5 %update.5 = f32[12288,256]{1,0:T(8,128)} custom-call(s32[8]{0:T(128)S(1)} %concatenate.48.s_ref, f32[12288,256]{1,0:T(8,128)} %source_ref.5, bf16[128,128]{1,0:T(8,128)(2,1)S(1)} %get-tuple-element.59.weight_ref, bf16[3072,128]{1,0:T(8,128)(2,1)S(1)} %collective-permute-done.19.refs_0_, ...), custom_call_target="tpu_custom_call", output_to_operand_aliasing={{}: (6, {})} | custom-call | bytes 11900000 | tf_op jit(solution)/shard_map/update/pallas_call | solution.py:385
  (61 shorter events, 16.6 us)
Async XLA Ops:
  2.6 4.7 %collective-permute-start.1 = (bf16[6144,128]{1,0:T(8,128)(2,1)S(1)}, bf16[6144,128]{1,0:T(8,128)(2,1)S(1)}, u32[]{:S(2)}, u32[]{:S(2)}) collective-permute-start(bf16[6144,128]{1,0:T(8,128)(2,1)S(1)} %cast_half.1), channel_id=1, source_target_pairs={{0,16},{16,0},{32,48},{48,32},{64,80},{80,64},{96,112},{112,96},{1... | collective-permute-start | bytes 4718600 | tf_op jit(solution)/shard_map/ppermute | solution.py:438
  5.7 5.9 %copy-start.3 = (bf16[384,128]{1,0:T(8,128)(2,1)}, bf16[384,128]{1,0:T(8,128)(2,1)S(1)}, u32[]{:S(2)}) copy-start(bf16[384,128]{1,0:T(8,128)(2,1)S(1)} %dynamic-slice_convert_fusion) | copy-start | bytes 294916
  5.7 1.5 %collective-permute-start = (bf16[384,128]{1,0:T(8,128)(2,1)S(1)}, bf16[384,128]{1,0:T(8,128)(2,1)S(1)}, u32[]{:S(2)}, u32[]{:S(2)}) collective-permute-start(bf16[384,128]{1,0:T(8,128)(2,1)S(1)} %dynamic-slice_convert_fusion), channel_id=1, source_target_pairs={{0,16},{16,0},{32,48},{48,32},{64,80},{80,64},{96,112},{112,96},{1... | collective-permute-start | bytes 294920 | tf_op jit(solution)/shard_map/ppermute | solution.py:406
  11.6 9.2 %collective-permute-start.5 = (bf16[768,128]{1,0:T(8,128)(2,1)S(1)}, bf16[768,128]{1,0:T(8,128)(2,1)S(1)}, u32[]{:S(2)}, u32[]{:S(2)}) collective-permute-start(bf16[768,128]{1,0:T(8,128)(2,1)S(1)} %maximum_select_fusion.refs_0_), channel_id=1, source_target_pairs={{0,32},{16,112},{32,64},{48,16},{64,96},{80,48},{96,0},{112,80},{1... | collective-permute-start | bytes 589832 | tf_op jit(solution)/shard_map/ppermute | solution.py:412
  14.1 6.7 %collective-permute-start.6 = (bf16[384,128]{1,0:T(8,128)(2,1)}, bf16[384,128]{1,0:T(8,128)(2,1)}, u32[]{:S(2)}, u32[]{:S(2)}) collective-permute-start(bf16[384,128]{1,0:T(8,128)(2,1)} %copy-done.3), channel_id=1, source_target_pairs={{0,64},{16,80},{32,96},{48,112},{64,0},{80,16},{96,32},{112,48},{1... | collective-permute-start | bytes 294920 | tf_op jit(solution)/shard_map/ppermute | solution.py:413
  14.6 26.7 %collective-permute-start.2 = (bf16[3072,128]{1,0:T(8,128)(2,1)}, bf16[3072,128]{1,0:T(8,128)(2,1)S(1)}, u32[]{:S(2)}, u32[]{:S(2)}) collective-permute-start(bf16[3072,128]{1,0:T(8,128)(2,1)} %copy-done.1), channel_id=1, source_target_pairs={{0,4},{1,5},{2,6},{3,7},{4,8},{5,9},{6,10},{7,11},{8,12},{9,13},{1... | collective-permute-start | bytes 2359304 | tf_op jit(solution)/shard_map/ppermute | solution.py:445
  15.9 25.4 %collective-permute-start.3 = (bf16[3072,128]{1,0:T(8,128)(2,1)}, bf16[3072,128]{1,0:T(8,128)(2,1)S(1)}, u32[]{:S(2)}, u32[]{:S(2)}) collective-permute-start(bf16[3072,128]{1,0:T(8,128)(2,1)} %copy-done), channel_id=1, source_target_pairs={{0,8},{1,9},{2,10},{3,11},{4,12},{5,13},{6,14},{7,15},{8,0},{9,1},... | collective-permute-start | bytes 2359304 | tf_op jit(solution)/shard_map/ppermute | solution.py:445
  18.6 22.7 %collective-permute-start.4 = (bf16[3072,128]{1,0:T(8,128)(2,1)S(1)}, bf16[3072,128]{1,0:T(8,128)(2,1)}, u32[]{:S(2)}, u32[]{:S(2)}) collective-permute-start(bf16[3072,128]{1,0:T(8,128)(2,1)S(1)} %get-tuple-element.48), channel_id=1, source_target_pairs={{0,12},{1,13},{2,14},{3,15},{4,0},{5,1},{6,2},{7,3},{8,4},{9,5},{1... | collective-permute-start | bytes 2359304 | tf_op jit(solution)/shard_map/ppermute | solution.py:445
  21.7 3.3 %collective-permute-start.7 = (bf16[1152,128]{1,0:T(8,128)(2,1)S(1)}, bf16[1152,128]{1,0:T(8,128)(2,1)S(1)}, u32[]{:S(2)}, u32[]{:S(2)}) collective-permute-start(bf16[1152,128]{1,0:T(8,128)(2,1)S(1)} %pad_maximum_fusion), channel_id=1, source_target_pairs={{0,16},{16,0},{32,48},{48,32},{64,80},{80,64},{96,112},{112,96},{1... | collective-permute-start | bytes 884744 | tf_op jit(solution)/shard_map/ppermute | solution.py:415
  27.3 14.0 %all-to-all-start = ((bf16[16,32,128]{2,1,0:T(8,128)(2,1)}), bf16[16,32,128]{2,1,0:T(8,128)(2,1)S(1)}, u32[]{:S(2)}, u32[]{:S(2)}) async-start(bf16[16,32,128]{2,1,0:T(8,128)(2,1)} %bitcast.12), calls=%async_computation | async-start | bytes 262144 | tf_op jit(solution)/shard_map/all_to_all | solution.py:452
  42.6 22.9 %collective-permute-start.10 = (bf16[3072,128]{1,0:T(8,128)(2,1)S(1)}, bf16[3072,128]{1,0:T(8,128)(2,1)S(1)}, u32[]{:S(2)}, u32[]{:S(2)}) collective-permute-start(bf16[3072,128]{1,0:T(8,128)(2,1)S(1)} %select_select_fusion.1), channel_id=1, source_target_pairs={{0,3},{1,0},{2,1},{3,2},{4,7},{5,4},{6,5},{7,6},{8,11},{9,8},{10,9... | collective-permute-start | bytes 2359304 | tf_op jit(solution)/shard_map/ppermute | solution.py:456
  43.5 22.0 %collective-permute-start.9 = (bf16[3072,128]{1,0:T(8,128)(2,1)S(1)}, bf16[3072,128]{1,0:T(8,128)(2,1)S(1)}, u32[]{:S(2)}, u32[]{:S(2)}) collective-permute-start(bf16[3072,128]{1,0:T(8,128)(2,1)S(1)} %select_select_fusion.1), channel_id=1, source_target_pairs={{0,2},{1,3},{2,0},{3,1},{4,6},{5,7},{6,4},{7,5},{8,10},{9,11},{10,... | collective-permute-start | bytes 2359304 | tf_op jit(solution)/shard_map/ppermute | solution.py:456
  44.6 21.0 %collective-permute-start.8 = (bf16[3072,128]{1,0:T(8,128)(2,1)S(1)}, bf16[3072,128]{1,0:T(8,128)(2,1)}, u32[]{:S(2)}, u32[]{:S(2)}) collective-permute-start(bf16[3072,128]{1,0:T(8,128)(2,1)S(1)} %select_select_fusion.1), channel_id=1, source_target_pairs={{0,1},{1,2},{2,3},{3,0},{4,5},{5,6},{6,7},{7,4},{8,9},{9,10},{10,1... | collective-permute-start | bytes 2359304 | tf_op jit(solution)/shard_map/ppermute | solution.py:456
  44.6 4.0 %collective-permute-start.11 = (bf16[32,128]{1,0:T(8,128)(2,1)S(1)}, bf16[32,128]{1,0:T(8,128)(2,1)S(1)}, u32[]{:S(2)}, u32[]{:S(2)}) collective-permute-start(bf16[32,128]{1,0:T(8,128)(2,1)S(1)} %constant_dynamic-slice_fusion), channel_id=1, source_target_pairs={{0,16},{16,0},{32,48},{48,32},{64,80},{80,64},{96,112},{112,96},{1... | collective-permute-start | bytes 24584 | tf_op jit(solution)/shard_map/ppermute | solution.py:406
  48.6 5.5 %collective-permute-start.12 = (bf16[64,128]{1,0:T(8,128)(2,1)S(1)}, bf16[64,128]{1,0:T(8,128)(2,1)S(1)}, u32[]{:S(2)}, u32[]{:S(2)}) collective-permute-start(bf16[64,128]{1,0:T(8,128)(2,1)S(1)} %maximum_select_fusion.2.refs_0_), channel_id=1, source_target_pairs={{0,32},{16,112},{32,64},{48,16},{64,96},{80,48},{96,0},{112,80},{1... | collective-permute-start | bytes 49160 | tf_op jit(solution)/shard_map/ppermute | solution.py:412
  49.7 4.3 %collective-permute-start.13 = (bf16[32,128]{1,0:T(8,128)(2,1)S(1)}, bf16[32,128]{1,0:T(8,128)(2,1)S(1)}, u32[]{:S(2)}, u32[]{:S(2)}) collective-permute-start(bf16[32,128]{1,0:T(8,128)(2,1)S(1)} %constant_dynamic-slice_fusion), channel_id=1, source_target_pairs={{0,64},{16,80},{32,96},{48,112},{64,0},{80,16},{96,32},{112,48},{1... | collective-permute-start | bytes 24584 | tf_op jit(solution)/shard_map/ppermute | solution.py:413
  54.0 1.2 %collective-permute-start.14 = (bf16[96,128]{1,0:T(8,128)(2,1)S(1)}, bf16[96,128]{1,0:T(8,128)(2,1)S(1)}, u32[]{:S(2)}, u32[]{:S(2)}) collective-permute-start(bf16[96,128]{1,0:T(8,128)(2,1)S(1)} %pad_maximum_fusion.1), channel_id=1, source_target_pairs={{0,16},{16,0},{32,48},{48,32},{64,80},{80,64},{96,112},{112,96},{1... | collective-permute-start | bytes 73736 | tf_op jit(solution)/shard_map/ppermute | solution.py:415
  66.6 5.3 %collective-permute-start.18 = (bf16[3072,128]{1,0:T(8,128)(2,1)S(1)}, bf16[3072,128]{1,0:T(8,128)(2,1)}, u32[]{:S(2)}, u32[]{:S(2)}) collective-permute-start(bf16[3072,128]{1,0:T(8,128)(2,1)S(1)} %select_select_fusion.refs_0_), channel_id=1, source_target_pairs={{0,16},{16,0},{32,48},{48,32},{64,80},{80,64},{96,112},{112,96},{1... | collective-permute-start | bytes 2359304 | tf_op jit(solution)/shard_map/ppermute | solution.py:470
  68.4 19.8 %collective-permute-start.17 = (bf16[3072,128]{1,0:T(8,128)(2,1)S(1)}, bf16[3072,128]{1,0:T(8,128)(2,1)S(1)}, u32[]{:S(2)}, u32[]{:S(2)}) collective-permute-start(bf16[3072,128]{1,0:T(8,128)(2,1)S(1)} %select_select_fusion.refs_0_), channel_id=1, source_target_pairs={{0,12},{1,13},{2,14},{3,15},{4,0},{5,1},{6,2},{7,3},{8,4},{9,5},{1... | collective-permute-start | bytes 2359304 | tf_op jit(solution)/shard_map/ppermute | solution.py:464
  70.9 17.4 %collective-permute-start.16 = (bf16[3072,128]{1,0:T(8,128)(2,1)S(1)}, bf16[3072,128]{1,0:T(8,128)(2,1)S(1)}, u32[]{:S(2)}, u32[]{:S(2)}) collective-permute-start(bf16[3072,128]{1,0:T(8,128)(2,1)S(1)} %select_select_fusion.refs_0_), channel_id=1, source_target_pairs={{0,8},{1,9},{2,10},{3,11},{4,12},{5,13},{6,14},{7,15},{8,0},{9,1},... | collective-permute-start | bytes 2359304 | tf_op jit(solution)/shard_map/ppermute | solution.py:464
  71.7 20.3 %collective-permute-start.15 = (bf16[3072,128]{1,0:T(8,128)(2,1)S(1)}, bf16[3072,128]{1,0:T(8,128)(2,1)S(1)}, u32[]{:S(2)}, u32[]{:S(2)}) collective-permute-start(bf16[3072,128]{1,0:T(8,128)(2,1)S(1)} %select_select_fusion.refs_0_), channel_id=1, source_target_pairs={{0,4},{1,5},{2,6},{3,7},{4,8},{5,9},{6,10},{7,11},{8,12},{9,13},{1... | collective-permute-start | bytes 2359304 | tf_op jit(solution)/shard_map/ppermute | solution.py:464
  92.0 5.0 %collective-permute-start.19 = (bf16[3072,128]{1,0:T(8,128)(2,1)S(1)}, bf16[3072,128]{1,0:T(8,128)(2,1)S(1)}, u32[]{:S(2)}, u32[]{:S(2)}) collective-permute-start(bf16[3072,128]{1,0:T(8,128)(2,1)S(1)} %collective-permute-done.15.refs_0_), channel_id=1, source_target_pairs={{0,16},{16,0},{32,48},{48,32},{64,80},{80,64},{96,112},{112,96},{1... | collective-permute-start | bytes 2359304 | tf_op jit(solution)/shard_map/ppermute | solution.py:470
  92.6 4.4 %collective-permute-start.20 = (bf16[3072,128]{1,0:T(8,128)(2,1)S(1)}, bf16[3072,128]{1,0:T(8,128)(2,1)}, u32[]{:S(2)}, u32[]{:S(2)}) collective-permute-start(bf16[3072,128]{1,0:T(8,128)(2,1)S(1)} %collective-permute-done.17.refs_1_), channel_id=1, source_target_pairs={{0,16},{16,0},{32,48},{48,32},{64,80},{80,64},{96,112},{112,96},{1... | collective-permute-start | bytes 2359304 | tf_op jit(solution)/shard_map/ppermute | solution.py:470
  92.6 4.4 %collective-permute-start.21 = (bf16[3072,128]{1,0:T(8,128)(2,1)S(1)}, bf16[3072,128]{1,0:T(8,128)(2,1)}, u32[]{:S(2)}, u32[]{:S(2)}) collective-permute-start(bf16[3072,128]{1,0:T(8,128)(2,1)S(1)} %collective-permute-done.16.refs_2_), channel_id=1, source_target_pairs={{0,16},{16,0},{32,48},{48,32},{64,80},{80,64},{96,112},{112,96},{1... | collective-permute-start | bytes 2359304 | tf_op jit(solution)/shard_map/ppermute | solution.py:470
  (3 other events, 2.7 us)

commit v3 on v2

--- a/solution.py
+++ b/solution.py
@@ -7,7 +7,8 @@
 
 NB = 128
 LOOK = 16
-VMEM_LIMIT = 48 * 1024 * 1024
+ORDER = ((1, 3, 2), (2, 3, 1), (2, 3, 1), (2, 3, 1))
+VMEM_LIMIT = 44 * 1024 * 1024
 F32 = jnp.float32
 BF16 = jnp.bfloat16
 HI = lax.Precision.HIGHEST
@@ -15,9 +16,8 @@
 HBM = pl.BlockSpec(memory_space=pltpu.HBM)
 SMEM = pl.BlockSpec(memory_space=pltpu.SMEM)
 VMEM = pl.BlockSpec(memory_space=pltpu.VMEM)
-SHARE = 16
+SHARE = 64
 PART = 1536
-SHIFTS = (1, 3, 2)
 BOTH = ("prow", "pcol")
 
 
@@ -85,74 +85,53 @@
 
 def pair_up(window, half, first, partners):
     def body(place_ref, window_ref, partners_ref, *refs):
-        outs, buffer, sem = refs[:4], refs[4], refs[5]
+        outs, buffer, paired, sem = refs[:4], refs[4], refs[5], refs[6]
         copies = read_half(place_ref, window_ref, buffer, sem)
         for copy in copies:
             copy.start()
-        for n in range(4):
-            outs[n][PART:, :] = partners_ref[n * PART : (n + 1) * PART, :]
+        writes = [pltpu.make_async_copy(paired.at[n], outs[n], sem.at[4 + n]) for n in range(4)]
+        for n in (1, 3, 2, 0):
+            paired[n, PART:, :] = partners_ref[n * PART : (n + 1) * PART, :]
         for n in range(4):
             copies[n].wait()
-            outs[n][:PART, :] = buffer[n].astype(BF16)
+            paired[n, :PART, :] = buffer[n].astype(BF16)
+            writes[n].start()
+        for write in writes:
+            write.wait()
 
     return pl.pallas_call(
         body,
         in_specs=[SMEM, HBM, VMEM],
-        out_specs=[VMEM] * 4,
+        out_specs=[ANY] * 4,
         out_shape=[jax.ShapeDtypeStruct((2 * PART, NB), BF16)] * 4,
-        scratch_shapes=[pltpu.VMEM((4, PART, NB), F32), pltpu.SemaphoreType.DMA((4,))],
+        scratch_shapes=[
+            pltpu.VMEM((4, PART, NB), F32),
+            pltpu.VMEM((4, 2 * PART, NB), BF16),
+            pltpu.SemaphoreType.DMA((8,)),
+        ],
         compiler_params=params(),
         cost_estimate=cost(2.5),
         name="pair_up",
     )(jnp.stack([half, first]).astype(jnp.int32), window, partners)
 
 
-def cut_shares(places, tiles):
-    def body(places_ref, *refs):
-        out_ref, stack = refs[4], refs[5]
-        for n in range(4):
-            stack[n * 6 * NB : (n + 1) * 6 * NB, :] = refs[n][...]
-
-        def share(n):
-            row = places_ref[n] * NB + places_ref[LOOK + 1] * SHARE
-            return stack[pl.ds(pl.multiple_of(row, SHARE), SHARE), :]
-
-        for n in range(LOOK):
-            out_ref[2 * n * SHARE : (2 * n + 1) * SHARE, :] = share(0)
-            out_ref[(2 * n + 1) * SHARE : (2 * n + 2) * SHARE, :] = share(n + 1)
-
-    return pl.pallas_call(
-        body,
-        in_specs=[SMEM] + [VMEM] * 4,
-        out_specs=VMEM,
-        out_shape=jax.ShapeDtypeStruct((2 * LOOK * SHARE, NB), BF16),
-        scratch_shapes=[pltpu.VMEM((24 * NB, NB), BF16)],
-        compiler_params=params(),
-        cost_estimate=cost(1.0),
-        name="cut_shares",
-    )(places, *tiles)
-
-
-def pick(choice, arrays):
+def pick(choice, arrays, order):
+    choice = jnp.where(choice == 0, 0, sum(jnp.where(choice == s, n + 1, 0) for n, s in enumerate(order)))
     return jnp.where(
         choice < 2, jnp.where(choice == 0, arrays[0], arrays[1]), jnp.where(choice == 2, arrays[2], arrays[3])
     )
 
 
-def factor(places, shares):
+def factor(places, tiles):
     block_rows = 16
 
     def body(places_ref, *refs):
-        low_ref, inv_ref, weights_ref, work, stack = refs[4:]
+        low_ref, inv_ref, weights_ref, work, stack, rows = refs[4:]
         for n in range(4):
-            stack[n * 4 * SHARE : (n + 1) * 4 * SHARE, :] = refs[n][...]
+            stack[n * 6 * NB : (n + 1) * 6 * NB, :] = refs[n][...]
 
         def tile_at(n):
-            shares = []
-            for p in range(8):
-                row = lax.rem(places_ref[0] - p // 2 + 4, 4) * 4 * SHARE + (p % 2 * 2 + n) * SHARE
-                shares.append(stack[pl.ds(pl.multiple_of(row, SHARE), SHARE), :])
-            return jnp.concatenate(shares, 0)
+            return stack[pl.ds(pl.multiple_of(places_ref[n] * NB, NB), NB), :]
 
         t = tile_at(0).astype(F32)
         row = lax.broadcasted_iota(jnp.int32, (NB, NB), 0)
@@ -197,9 +176,15 @@
         low_ref[...] = jnp.where(row >= col, up.T, 0.0)
         inv = jnp.where(row >= col, jnp.concatenate(inverse, 0), 0.0)
         inv_ref[...] = inv
-        tile = tile_at(1).astype(F32)
-        half = lax.dot_general(inv, tile, (((1,), (1,)), ((), ())), precision=HI, preferred_element_type=F32)
-        full = lax.dot_general(inv, half, (((0,), (0,)), ((), ())), precision=HI, preferred_element_type=F32)
+        both = lax.dot_general(inv, inv, (((0,), (0,)), ((), ())), precision=HI, preferred_element_type=F32)
+        high = both.astype(BF16)
+        rest = (both - high.astype(F32)).astype(BF16)
+        for n in range(1, LOOK + 1):
+            row = places_ref[n] * NB + places_ref[2 * LOOK + 1] * SHARE
+            place = pl.multiple_of(places_ref[LOOK + n] * SHARE, SHARE)
+            rows[pl.ds(place, SHARE), :] = stack[pl.ds(pl.multiple_of(row, SHARE), SHARE), :]
+        full = lax.dot_general(rows[...], high, (((1,), (0,)), ((), ())), preferred_element_type=F32)
+        full += lax.dot_general(rows[...], rest, (((1,), (0,)), ((), ())), preferred_element_type=F32)
         weights_ref[...] = full.astype(BF16)
 
     return pl.pallas_call(
@@ -209,13 +194,13 @@
         out_shape=[
             jax.ShapeDtypeStruct((NB, NB), F32),
             jax.ShapeDtypeStruct((NB, NB), F32),
-            jax.ShapeDtypeStruct((NB, NB), BF16),
+            jax.ShapeDtypeStruct((LOOK * SHARE, NB), BF16),
         ],
-        scratch_shapes=[pltpu.VMEM((NB, 2 * NB), F32), pltpu.VMEM((16 * SHARE, NB), BF16)],
+        scratch_shapes=[pltpu.VMEM((NB, 2 * NB), F32), pltpu.VMEM((24 * NB, NB), BF16), pltpu.VMEM((LOOK * SHARE, NB), BF16)],
         compiler_params=params(),
         cost_estimate=cost(10.0),
         name="factor",
-    )(places, *shares)
+    )(places, *tiles)
 
 
 def column_copies(source, buffer, target, lane, sem, count):
@@ -306,42 +291,13 @@
     )(scalars, window, low, inv, out)
 
 
-def hold(scalars, window, places):
-    n = len(places)
-
-    def body(s_ref, window_ref, out_ref, sem):
-        lanes = pl.ds(pl.multiple_of(s_ref[3] * NB, NB), NB)
-        copies = [
-            pltpu.make_async_copy(
-                window_ref.at[pl.ds(pl.multiple_of(s_ref[5 + m] * PART, PART), PART), lanes], out_ref.at[m], sem.at[m]
-            )
-            for m in range(n)
-        ]
-        for copy in copies:
-            copy.start()
-        for copy in copies:
-            copy.wait()
-
-    return pl.pallas_call(
-        body,
-        in_specs=[SMEM, HBM],
-        out_specs=VMEM,
-        out_shape=jax.ShapeDtypeStruct((n, PART, NB), F32),
-        scratch_shapes=[pltpu.SemaphoreType.DMA((n,))],
-        compiler_params=params(),
-        cost_estimate=cost(1.5),
-        name="hold",
-    )(jnp.concatenate([scalars, jnp.stack(places).astype(jnp.int32)]), window)
-
-
-def update(scalars, window, weights, parts, places, out, held=None):
+def update(scalars, window, weights, parts, places, out):
     n = len(parts)
     size = PART // 2
     blocks = [(m, i) for m in range(n) for i in range(2)]
     s_all = jnp.concatenate([scalars, jnp.stack(places).astype(jnp.int32)])
-    source = window if held is None else held[0]
-
-    def body(s_ref, source_ref, weight_ref, *refs):
+
+    def body(s_ref, window_ref, weight_ref, *refs):
         panels, out_ref = refs[:n], refs[n + 1]
         buffer, sem = refs[n + 2 :]
         p, j = s_ref[1], s_ref[4]
@@ -351,32 +307,26 @@
             return pl.ds(pl.multiple_of(s_ref[5 + m] * PART + i * size, size), size)
 
         def read(m, i):
-            return pltpu.make_async_copy(source_ref.at[rows(m, i), lanes], buffer.at[m, i], sem.at[0, m, i])
+            return pltpu.make_async_copy(window_ref.at[rows(m, i), lanes], buffer.at[m, i], sem.at[0, m, i])
 
         def write(m, i):
             return pltpu.make_async_copy(buffer.at[m, i], out_ref.at[rows(m, i), lanes], sem.at[1, m, i])
 
-        if held is None:
-            for m, i in blocks:
-                read(m, i).start()
         for m, i in blocks:
-            first = parts[m][1] * PART + i * size
-            if held is None:
-                read(m, i).wait()
+            read(m, i).start()
+        for m, i in blocks:
+            read(m, i).wait()
             for t in range(size // 256):
                 change = lax.dot_general(
-                    panels[m][first + t * 256 : first + (t + 1) * 256, :],
+                    panels[m][i * size + t * 256 : i * size + (t + 1) * 256, :],
                     weight_ref[...],
-                    (((1,), (0,)), ((), ())),
+                    (((1,), (1,)), ((), ())),
                     preferred_element_type=F32,
                 )
                 for u in range(2):
                     at = t * 256 + u * NB
                     tile = (s_ref[5 + m] * (PART // NB) + (i * size + at) // NB) * 8 + p
-                    if held is None:
-                        old = buffer[m, i, at : at + NB, :]
-                    else:
-                        old = source_ref[held[1] + m, i * size + at : i * size + at + NB, :]
+                    old = buffer[m, i, at : at + NB, :]
                     buffer[m, i, at : at + NB, :] = old - jnp.where(tile >= j, change[u * NB : (u + 1) * NB, :], 0.0)
             write(m, i).start()
         for m, i in blocks:
@@ -384,7 +334,7 @@
 
     return pl.pallas_call(
         body,
-        in_specs=[SMEM, HBM if held is None else VMEM, VMEM] + [VMEM] * n + [HBM],
+        in_specs=[SMEM, HBM, VMEM] + [VMEM] * n + [HBM],
         out_specs=HBM,
         out_shape=jax.ShapeDtypeStruct(window.shape, F32),
         scratch_shapes=[
@@ -395,27 +345,30 @@
         compiler_params=params(),
         cost_estimate=cost(1.0 + 0.8 * n),
         name="update",
-    )(s_all, source, weights, *[part[0] for part in parts], out)
+    )(s_all, window, weights, *parts, out)
 
 
 def turn(s):
     return [(n * 2 + c, (n + (s if c == 0 else -s)) % 4 * 2 + c) for n in range(4) for c in range(2)]
 
 
-def pair_of(block, c):
-    partner = lax.ppermute(block, "prow", core_swap())
+def stage(arrays, axis, order):
+    return [arrays[0]] + [lax.ppermute(arrays[s], BOTH, split_shift(s, axis)) for s in order]
+
+
+def side_by_side(block, partner, c):
     return jnp.where(c == 0, jnp.concatenate([block, partner]), jnp.concatenate([partner, block]))
 
 
-def over_rows(block, pair, c):
-    n = block.shape[0]
-    beside = lax.ppermute(pair, "prow", turn(1))
-    across = lax.ppermute(block, "prow", x_shift(2))
-    got = jnp.concatenate([beside, across])
+def send_rows(block, pair):
+    return jnp.concatenate([lax.ppermute(pair, "prow", turn(1)), lax.ppermute(block, "prow", x_shift(2))])
+
+
+def over_rows(pair, got, c):
+    n = pair.shape[0] // 2
     other = lax.ppermute(got, "prow", core_swap())
-    far = jnp.where(
-        c == 0, jnp.concatenate([across, other[2 * n :]]), jnp.concatenate([other[2 * n :], across])
-    )
+    beside, across = got[: 2 * n], got[2 * n :]
+    far = jnp.where(c == 0, jnp.concatenate([across, other[2 * n :]]), jnp.concatenate([other[2 * n :], across]))
     one = jnp.where(c == 0, beside, other[: 2 * n])
     three = jnp.where(c == 0, other[: 2 * n], beside)
     return [pair, one, far, three]
@@ -437,48 +390,43 @@
     d_along, d_across = jnp.where(c == 0, dz, dy), jnp.where(c == 0, dy, dz)
     others = lax.ppermute(cast_half(window, 1 - c, across), "prow", core_swap())
     own = lax.dynamic_slice(window, (k // 8 * NB, 0), (3 * NB, NB)).astype(BF16)
-    pair = pair_of(own, c)
-    pair, others = lax.optimization_barrier((pair, others))
+    partner = lax.ppermute(own, "prow", core_swap())
+    partner, others = lax.optimization_barrier((partner, others))
     messages = pair_up(window, c, along, others)
-    messages, own, pair = lax.optimization_barrier((messages, own, pair))
-
-    moved = [messages[0]] + [lax.ppermute(messages[s], BOTH, split_shift(s, 0)) for s in (1, 2, 3)]
-
-    tiles = over_rows(own, pair, c)
-    column = jnp.arange(LOOK)
-    look = jnp.concatenate([jnp.reshape(k, (1,)), column + jnp.where(column <= k, 16, 0)])
+    messages, own, partner, keep_scalars = lax.optimization_barrier((messages, own, partner, scalars))
+
+    moved = stage(messages, 0, ORDER[0])
+    pair = side_by_side(own, partner, c)
+    got = send_rows(own, pair)
+    out = keep_column(keep_scalars, window)
+    moved, got, out = lax.optimization_barrier((moved, got, out))
+    message = pick(d_along, moved, ORDER[0])
+
+    message, got = lax.optimization_barrier((message, got))
+    moved = stage([message] * 4, 1, ORDER[1])
+
+    tiles = over_rows(pair, got, c)
+    look = k + jnp.arange(LOOK + 1)
     at = (x - look % 8 // 2) % 4 * 6 + look % 2 * 3 + look // 8 - k // 8
-    shares = cut_shares(jnp.concatenate([at, jnp.reshape(p, (1,))]).astype(jnp.int32), tiles)
-    shares = lax.all_to_all(shares, "pcol", 0, 0, tiled=True)
-    moved, shares = lax.optimization_barrier((moved, shares))
-    message = pick(d_along, moved)
-
-    moved = [message] + [lax.ppermute(message, BOTH, split_shift(s, 1)) for s in (1, 2, 3)]
-    share = lax.dynamic_slice(shares, (k * 2 * SHARE, 0), (2 * SHARE, NB))
-    low, inv, weights = factor(jnp.reshape(x, (1,)).astype(jnp.int32), over_rows(share, pair_of(share, c), c))
-    out = keep_column(scalars, window)
+    places = jnp.concatenate([at, look[1:] % 16, jnp.reshape(c, (1,))])
+    low, inv, weights = factor(places.astype(jnp.int32), tiles)
+    weights = lax.all_to_all(weights, "pcol", 0, 0, tiled=True)
+    moved, weights = lax.optimization_barrier((moved, weights))
+    message = pick(d_across, moved, ORDER[1])
+
+    message, weights, low = lax.optimization_barrier((message, weights, low))
+    mine = message[:PART]
+    other = lax.ppermute(message[PART:], "prow", core_swap())
+    first = stage([mine] * 4, 0, ORDER[2])
+    second = stage([other] * 4, 1, ORDER[3])
+    places = [4 * c + (along - s) % 4 for s in (0,) + ORDER[2]] + [4 * (1 - c) + (across - s) % 4 for s in (0,) + ORDER[3]]
+
+    weights = lax.dynamic_slice(weights, (k * SHARE, 0), (SHARE, NB))
+    weights = side_by_side(weights, lax.ppermute(weights, "prow", core_swap()), c)
     out = write_panel(scalars, window, low, inv, out)
-    moved, out, weights = lax.optimization_barrier((moved, out, weights))
-    message = pick(d_across, moved)
-
-    gathered = [message] + [lax.ppermute(message, BOTH, split_shift(s, 0)) for s in (1, 2, 3)]
-
-    def places_of(s):
-        return [4 * c + (along - s) % 4, 4 * (1 - c) + (across - s) % 4]
-
-    def swapped(block):
-        return lax.ppermute(block, "prow", core_swap())
-
-    out = update(scalars, window, weights, [(gathered[0], 0), (swapped(gathered[0]), 1)], places_of(0), out)
-    gathered, out = lax.optimization_barrier((gathered, out))
-    others = [swapped(gathered[s]) for s in SHIFTS]
-    out = update(
-        scalars, window, weights, [(gathered[s], 0) for s in SHIFTS], [places_of(s)[0] for s in SHIFTS], out
-    )
-    others, out = lax.optimization_barrier((others, out))
-    return update(
-        scalars, window, weights, [(other, 1) for other in others], [places_of(s)[1] for s in SHIFTS], out
-    )
+    out = update(scalars, window, weights, [mine, other], places[::4], out)
+    first, second, out = lax.optimization_barrier((first, second, out))
+    return update(scalars, window, weights, first[1:] + second[1:], places[1:4] + places[5:], out)
 
 
 def solution(mesh):

time: 103 us -> 92.7 us (0.900)
  waiting for transfers between devices: 31.8 us -> 28.4 us
  local copies, waits for them, and re-layouts: 3.99 us -> 1.92 us
  Pallas kernels: 29.1 us -> 27.2 us
  starting transfers between devices: 31.8 us -> 29.9 us
    pallas_call x1, Pallas kernels: 0.63 us -> 5.7 us  [keep_column(): pl.pallas_call(body, in_specs=[SMEM, HBM], out_specs=HBM, out_shape=jax.S...]
    pallas_call x1, Pallas kernels: 5.15 us -> 0.63 us  [write_panel(): pl.pallas_call(body, in_specs=[SMEM, HBM, VMEM, VMEM, HBM], out_specs=HBM...]
    ppermute x19 -> x17, waiting for transfers between devices: 23.8 us -> 19.3 us  [the longest x12 18 us: stage(): lax.ppermute(arrays[s], BOTH, split_shift(s, axis))]
    pallas_call x5 -> x3, Pallas kernels: 15.8 us -> 11.9 us  [the longest x2 8.51 us: update(): pl.pallas_call(body, in_specs=[SMEM, HBM, VMEM] + [VMEM] * n + [HBM], out...]
    all_to_all x1, waiting for transfers between devices: 6.76 us -> 9.14 us  [body(): weights = lax.all_to_all(weights, 'pcol', 0, 0, tiled=True)]
    unnamed x8, local copies, waits for them, and re-layouts: 2.7 us -> 0.65 us
    ppermute x19 -> x17, starting transfers between devices: 21 us -> 19.4 us  [the longest x12 15.9 us: stage(): lax.ppermute(arrays[s], BOTH, split_shift(s, axis))]
    pallas_call x1, Pallas kernels: 5.09 us -> 6.52 us  [factor(): pl.pallas_call(body, in_specs=[SMEM] + [VMEM] * 4, out_specs=[VMEM] * 3,...]
  transfers between devices with their start and end apart: 23 -> 20, of which waited for: 9 -> 7; matrix products, arithmetic and copies ran while one was open for 4% -> 2% of each run, Pallas kernels for 19% -> 18%
where the time goes in v3:
time: 92.7 us; the launch traced here: 91.7 us
  starting transfers between devices  29.9 us (32%)
  waiting for transfers between devices  28.4 us (31%)
  Pallas kernels  27.2 us (29%)
  other arithmetic  3.3 us (4%)
  local copies, waits for them, and re-layouts  1.92 us (2%)
    ppermute x12, waiting for transfers between devices, stage(): lax.ppermute(arrays[s], BOTH, split_shift(s, axis))  18 us
    ppermute x12, starting transfers between devices, stage(): lax.ppermute(arrays[s], BOTH, split_shift(s, axis))  15.9 us
    all_to_all x1, waiting for transfers between devices, body(): weights = lax.all_to_all(weights, 'pcol', 0, 0, tiled=True)  9.14 us
    pallas_call x2, Pallas kernels, update(): pl.pallas_call(body, in_specs=[SMEM, HBM, VMEM] + [VMEM] * n + [HBM], out...  8.51 us
    all_to_all x1, starting transfers between devices, body(): weights = lax.all_to_all(weights, 'pcol', 0, 0, tiled=True)  6.64 us
    pallas_call x1, Pallas kernels, factor(): pl.pallas_call(body, in_specs=[SMEM] + [VMEM] * 4, out_specs=[VMEM] * 3,...  6.52 us
    pallas_call x1, Pallas kernels, keep_column(): pl.pallas_call(body, in_specs=[SMEM, HBM], out_specs=HBM, out_shape=jax.S...  5.7 us
    pallas_call x1, Pallas kernels, pair_up(): pl.pallas_call(body, in_specs=[SMEM, HBM, VMEM], out_specs=[ANY] * 4, out...  3.43 us
  transfers between devices with their start and end apart: 20, of which 7 were waited for; matrix products, arithmetic and copies ran while one was open for 2% of the time, Pallas kernels for 18%

profile of v3, /device:TPU:1, one launch (start us, length us, event | category | flops | bytes accessed | tf_op | source)
XLA Modules:
  0.0 91.7 jit_solution(6061907225125898232)
XLA Ops:
  0.1 2.5 %cast_half.1 = bf16[6144,128]{1,0:T(8,128)(2,1)S(1)} custom-call(s32[2]{0:T(128)S(1)} %pad_add_fusion.1.place_ref, f32[12288,256]{1,0:T(8,128)} %window_ref.11), custom_call_target="tpu_custom_call" | custom-call | bytes 7000000 | tf_op jit(solution)/shard_map/cast_half/pallas_call | solution.py:74
  2.6 1.5 %collective-permute-start.1 = (bf16[6144,128]{1,0:T(8,128)(2,1)S(1)}, bf16[6144,128]{1,0:T(8,128)(2,1)S(1)}, u32[]{:S(2)}, u32[]{:S(2)}) collective-permute-start(bf16[6144,128]{1,0:T(8,128)(2,1)S(1)} %cast_half.1), channel_id=1, source_target_pairs={{0,16},{16,0},{32,48},{48,32},{64,80},{80,64},{96,112},{112,96},{1... | collective-permute-start | bytes 4718600 | tf_op jit(solution)/shard_map/ppermute | solution.py:391
  7.9 3.4 %pair_up.1 = (bf16[3072,128]{1,0:T(8,128)(2,1)S(1)}, bf16[3072,128]{1,0:T(8,128)(2,1)}, bf16[3072,128]{1,0:T(8,128)(2,1)S(1)}, bf16[3072,128]{1,0:T(8,128)(2,1)}) custom-call(s32[2]{0:T(128)S(1)} %pad_add_fusion.place_ref, f32[12288,256]{1,0:T(8,128)} %window_ref.11, bf16[6144,128]{1,0:T(8,128)(2,1)S(1)} %collective-permute-done.1.partners_ref), custom_call_target="tpu_custom_call" | custom-call | bytes 8750000 | tf_op jit(solution)/shard_map/pair_up/pallas_call | solution.py:102
  11.3 1.4 %collective-permute-start.2 = (bf16[3072,128]{1,0:T(8,128)(2,1)}, bf16[3072,128]{1,0:T(8,128)(2,1)S(1)}, u32[]{:S(2)}, u32[]{:S(2)}) collective-permute-start(bf16[3072,128]{1,0:T(8,128)(2,1)} %get-tuple-element.51), channel_id=1, source_target_pairs={{0,4},{1,5},{2,6},{3,7},{4,8},{5,9},{6,10},{7,11},{8,12},{9,13},{1... | collective-permute-start | bytes 2359304 | tf_op jit(solution)/shard_map/ppermute | solution.py:356
  12.8 1.5 %collective-permute-start.3 = (bf16[3072,128]{1,0:T(8,128)(2,1)}, bf16[3072,128]{1,0:T(8,128)(2,1)}, u32[]{:S(2)}, u32[]{:S(2)}) collective-permute-start(bf16[3072,128]{1,0:T(8,128)(2,1)} %get-tuple-element.52), channel_id=1, source_target_pairs={{0,12},{1,13},{2,14},{3,15},{4,0},{5,1},{6,2},{7,3},{8,4},{9,5},{1... | collective-permute-start | bytes 2359304 | tf_op jit(solution)/shard_map/ppermute | solution.py:356
  14.3 1.6 %collective-permute-start.4 = (bf16[3072,128]{1,0:T(8,128)(2,1)S(1)}, bf16[3072,128]{1,0:T(8,128)(2,1)}, u32[]{:S(2)}, u32[]{:S(2)}) collective-permute-start(bf16[3072,128]{1,0:T(8,128)(2,1)S(1)} %get-tuple-element.53), channel_id=1, source_target_pairs={{0,8},{1,9},{2,10},{3,11},{4,12},{5,13},{6,14},{7,15},{8,0},{9,1},... | collective-permute-start | bytes 2359304 | tf_op jit(solution)/shard_map/ppermute | solution.py:356
  15.9 2.5 %collective-permute-start.5 = (bf16[768,128]{1,0:T(8,128)(2,1)S(1)}, bf16[768,128]{1,0:T(8,128)(2,1)S(1)}, u32[]{:S(2)}, u32[]{:S(2)}) collective-permute-start(bf16[768,128]{1,0:T(8,128)(2,1)S(1)} %maximum_select_fusion.refs_0_), channel_id=1, source_target_pairs={{0,32},{16,112},{32,64},{48,16},{64,96},{80,48},{96,0},{112,80},{1... | collective-permute-start | bytes 589832 | tf_op jit(solution)/shard_map/ppermute | solution.py:364
  19.0 5.7 %keep_column.1._ = f32[12288,256]{1,0:T(8,128)} custom-call(s32[5]{0:T(128)S(1)} %stack.73.s_ref, f32[12288,256]{1,0:T(8,128)} %window_ref.11), custom_call_target="tpu_custom_call" | custom-call | bytes 19250000 | tf_op jit(solution)/shard_map/keep_column/pallas_call | solution.py:230
  24.8 7.2 %collective-permute-done.3 = bf16[3072,128]{1,0:T(8,128)(2,1)} collective-permute-done((bf16[3072,128]{1,0:T(8,128)(2,1)}, bf16[3072,128]{1,0:T(8,128)(2,1)}, u32[]{:S(2)}, u32[]{:S(2)}) %collective-permute-start.3) | collective-permute-done | bytes 786464 | tf_op jit(solution)/shard_map/ppermute | solution.py:356
  32.0 1.8 %collective-permute-done.4 = bf16[3072,128]{1,0:T(8,128)(2,1)} collective-permute-done((bf16[3072,128]{1,0:T(8,128)(2,1)S(1)}, bf16[3072,128]{1,0:T(8,128)(2,1)}, u32[]{:S(2)}, u32[]{:S(2)}) %collective-permute-start.4) | collective-permute-done | bytes 786464 | tf_op jit(solution)/shard_map/ppermute | solution.py:356
  33.8 1.4 %select_select_fusion.1 = bf16[3072,128]{1,0:T(8,128)(2,1)S(1)} fusion(bf16[3072,128]{1,0:T(8,128)(2,1)} %collective-permute-done.3, bf16[3072,128]{1,0:T(8,128)(2,1)} %collective-permute-done.4, bf16[3072,128]{1,0:T(8,128)(2,1)S(1)} %get-tuple-element.57, bf16[3072,128]{1,0:T(8,128)(2,1)S(1)} %collective-permute-done.2, pred[]{:T(512)S(6)} %eq.82, ...), kind=kLoop, calls=%fused_computation.1 | loop fusion | flops 1179648 | bytes 3932163 | tf_op jit(solution)/shard_map/jit(_where)/select_n | solution.py:120
  35.2 2.3 %collective-permute-start.10 = (bf16[1152,128]{1,0:T(8,128)(2,1)S(1)}, bf16[1152,128]{1,0:T(8,128)(2,1)S(1)}, u32[]{:S(2)}, u32[]{:S(2)}) collective-permute-start(bf16[1152,128]{1,0:T(8,128)(2,1)S(1)} %pad_maximum_fusion), channel_id=1, source_target_pairs={{0,16},{16,0},{32,48},{48,32},{64,80},{80,64},{96,112},{112,96},{1... | collective-permute-start | bytes 884744 | tf_op jit(solution)/shard_map/ppermute | solution.py:369
  38.8 1.5 %collective-permute-start.8 = (bf16[3072,128]{1,0:T(8,128)(2,1)S(1)}, bf16[3072,128]{1,0:T(8,128)(2,1)S(1)}, u32[]{:S(2)}, u32[]{:S(2)}) collective-permute-start(bf16[3072,128]{1,0:T(8,128)(2,1)S(1)} %select_select_fusion.1), channel_id=1, source_target_pairs={{0,3},{1,0},{2,1},{3,2},{4,7},{5,4},{6,5},{7,6},{8,11},{9,8},{10,9... | collective-permute-start | bytes 2359304 | tf_op jit(solution)/shard_map/ppermute | solution.py:356
  40.9 6.5 %factor.1 = (f32[128,128]{1,0:T(8,128)S(1)}, f32[128,128]{1,0:T(8,128)S(1)}, bf16[1024,128]{1,0:T(8,128)(2,1)}) custom-call(s32[34]{0:T(128)S(1)} %pad_add_fusion.2.places_ref, bf16[768,128]{1,0:T(8,128)(2,1)S(1)} %maximum_select_fusion.refs_0_, bf16[768,128]{1,0:T(8,128)(2,1)S(1)} %get-tuple-element.86.refs_1_, ...), custom_call_target="tpu_custom_call" | custom-call | bytes 35000000 | tf_op jit(solution)/shard_map/factor/pallas_call | solution.py:190
  47.4 6.6 %all-to-all-start = ((bf16[16,64,128]{2,1,0:T(8,128)(2,1)}), bf16[16,64,128]{2,1,0:T(8,128)(2,1)S(1)}, u32[]{:S(2)}, u32[]{:S(2)}) async-start(bf16[16,64,128]{2,1,0:T(8,128)(2,1)} %bitcast.15), calls=%async_computation | async-start | bytes 524288 | tf_op jit(solution)/shard_map/all_to_all | solution.py:413
  54.1 9.1 %all-to-all-done = bf16[16,64,128]{2,1,0:T(8,128)(2,1)S(1)} async-done(((bf16[16,64,128]{2,1,0:T(8,128)(2,1)}), bf16[16,64,128]{2,1,0:T(8,128)(2,1)S(1)}, u32[]{:S(2)}, u32[]{:S(2)}) %all-to-all-start) | async-done | bytes 262176 | tf_op jit(solution)/shard_map/all_to_all | solution.py:413
  63.2 1.4 %select_select_fusion = bf16[3072,128]{1,0:T(8,128)(2,1)S(1)} fusion(bf16[3072,128]{1,0:T(8,128)(2,1)S(1)} %collective-permute-done.8, bf16[3072,128]{1,0:T(8,128)(2,1)S(1)} %collective-permute-done.9, bf16[3072,128]{1,0:T(8,128)(2,1)S(1)} %select_select_fusion.1, bf16[3072,128]{1,0:T(8,128)(2,1)} %collective-permute-done.7, pred[]{:T(512)S(6)} %eq.83, ...), kind=kLoop, calls=%fused_computation | loop fusion | flops 1179648 | bytes 3932163 | tf_op jit(solution)/shard_map/jit(_where)/select_n | solution.py:120
  65.0 2.3 %collective-permute-start.14 = (bf16[1536,128]{1,0:T(8,128)(2,1)S(1)}, bf16[1536,128]{1,0:T(8,128)(2,1)S(1)}, u32[]{:S(2)}, u32[]{:S(2)}) collective-permute-start(bf16[1536,128]{1,0:T(8,128)(2,1)S(1)} %get-tuple-element.84.refs_0_), channel_id=1, source_target_pairs={{0,4},{1,5},{2,6},{3,7},{4,8},{5,9},{6,10},{7,11},{8,12},{9,13},{1... | collective-permute-start | bytes 1179656 | tf_op jit(solution)/shard_map/ppermute | solution.py:356
  67.3 1.4 %collective-permute-start.13 = (bf16[1536,128]{1,0:T(8,128)(2,1)S(1)}, bf16[1536,128]{1,0:T(8,128)(2,1)S(1)}, u32[]{:S(2)}, u32[]{:S(2)}) collective-permute-start(bf16[1536,128]{1,0:T(8,128)(2,1)S(1)} %get-tuple-element.84.refs_0_), channel_id=1, source_target_pairs={{0,12},{1,13},{2,14},{3,15},{4,0},{5,1},{6,2},{7,3},{8,4},{9,5},{1... | collective-permute-start | bytes 1179656 | tf_op jit(solution)/shard_map/ppermute | solution.py:356
  70.5 1.7 %collective-permute-start.17 = (bf16[1536,128]{1,0:T(8,128)(2,1)S(1)}, bf16[1536,128]{1,0:T(8,128)(2,1)S(1)}, u32[]{:S(2)}, u32[]{:S(2)}) collective-permute-start(bf16[1536,128]{1,0:T(8,128)(2,1)S(1)} %collective-permute-done.15.refs_1_), channel_id=1, source_target_pairs={{0,3},{1,0},{2,1},{3,2},{4,7},{5,4},{6,5},{7,6},{8,11},{9,8},{10,9... | collective-permute-start | bytes 1179656 | tf_op jit(solution)/shard_map/ppermute | solution.py:356
  75.2 3.3 %update.2.refs_6_ = f32[12288,256]{1,0:T(8,128)} custom-call(s32[7]{0:T(128)S(1)} %concatenate.41.s_ref, f32[12288,256]{1,0:T(8,128)} %window_ref.11, bf16[128,128]{1,0:T(8,128)(2,1)S(1)} %maximum_select_fusion.2.weight_ref, bf16[1536,128]{1,0:T(8,128)(2,1)S(1)} %get-tuple-element.84.refs_0_, ...), custom_call_target="tpu_custom_call", output_to_operand_aliasing={{}: (5, {})} | custom-call | bytes 9100000 | tf_op jit(solution)/shard_map/update/pallas_call | solution.py:335
  78.5 3.7 %collective-permute-done.12.refs_0_ = bf16[1536,128]{1,0:T(8,128)(2,1)S(1)} collective-permute-done((bf16[1536,128]{1,0:T(8,128)(2,1)S(1)}, bf16[1536,128]{1,0:T(8,128)(2,1)S(1)}, u32[]{:S(2)}, u32[]{:S(2)}) %collective-permute-start.12) | collective-permute-done | bytes 393248 | tf_op jit(solution)/shard_map/ppermute | solution.py:356
  82.2 4.3 %collective-permute-done.18.refs_5_ = bf16[1536,128]{1,0:T(8,128)(2,1)S(1)} collective-permute-done((bf16[1536,128]{1,0:T(8,128)(2,1)S(1)}, bf16[1536,128]{1,0:T(8,128)(2,1)S(1)}, u32[]{:S(2)}, u32[]{:S(2)}) %collective-permute-start.18) | collective-permute-done | bytes 393248 | tf_op jit(solution)/shard_map/ppermute | solution.py:356
  86.5 5.2 %update.3 = f32[12288,256]{1,0:T(8,128)} custom-call(s32[11]{0:T(128)S(1)} %concatenate.32.s_ref, f32[12288,256]{1,0:T(8,128)} %window_ref.11, bf16[128,128]{1,0:T(8,128)(2,1)S(1)} %maximum_select_fusion.2.weight_ref, bf16[1536,128]{1,0:T(8,128)(2,1)S(1)} %collective-permute-done.12.refs_0_, ...), custom_call_target="tpu_custom_call", output_to_operand_aliasing={{}: (9, {})} | custom-call | bytes 20300000 | tf_op jit(solution)/shard_map/update/pallas_call | solution.py:335
  (52 shorter events, 10.7 us)
Async XLA Ops:
  2.6 5.3 %collective-permute-start.1 = (bf16[6144,128]{1,0:T(8,128)(2,1)S(1)}, bf16[6144,128]{1,0:T(8,128)(2,1)S(1)}, u32[]{:S(2)}, u32[]{:S(2)}) collective-permute-start(bf16[6144,128]{1,0:T(8,128)(2,1)S(1)} %cast_half.1), channel_id=1, source_target_pairs={{0,16},{16,0},{32,48},{48,32},{64,80},{80,64},{96,112},{112,96},{1... | collective-permute-start | bytes 4718600 | tf_op jit(solution)/shard_map/ppermute | solution.py:391
  5.7 1.6 %copy-start = (bf16[384,128]{1,0:T(8,128)(2,1)}, bf16[384,128]{1,0:T(8,128)(2,1)S(1)}, u32[]{:S(2)}) copy-start(bf16[384,128]{1,0:T(8,128)(2,1)S(1)} %dynamic-slice_convert_fusion) | copy-start | bytes 294916
  5.7 1.5 %collective-permute-start = (bf16[384,128]{1,0:T(8,128)(2,1)S(1)}, bf16[384,128]{1,0:T(8,128)(2,1)S(1)}, u32[]{:S(2)}, u32[]{:S(2)}) collective-permute-start(bf16[384,128]{1,0:T(8,128)(2,1)S(1)} %dynamic-slice_convert_fusion), channel_id=1, source_target_pairs={{0,16},{16,0},{32,48},{48,32},{64,80},{80,64},{96,112},{112,96},{1... | collective-permute-start | bytes 294920 | tf_op jit(solution)/shard_map/ppermute | solution.py:393
  7.2 0.6 copy-start.2
  7.9 8.0 %copy-start.1 = (bf16[384,128]{1,0:T(8,128)(2,1)S(1)}, bf16[384,128]{1,0:T(8,128)(2,1)}, u32[]{:S(2)}) copy-start(bf16[384,128]{1,0:T(8,128)(2,1)} %copy-done) | copy-start | bytes 294916
  7.9 8.0 %copy-start.3 = (bf16[384,128]{1,0:T(8,128)(2,1)S(1)}, bf16[384,128]{1,0:T(8,128)(2,1)}, u32[]{:S(2)}) copy-start(bf16[384,128]{1,0:T(8,128)(2,1)} %copy-done.2) | copy-start | bytes 294916
  11.3 13.4 %collective-permute-start.2 = (bf16[3072,128]{1,0:T(8,128)(2,1)}, bf16[3072,128]{1,0:T(8,128)(2,1)S(1)}, u32[]{:S(2)}, u32[]{:S(2)}) collective-permute-start(bf16[3072,128]{1,0:T(8,128)(2,1)} %get-tuple-element.51), channel_id=1, source_target_pairs={{0,4},{1,5},{2,6},{3,7},{4,8},{5,9},{6,10},{7,11},{8,12},{9,13},{1... | collective-permute-start | bytes 2359304 | tf_op jit(solution)/shard_map/ppermute | solution.py:356
  12.8 19.2 %collective-permute-start.3 = (bf16[3072,128]{1,0:T(8,128)(2,1)}, bf16[3072,128]{1,0:T(8,128)(2,1)}, u32[]{:S(2)}, u32[]{:S(2)}) collective-permute-start(bf16[3072,128]{1,0:T(8,128)(2,1)} %get-tuple-element.52), channel_id=1, source_target_pairs={{0,12},{1,13},{2,14},{3,15},{4,0},{5,1},{6,2},{7,3},{8,4},{9,5},{1... | collective-permute-start | bytes 2359304 | tf_op jit(solution)/shard_map/ppermute | solution.py:356
  14.3 19.5 %collective-permute-start.4 = (bf16[3072,128]{1,0:T(8,128)(2,1)S(1)}, bf16[3072,128]{1,0:T(8,128)(2,1)}, u32[]{:S(2)}, u32[]{:S(2)}) collective-permute-start(bf16[3072,128]{1,0:T(8,128)(2,1)S(1)} %get-tuple-element.53), channel_id=1, source_target_pairs={{0,8},{1,9},{2,10},{3,11},{4,12},{5,13},{6,14},{7,15},{8,0},{9,1},... | collective-permute-start | bytes 2359304 | tf_op jit(solution)/shard_map/ppermute | solution.py:356
  15.9 8.8 %collective-permute-start.5 = (bf16[768,128]{1,0:T(8,128)(2,1)S(1)}, bf16[768,128]{1,0:T(8,128)(2,1)S(1)}, u32[]{:S(2)}, u32[]{:S(2)}) collective-permute-start(bf16[768,128]{1,0:T(8,128)(2,1)S(1)} %maximum_select_fusion.refs_0_), channel_id=1, source_target_pairs={{0,32},{16,112},{32,64},{48,16},{64,96},{80,48},{96,0},{112,80},{1... | collective-permute-start | bytes 589832 | tf_op jit(solution)/shard_map/ppermute | solution.py:364
  18.5 6.2 %collective-permute-start.6 = (bf16[384,128]{1,0:T(8,128)(2,1)S(1)}, bf16[384,128]{1,0:T(8,128)(2,1)S(1)}, u32[]{:S(2)}, u32[]{:S(2)}) collective-permute-start(bf16[384,128]{1,0:T(8,128)(2,1)S(1)} %copy-done.1), channel_id=1, source_target_pairs={{0,64},{16,80},{32,96},{48,112},{64,0},{80,16},{96,32},{112,48},{1... | collective-permute-start | bytes 294920 | tf_op jit(solution)/shard_map/ppermute | solution.py:364
  35.2 5.6 %collective-permute-start.10 = (bf16[1152,128]{1,0:T(8,128)(2,1)S(1)}, bf16[1152,128]{1,0:T(8,128)(2,1)S(1)}, u32[]{:S(2)}, u32[]{:S(2)}) collective-permute-start(bf16[1152,128]{1,0:T(8,128)(2,1)S(1)} %pad_maximum_fusion), channel_id=1, source_target_pairs={{0,16},{16,0},{32,48},{48,32},{64,80},{80,64},{96,112},{112,96},{1... | collective-permute-start | bytes 884744 | tf_op jit(solution)/shard_map/ppermute | solution.py:369
  37.6 25.6 %collective-permute-start.9 = (bf16[3072,128]{1,0:T(8,128)(2,1)S(1)}, bf16[3072,128]{1,0:T(8,128)(2,1)S(1)}, u32[]{:S(2)}, u32[]{:S(2)}) collective-permute-start(bf16[3072,128]{1,0:T(8,128)(2,1)S(1)} %select_select_fusion.1), channel_id=1, source_target_pairs={{0,1},{1,2},{2,3},{3,0},{4,5},{5,6},{6,7},{7,4},{8,9},{9,10},{10,1... | collective-permute-start | bytes 2359304 | tf_op jit(solution)/shard_map/ppermute | solution.py:356
  38.8 24.5 %collective-permute-start.8 = (bf16[3072,128]{1,0:T(8,128)(2,1)S(1)}, bf16[3072,128]{1,0:T(8,128)(2,1)S(1)}, u32[]{:S(2)}, u32[]{:S(2)}) collective-permute-start(bf16[3072,128]{1,0:T(8,128)(2,1)S(1)} %select_select_fusion.1), channel_id=1, source_target_pairs={{0,3},{1,0},{2,1},{3,2},{4,7},{5,4},{6,5},{7,6},{8,11},{9,8},{10,9... | collective-permute-start | bytes 2359304 | tf_op jit(solution)/shard_map/ppermute | solution.py:356
  40.3 22.9 %collective-permute-start.7 = (bf16[3072,128]{1,0:T(8,128)(2,1)S(1)}, bf16[3072,128]{1,0:T(8,128)(2,1)}, u32[]{:S(2)}, u32[]{:S(2)}) collective-permute-start(bf16[3072,128]{1,0:T(8,128)(2,1)S(1)} %select_select_fusion.1), channel_id=1, source_target_pairs={{0,2},{1,3},{2,0},{3,1},{4,6},{5,7},{6,4},{7,5},{8,10},{9,11},{10,... | collective-permute-start | bytes 2359304 | tf_op jit(solution)/shard_map/ppermute | solution.py:356
  47.4 15.8 %all-to-all-start = ((bf16[16,64,128]{2,1,0:T(8,128)(2,1)}), bf16[16,64,128]{2,1,0:T(8,128)(2,1)S(1)}, u32[]{:S(2)}, u32[]{:S(2)}) async-start(bf16[16,64,128]{2,1,0:T(8,128)(2,1)} %bitcast.15), calls=%async_computation | async-start | bytes 524288 | tf_op jit(solution)/shard_map/all_to_all | solution.py:413
  64.7 4.7 %collective-permute-start.15 = (bf16[1536,128]{1,0:T(8,128)(2,1)S(1)}, bf16[1536,128]{1,0:T(8,128)(2,1)S(1)}, u32[]{:S(2)}, u32[]{:S(2)}) collective-permute-start(bf16[1536,128]{1,0:T(8,128)(2,1)S(1)} %get-tuple-element.83), channel_id=1, source_target_pairs={{0,16},{16,0},{32,48},{48,32},{64,80},{80,64},{96,112},{112,96},{1... | collective-permute-start | bytes 1179656 | tf_op jit(solution)/shard_map/ppermute | solution.py:419
  65.0 8.1 %collective-permute-start.14 = (bf16[1536,128]{1,0:T(8,128)(2,1)S(1)}, bf16[1536,128]{1,0:T(8,128)(2,1)S(1)}, u32[]{:S(2)}, u32[]{:S(2)}) collective-permute-start(bf16[1536,128]{1,0:T(8,128)(2,1)S(1)} %get-tuple-element.84.refs_0_), channel_id=1, source_target_pairs={{0,4},{1,5},{2,6},{3,7},{4,8},{5,9},{6,10},{7,11},{8,12},{9,13},{1... | collective-permute-start | bytes 1179656 | tf_op jit(solution)/shard_map/ppermute | solution.py:356
  67.3 3.2 %collective-permute-start.11 = (bf16[64,128]{1,0:T(8,128)(2,1)S(1)}, bf16[64,128]{1,0:T(8,128)(2,1)S(1)}, u32[]{:S(2)}, u32[]{:S(2)}) collective-permute-start(bf16[64,128]{1,0:T(8,128)(2,1)S(1)} %constant_dynamic-slice_fusion), channel_id=1, source_target_pairs={{0,16},{16,0},{32,48},{48,32},{64,80},{80,64},{96,112},{112,96},{1... | collective-permute-start | bytes 49160 | tf_op jit(solution)/shard_map/ppermute | solution.py:425
  67.3 11.1 %collective-permute-start.13 = (bf16[1536,128]{1,0:T(8,128)(2,1)S(1)}, bf16[1536,128]{1,0:T(8,128)(2,1)S(1)}, u32[]{:S(2)}, u32[]{:S(2)}) collective-permute-start(bf16[1536,128]{1,0:T(8,128)(2,1)S(1)} %get-tuple-element.84.refs_0_), channel_id=1, source_target_pairs={{0,12},{1,13},{2,14},{3,15},{4,0},{5,1},{6,2},{7,3},{8,4},{9,5},{1... | collective-permute-start | bytes 1179656 | tf_op jit(solution)/shard_map/ppermute | solution.py:356
  68.7 13.5 %collective-permute-start.12 = (bf16[1536,128]{1,0:T(8,128)(2,1)S(1)}, bf16[1536,128]{1,0:T(8,128)(2,1)S(1)}, u32[]{:S(2)}, u32[]{:S(2)}) collective-permute-start(bf16[1536,128]{1,0:T(8,128)(2,1)S(1)} %get-tuple-element.84.refs_0_), channel_id=1, source_target_pairs={{0,8},{1,9},{2,10},{3,11},{4,12},{5,13},{6,14},{7,15},{8,0},{9,1},... | collective-permute-start | bytes 1179656 | tf_op jit(solution)/shard_map/ppermute | solution.py:356
  69.4 17.1 %collective-permute-start.18 = (bf16[1536,128]{1,0:T(8,128)(2,1)S(1)}, bf16[1536,128]{1,0:T(8,128)(2,1)S(1)}, u32[]{:S(2)}, u32[]{:S(2)}) collective-permute-start(bf16[1536,128]{1,0:T(8,128)(2,1)S(1)} %collective-permute-done.15.refs_1_), channel_id=1, source_target_pairs={{0,1},{1,2},{2,3},{3,0},{4,5},{5,6},{6,7},{7,4},{8,9},{9,10},{10,1... | collective-permute-start | bytes 1179656 | tf_op jit(solution)/shard_map/ppermute | solution.py:356
  70.5 16.0 %collective-permute-start.17 = (bf16[1536,128]{1,0:T(8,128)(2,1)S(1)}, bf16[1536,128]{1,0:T(8,128)(2,1)S(1)}, u32[]{:S(2)}, u32[]{:S(2)}) collective-permute-start(bf16[1536,128]{1,0:T(8,128)(2,1)S(1)} %collective-permute-done.15.refs_1_), channel_id=1, source_target_pairs={{0,3},{1,0},{2,1},{3,2},{4,7},{5,4},{6,5},{7,6},{8,11},{9,8},{10,9... | collective-permute-start | bytes 1179656 | tf_op jit(solution)/shard_map/ppermute | solution.py:356
  73.2 13.4 %collective-permute-start.16 = (bf16[1536,128]{1,0:T(8,128)(2,1)S(1)}, bf16[1536,128]{1,0:T(8,128)(2,1)S(1)}, u32[]{:S(2)}, u32[]{:S(2)}) collective-permute-start(bf16[1536,128]{1,0:T(8,128)(2,1)S(1)} %collective-permute-done.15.refs_1_), channel_id=1, source_target_pairs={{0,2},{1,3},{2,0},{3,1},{4,6},{5,7},{6,4},{7,5},{8,10},{9,11},{10,... | collective-permute-start | bytes 1179656 | tf_op jit(solution)/shard_map/ppermute | solution.py:356

commit v4 on v3

--- a/solution.py
+++ b/solution.py
@@ -8,7 +8,7 @@
 NB = 128
 LOOK = 16
 ORDER = ((1, 3, 2), (2, 3, 1), (2, 3, 1), (2, 3, 1))
-VMEM_LIMIT = 44 * 1024 * 1024
+VMEM_LIMIT = 42 * 1024 * 1024
 F32 = jnp.float32
 BF16 = jnp.bfloat16
 HI = lax.Precision.HIGHEST
@@ -53,12 +53,12 @@
     return pl.CostEstimate(flops=0, transcendentals=0, bytes_accessed=int(us * 3.5e6))
 
 
-def read_half(place_ref, window_ref, buffer, sem):
+def read_half(place_ref, window_ref, buffer, sem, parts=(0, 1, 2, 3)):
     copies = []
-    for n in range(4):
+    for m, n in enumerate(parts):
         part = place_ref[0] * 4 + lax.rem(place_ref[1] + n, 4)
         rows = pl.ds(pl.multiple_of(part * PART, PART), PART)
-        copies.append(pltpu.make_async_copy(window_ref.at[rows, pl.ds(0, NB)], buffer.at[n], sem.at[n]))
+        copies.append(pltpu.make_async_copy(window_ref.at[rows, pl.ds(0, NB)], buffer.at[m], sem.at[m]))
     return copies
 
 
@@ -83,34 +83,36 @@
     )(jnp.stack([half, first]).astype(jnp.int32), window)
 
 
-def pair_up(window, half, first, partners):
+def pair_up(window, half, first, partners, parts):
+    count = len(parts)
+
     def body(place_ref, window_ref, partners_ref, *refs):
-        outs, buffer, paired, sem = refs[:4], refs[4], refs[5], refs[6]
-        copies = read_half(place_ref, window_ref, buffer, sem)
+        outs, buffer, paired, sem = refs[:count], refs[count], refs[count + 1], refs[count + 2]
+        copies = read_half(place_ref, window_ref, buffer, sem, parts)
         for copy in copies:
             copy.start()
-        writes = [pltpu.make_async_copy(paired.at[n], outs[n], sem.at[4 + n]) for n in range(4)]
-        for n in (1, 3, 2, 0):
-            paired[n, PART:, :] = partners_ref[n * PART : (n + 1) * PART, :]
-        for n in range(4):
-            copies[n].wait()
-            paired[n, :PART, :] = buffer[n].astype(BF16)
-            writes[n].start()
+        writes = [pltpu.make_async_copy(paired.at[m], outs[m], sem.at[count + m]) for m in range(count)]
+        for m, n in enumerate(parts):
+            paired[m, PART:, :] = partners_ref[n * PART : (n + 1) * PART, :]
+        for m in range(count):
+            copies[m].wait()
+            paired[m, :PART, :] = buffer[m].astype(BF16)
+            writes[m].start()
         for write in writes:
             write.wait()
 
     return pl.pallas_call(
         body,
         in_specs=[SMEM, HBM, VMEM],
-        out_specs=[ANY] * 4,
-        out_shape=[jax.ShapeDtypeStruct((2 * PART, NB), BF16)] * 4,
+        out_specs=[ANY] * count,
+        out_shape=[jax.ShapeDtypeStruct((2 * PART, NB), BF16)] * count,
         scratch_shapes=[
-            pltpu.VMEM((4, PART, NB), F32),
-            pltpu.VMEM((4, 2 * PART, NB), BF16),
-            pltpu.SemaphoreType.DMA((8,)),
+            pltpu.VMEM((count, PART, NB), F32),
+            pltpu.VMEM((count, 2 * PART, NB), BF16),
+            pltpu.SemaphoreType.DMA((2 * count,)),
         ],
         compiler_params=params(),
-        cost_estimate=cost(2.5),
+        cost_estimate=cost(1.0 + 0.4 * count),
         name="pair_up",
     )(jnp.stack([half, first]).astype(jnp.int32), window, partners)
 
@@ -124,6 +126,9 @@
 
 def factor(places, tiles):
     block_rows = 16
+
+    def across(one, two):
+        return lax.dot_general(one, two, (((0,), (0,)), ((), ())), preferred_element_type=F32)
 
     def body(places_ref, *refs):
         low_ref, inv_ref, weights_ref, work, stack, rows = refs[4:]
@@ -165,13 +170,11 @@
             upper.append(done_left)
             inverse.append(done_right)
             if base + block_rows < NB:
-                work[...] -= lax.dot_general(
-                    done_left,
-                    jnp.concatenate([done_left, done_right], 1),
-                    (((0,), (0,)), ((), ())),
-                    precision=HI,
-                    preferred_element_type=F32,
-                )
+                done = jnp.concatenate([done_left, done_right], 1)
+                high = done.astype(BF16)
+                rest = (done - high.astype(F32)).astype(BF16)
+                change = across(high[:, :NB], high) + across(high[:, :NB], rest) + across(rest[:, :NB], high)
+                work[...] -= change
         up = jnp.concatenate(upper, 0)
         low_ref[...] = jnp.where(row >= col, up.T, 0.0)
         inv = jnp.where(row >= col, jnp.concatenate(inverse, 0), 0.0)
@@ -392,8 +395,9 @@
     own = lax.dynamic_slice(window, (k // 8 * NB, 0), (3 * NB, NB)).astype(BF16)
     partner = lax.ppermute(own, "prow", core_swap())
     partner, others = lax.optimization_barrier((partner, others))
-    messages = pair_up(window, c, along, others)
-    messages, own, partner, keep_scalars = lax.optimization_barrier((messages, own, partner, scalars))
+    messages = pair_up(window, c, along, others, (1, 2, 3))
+    messages, own, partner, others, keep_scalars = lax.optimization_barrier((messages, own, partner, others, scalars))
+    messages = pair_up(window, c, along, others, (0,)) + messages
 
     moved = stage(messages, 0, ORDER[0])
     pair = side_by_side(own, partner, c)
@@ -403,18 +407,20 @@
     message = pick(d_along, moved, ORDER[0])
 
     message, got = lax.optimization_barrier((message, got))
-    moved = stage([message] * 4, 1, ORDER[1])
 
     tiles = over_rows(pair, got, c)
     look = k + jnp.arange(LOOK + 1)
     at = (x - look % 8 // 2) % 4 * 6 + look % 2 * 3 + look // 8 - k // 8
     places = jnp.concatenate([at, look[1:] % 16, jnp.reshape(c, (1,))])
     low, inv, weights = factor(places.astype(jnp.int32), tiles)
+    late, weights = lax.optimization_barrier((message, weights))
+    moved = stage([message, message, late, message], 1, ORDER[1])
     weights = lax.all_to_all(weights, "pcol", 0, 0, tiled=True)
-    moved, weights = lax.optimization_barrier((moved, weights))
+    out = write_panel(scalars, window, low, inv, out)
+    moved, weights, out = lax.optimization_barrier((moved, weights, out))
     message = pick(d_across, moved, ORDER[1])
 
-    message, weights, low = lax.optimization_barrier((message, weights, low))
+    message, weights = lax.optimization_barrier((message, weights))
     mine = message[:PART]
     other = lax.ppermute(message[PART:], "prow", core_swap())
     first = stage([mine] * 4, 0, ORDER[2])
@@ -423,7 +429,6 @@
 
     weights = lax.dynamic_slice(weights, (k * SHARE, 0), (SHARE, NB))
     weights = side_by_side(weights, lax.ppermute(weights, "prow", core_swap()), c)
-    out = write_panel(scalars, window, low, inv, out)
     out = update(scalars, window, weights, [mine, other], places[::4], out)
     first, second, out = lax.optimization_barrier((first, second, out))
     return update(scalars, window, weights, first[1:] + second[1:], places[1:4] + places[5:], out)

time: 92.7 us -> 91.1 us (0.983)
  waiting for transfers between devices: 28.4 us -> 27.4 us
    ppermute x12, waiting for transfers between devices: 18 us -> 16.8 us  [stage(): lax.ppermute(arrays[s], BOTH, split_shift(s, axis))]
    pallas_call x1 -> x2, Pallas kernels: 3.43 us -> 4.46 us  [pair_up(): pl.pallas_call(body, in_specs=[SMEM, HBM, VMEM], out_specs=[ANY] * count,...]
  transfers between devices with their start and end apart: 20 -> 20, of which waited for: 7 -> 7; matrix products, arithmetic and copies ran while one was open for 2% -> 2% of each run, Pallas kernels for 18% -> 19%
where the time goes in v4:
time: 91.1 us; the launch traced here: 90.4 us
  starting transfers between devices  30.2 us (33%)
  Pallas kernels  27.4 us (30%)
  waiting for transfers between devices  27.4 us (30%)
  other arithmetic  3.16 us (3%)
  local copies, waits for them, and re-layouts  1.27 us (1%)
    ppermute x12, waiting for transfers between devices, stage(): lax.ppermute(arrays[s], BOTH, split_shift(s, axis))  16.8 us
    ppermute x12, starting transfers between devices, stage(): lax.ppermute(arrays[s], BOTH, split_shift(s, axis))  16.1 us
    all_to_all x1, waiting for transfers between devices, body(): weights = lax.all_to_all(weights, 'pcol', 0, 0, tiled=True)  9.28 us
    pallas_call x2, Pallas kernels, update(): pl.pallas_call(body, in_specs=[SMEM, HBM, VMEM] + [VMEM] * n + [HBM], out...  8.51 us
    all_to_all x1, starting transfers between devices, body(): weights = lax.all_to_all(weights, 'pcol', 0, 0, tiled=True)  6.86 us
    pallas_call x1, Pallas kernels, keep_column(): pl.pallas_call(body, in_specs=[SMEM, HBM], out_specs=HBM, out_shape=jax.S...  5.7 us
    pallas_call x1, Pallas kernels, factor(): pl.pallas_call(body, in_specs=[SMEM] + [VMEM] * 4, out_specs=[VMEM] * 3,...  5.68 us
    pallas_call x2, Pallas kernels, pair_up(): pl.pallas_call(body, in_specs=[SMEM, HBM, VMEM], out_specs=[ANY] * count,...  4.46 us
  transfers between devices with their start and end apart: 20, of which 7 were waited for; matrix products, arithmetic and copies ran while one was open for 2% of the time, Pallas kernels for 19%

profile of v4, /device:TPU:1, one launch (start us, length us, event | category | flops | bytes accessed | tf_op | source)
XLA Modules:
  0.0 90.4 jit_solution(8982292861889982033)
XLA Ops:
  0.1 2.5 %cast_half.1 = bf16[6144,128]{1,0:T(8,128)(2,1)S(1)} custom-call(s32[2]{0:T(128)S(1)} %pad_add_fusion.1.place_ref, f32[12288,256]{1,0:T(8,128)} %window_ref.13), custom_call_target="tpu_custom_call" | custom-call | bytes 7000000 | tf_op jit(solution)/shard_map/cast_half/pallas_call | solution.py:74
  2.6 1.5 %collective-permute-start.1 = (bf16[6144,128]{1,0:T(8,128)(2,1)S(1)}, bf16[6144,128]{1,0:T(8,128)(2,1)S(1)}, u32[]{:S(2)}, u32[]{:S(2)}) collective-permute-start(bf16[6144,128]{1,0:T(8,128)(2,1)S(1)} %cast_half.1), channel_id=1, source_target_pairs={{0,16},{16,0},{32,48},{48,32},{64,80},{80,64},{96,112},{112,96},{1... | collective-permute-start | bytes 4718600 | tf_op jit(solution)/shard_map/ppermute | solution.py:394
  7.2 2.7 %pair_up.2 = (bf16[3072,128]{1,0:T(8,128)(2,1)}, bf16[3072,128]{1,0:T(8,128)(2,1)S(1)}, bf16[3072,128]{1,0:T(8,128)(2,1)S(1)}) custom-call(s32[2]{0:T(128)S(1)} %pad_add_fusion.place_ref, f32[12288,256]{1,0:T(8,128)} %window_ref.13, bf16[6144,128]{1,0:T(8,128)(2,1)S(1)} %collective-permute-done.1.partners_ref), custom_call_target="tpu_custom_call" | custom-call | bytes 7700000 | tf_op jit(solution)/shard_map/pair_up/pallas_call | solution.py:104
  9.9 1.4 %collective-permute-start.2 = (bf16[3072,128]{1,0:T(8,128)(2,1)}, bf16[3072,128]{1,0:T(8,128)(2,1)}, u32[]{:S(2)}, u32[]{:S(2)}) collective-permute-start(bf16[3072,128]{1,0:T(8,128)(2,1)} %get-tuple-element.51), channel_id=1, source_target_pairs={{0,4},{1,5},{2,6},{3,7},{4,8},{5,9},{6,10},{7,11},{8,12},{9,13},{1... | collective-permute-start | bytes 2359304 | tf_op jit(solution)/shard_map/ppermute | solution.py:359
  11.4 1.5 %collective-permute-start.3 = (bf16[3072,128]{1,0:T(8,128)(2,1)S(1)}, bf16[3072,128]{1,0:T(8,128)(2,1)}, u32[]{:S(2)}, u32[]{:S(2)}) collective-permute-start(bf16[3072,128]{1,0:T(8,128)(2,1)S(1)} %get-tuple-element.52), channel_id=1, source_target_pairs={{0,12},{1,13},{2,14},{3,15},{4,0},{5,1},{6,2},{7,3},{8,4},{9,5},{1... | collective-permute-start | bytes 2359304 | tf_op jit(solution)/shard_map/ppermute | solution.py:359
  12.9 1.6 %collective-permute-start.4 = (bf16[3072,128]{1,0:T(8,128)(2,1)S(1)}, bf16[3072,128]{1,0:T(8,128)(2,1)}, u32[]{:S(2)}, u32[]{:S(2)}) collective-permute-start(bf16[3072,128]{1,0:T(8,128)(2,1)S(1)} %get-tuple-element.53), channel_id=1, source_target_pairs={{0,8},{1,9},{2,10},{3,11},{4,12},{5,13},{6,14},{7,15},{8,0},{9,1},... | collective-permute-start | bytes 2359304 | tf_op jit(solution)/shard_map/ppermute | solution.py:359
  14.5 2.5 %collective-permute-start.5 = (bf16[768,128]{1,0:T(8,128)(2,1)S(1)}, bf16[768,128]{1,0:T(8,128)(2,1)S(1)}, u32[]{:S(2)}, u32[]{:S(2)}) collective-permute-start(bf16[768,128]{1,0:T(8,128)(2,1)S(1)} %maximum_select_fusion.refs_0_), channel_id=1, source_target_pairs={{0,32},{16,112},{32,64},{48,16},{64,96},{80,48},{96,0},{112,80},{1... | collective-permute-start | bytes 589832 | tf_op jit(solution)/shard_map/ppermute | solution.py:367
  17.6 1.8 %pair_up.3 = bf16[3072,128]{1,0:T(8,128)(2,1)S(1)} custom-call(s32[2]{0:T(128)S(1)} %pad_add_fusion.place_ref, f32[12288,256]{1,0:T(8,128)} %window_ref.13, bf16[6144,128]{1,0:T(8,128)(2,1)S(1)} %collective-permute-done.1.partners_ref), custom_call_target="tpu_custom_call" | custom-call | bytes 4900000 | tf_op jit(solution)/shard_map/pair_up/pallas_call | solution.py:104
  19.4 5.7 %keep_column.1._ = f32[12288,256]{1,0:T(8,128)} custom-call(s32[5]{0:T(128)S(1)} %stack.76.s_ref, f32[12288,256]{1,0:T(8,128)} %window_ref.13), custom_call_target="tpu_custom_call" | custom-call | bytes 19250000 | tf_op jit(solution)/shard_map/keep_column/pallas_call | solution.py:233
  25.2 5.1 %collective-permute-done.3 = bf16[3072,128]{1,0:T(8,128)(2,1)} collective-permute-done((bf16[3072,128]{1,0:T(8,128)(2,1)S(1)}, bf16[3072,128]{1,0:T(8,128)(2,1)}, u32[]{:S(2)}, u32[]{:S(2)}) %collective-permute-start.3) | collective-permute-done | bytes 786464 | tf_op jit(solution)/shard_map/ppermute | solution.py:359
  30.2 2.1 %collective-permute-done.4 = bf16[3072,128]{1,0:T(8,128)(2,1)} collective-permute-done((bf16[3072,128]{1,0:T(8,128)(2,1)S(1)}, bf16[3072,128]{1,0:T(8,128)(2,1)}, u32[]{:S(2)}, u32[]{:S(2)}) %collective-permute-start.4) | collective-permute-done | bytes 786464 | tf_op jit(solution)/shard_map/ppermute | solution.py:359
  33.7 2.6 %collective-permute-start.7 = (bf16[1152,128]{1,0:T(8,128)(2,1)S(1)}, bf16[1152,128]{1,0:T(8,128)(2,1)S(1)}, u32[]{:S(2)}, u32[]{:S(2)}) collective-permute-start(bf16[1152,128]{1,0:T(8,128)(2,1)S(1)} %pad_maximum_fusion), channel_id=1, source_target_pairs={{0,16},{16,0},{32,48},{48,32},{64,80},{80,64},{96,112},{112,96},{1... | collective-permute-start | bytes 884744 | tf_op jit(solution)/shard_map/ppermute | solution.py:372
  37.4 1.7 %collective-permute-start.9 = (bf16[3072,128]{1,0:T(8,128)(2,1)S(1)}, bf16[3072,128]{1,0:T(8,128)(2,1)S(1)}, u32[]{:S(2)}, u32[]{:S(2)}) collective-permute-start(bf16[3072,128]{1,0:T(8,128)(2,1)S(1)} %select_select_fusion.1), channel_id=1, source_target_pairs={{0,3},{1,0},{2,1},{3,2},{4,7},{5,4},{6,5},{7,6},{8,11},{9,8},{10,9... | collective-permute-start | bytes 2359304 | tf_op jit(solution)/shard_map/ppermute | solution.py:359
  39.3 5.7 %factor.1 = (f32[128,128]{1,0:T(8,128)S(1)}, f32[128,128]{1,0:T(8,128)S(1)}, bf16[1024,128]{1,0:T(8,128)(2,1)}) custom-call(s32[34]{0:T(128)S(1)} %pad_add_fusion.2.places_ref, bf16[768,128]{1,0:T(8,128)(2,1)S(1)} %maximum_select_fusion.refs_0_, bf16[768,128]{1,0:T(8,128)(2,1)S(1)} %get-tuple-element.88.refs_1_, ...), custom_call_target="tpu_custom_call" | custom-call | bytes 35000000 | tf_op jit(solution)/shard_map/factor/pallas_call | solution.py:193
  45.1 6.9 %all-to-all-start = ((bf16[16,64,128]{2,1,0:T(8,128)(2,1)}), bf16[16,64,128]{2,1,0:T(8,128)(2,1)S(1)}, u32[]{:S(2)}, u32[]{:S(2)}) async-start(bf16[16,64,128]{2,1,0:T(8,128)(2,1)} %bitcast.15), calls=%async_computation | async-start | bytes 524288 | tf_op jit(solution)/shard_map/all_to_all | solution.py:418
  52.6 9.3 %all-to-all-done = bf16[16,64,128]{2,1,0:T(8,128)(2,1)S(1)} async-done(((bf16[16,64,128]{2,1,0:T(8,128)(2,1)}), bf16[16,64,128]{2,1,0:T(8,128)(2,1)S(1)}, u32[]{:S(2)}, u32[]{:S(2)}) %all-to-all-start) | async-done | bytes 262176 | tf_op jit(solution)/shard_map/all_to_all | solution.py:418
  61.9 1.4 %select_select_fusion = bf16[3072,128]{1,0:T(8,128)(2,1)S(1)} fusion(bf16[3072,128]{1,0:T(8,128)(2,1)S(1)} %collective-permute-done.9, bf16[3072,128]{1,0:T(8,128)(2,1)S(1)} %collective-permute-done.10, bf16[3072,128]{1,0:T(8,128)(2,1)S(1)} %select_select_fusion.1, bf16[3072,128]{1,0:T(8,128)(2,1)} %collective-permute-done.8, pred[]{:T(512)S(6)} %eq.83, ...), kind=kLoop, calls=%fused_computation | loop fusion | flops 1179648 | bytes 3932163 | tf_op jit(solution)/shard_map/jit(_where)/select_n | solution.py:122
  63.4 2.3 %collective-permute-start.14 = (bf16[1536,128]{1,0:T(8,128)(2,1)S(1)}, bf16[1536,128]{1,0:T(8,128)(2,1)S(1)}, u32[]{:S(2)}, u32[]{:S(2)}) collective-permute-start(bf16[1536,128]{1,0:T(8,128)(2,1)S(1)} %get-tuple-element.86.refs_0_), channel_id=1, source_target_pairs={{0,4},{1,5},{2,6},{3,7},{4,8},{5,9},{6,10},{7,11},{8,12},{9,13},{1... | collective-permute-start | bytes 1179656 | tf_op jit(solution)/shard_map/ppermute | solution.py:359
  65.7 1.6 %collective-permute-start.13 = (bf16[1536,128]{1,0:T(8,128)(2,1)S(1)}, bf16[1536,128]{1,0:T(8,128)(2,1)S(1)}, u32[]{:S(2)}, u32[]{:S(2)}) collective-permute-start(bf16[1536,128]{1,0:T(8,128)(2,1)S(1)} %get-tuple-element.86.refs_0_), channel_id=1, source_target_pairs={{0,12},{1,13},{2,14},{3,15},{4,0},{5,1},{6,2},{7,3},{8,4},{9,5},{1... | collective-permute-start | bytes 1179656 | tf_op jit(solution)/shard_map/ppermute | solution.py:359
  69.1 1.7 %collective-permute-start.17 = (bf16[1536,128]{1,0:T(8,128)(2,1)S(1)}, bf16[1536,128]{1,0:T(8,128)(2,1)S(1)}, u32[]{:S(2)}, u32[]{:S(2)}) collective-permute-start(bf16[1536,128]{1,0:T(8,128)(2,1)S(1)} %collective-permute-done.15.refs_1_), channel_id=1, source_target_pairs={{0,3},{1,0},{2,1},{3,2},{4,7},{5,4},{6,5},{7,6},{8,11},{9,8},{10,9... | collective-permute-start | bytes 1179656 | tf_op jit(solution)/shard_map/ppermute | solution.py:359
  73.1 3.3 %update.2.refs_6_ = f32[12288,256]{1,0:T(8,128)} custom-call(s32[7]{0:T(128)S(1)} %concatenate.41.s_ref, f32[12288,256]{1,0:T(8,128)} %window_ref.13, bf16[128,128]{1,0:T(8,128)(2,1)S(1)} %maximum_select_fusion.2.weight_ref, bf16[1536,128]{1,0:T(8,128)(2,1)S(1)} %get-tuple-element.86.refs_0_, ...), custom_call_target="tpu_custom_call", output_to_operand_aliasing={{}: (5, {})} | custom-call | bytes 9100000 | tf_op jit(solution)/shard_map/update/pallas_call | solution.py:338
  76.4 4.4 %collective-permute-done.12.refs_0_ = bf16[1536,128]{1,0:T(8,128)(2,1)S(1)} collective-permute-done((bf16[1536,128]{1,0:T(8,128)(2,1)S(1)}, bf16[1536,128]{1,0:T(8,128)(2,1)S(1)}, u32[]{:S(2)}, u32[]{:S(2)}) %collective-permute-start.12) | collective-permute-done | bytes 393248 | tf_op jit(solution)/shard_map/ppermute | solution.py:359
  80.8 4.3 %collective-permute-done.18.refs_5_ = bf16[1536,128]{1,0:T(8,128)(2,1)S(1)} collective-permute-done((bf16[1536,128]{1,0:T(8,128)(2,1)S(1)}, bf16[1536,128]{1,0:T(8,128)(2,1)S(1)}, u32[]{:S(2)}, u32[]{:S(2)}) %collective-permute-start.18) | collective-permute-done | bytes 393248 | tf_op jit(solution)/shard_map/ppermute | solution.py:359
  85.2 5.2 %update.3 = f32[12288,256]{1,0:T(8,128)} custom-call(s32[11]{0:T(128)S(1)} %concatenate.32.s_ref, f32[12288,256]{1,0:T(8,128)} %window_ref.13, bf16[128,128]{1,0:T(8,128)(2,1)S(1)} %maximum_select_fusion.2.weight_ref, bf16[1536,128]{1,0:T(8,128)(2,1)S(1)} %collective-permute-done.12.refs_0_, ...), custom_call_target="tpu_custom_call", output_to_operand_aliasing={{}: (9, {})} | custom-call | bytes 20300000 | tf_op jit(solution)/shard_map/update/pallas_call | solution.py:338
  (45 shorter events, 10.7 us)
Async XLA Ops:
  2.6 4.7 %collective-permute-start.1 = (bf16[6144,128]{1,0:T(8,128)(2,1)S(1)}, bf16[6144,128]{1,0:T(8,128)(2,1)S(1)}, u32[]{:S(2)}, u32[]{:S(2)}) collective-permute-start(bf16[6144,128]{1,0:T(8,128)(2,1)S(1)} %cast_half.1), channel_id=1, source_target_pairs={{0,16},{16,0},{32,48},{48,32},{64,80},{80,64},{96,112},{112,96},{1... | collective-permute-start | bytes 4718600 | tf_op jit(solution)/shard_map/ppermute | solution.py:394
  5.7 1.5 %collective-permute-start = (bf16[384,128]{1,0:T(8,128)(2,1)S(1)}, bf16[384,128]{1,0:T(8,128)(2,1)S(1)}, u32[]{:S(2)}, u32[]{:S(2)}) collective-permute-start(bf16[384,128]{1,0:T(8,128)(2,1)S(1)} %dynamic-slice_convert_fusion), channel_id=1, source_target_pairs={{0,16},{16,0},{32,48},{48,32},{64,80},{80,64},{96,112},{112,96},{1... | collective-permute-start | bytes 294920 | tf_op jit(solution)/shard_map/ppermute | solution.py:396
  9.9 15.3 %collective-permute-start.2 = (bf16[3072,128]{1,0:T(8,128)(2,1)}, bf16[3072,128]{1,0:T(8,128)(2,1)}, u32[]{:S(2)}, u32[]{:S(2)}) collective-permute-start(bf16[3072,128]{1,0:T(8,128)(2,1)} %get-tuple-element.51), channel_id=1, source_target_pairs={{0,4},{1,5},{2,6},{3,7},{4,8},{5,9},{6,10},{7,11},{8,12},{9,13},{1... | collective-permute-start | bytes 2359304 | tf_op jit(solution)/shard_map/ppermute | solution.py:359
  11.4 18.9 %collective-permute-start.3 = (bf16[3072,128]{1,0:T(8,128)(2,1)S(1)}, bf16[3072,128]{1,0:T(8,128)(2,1)}, u32[]{:S(2)}, u32[]{:S(2)}) collective-permute-start(bf16[3072,128]{1,0:T(8,128)(2,1)S(1)} %get-tuple-element.52), channel_id=1, source_target_pairs={{0,12},{1,13},{2,14},{3,15},{4,0},{5,1},{6,2},{7,3},{8,4},{9,5},{1... | collective-permute-start | bytes 2359304 | tf_op jit(solution)/shard_map/ppermute | solution.py:359
  12.9 19.5 %collective-permute-start.4 = (bf16[3072,128]{1,0:T(8,128)(2,1)S(1)}, bf16[3072,128]{1,0:T(8,128)(2,1)}, u32[]{:S(2)}, u32[]{:S(2)}) collective-permute-start(bf16[3072,128]{1,0:T(8,128)(2,1)S(1)} %get-tuple-element.53), channel_id=1, source_target_pairs={{0,8},{1,9},{2,10},{3,11},{4,12},{5,13},{6,14},{7,15},{8,0},{9,1},... | collective-permute-start | bytes 2359304 | tf_op jit(solution)/shard_map/ppermute | solution.py:359
  14.5 10.6 %collective-permute-start.5 = (bf16[768,128]{1,0:T(8,128)(2,1)S(1)}, bf16[768,128]{1,0:T(8,128)(2,1)S(1)}, u32[]{:S(2)}, u32[]{:S(2)}) collective-permute-start(bf16[768,128]{1,0:T(8,128)(2,1)S(1)} %maximum_select_fusion.refs_0_), channel_id=1, source_target_pairs={{0,32},{16,112},{32,64},{48,16},{64,96},{80,48},{96,0},{112,80},{1... | collective-permute-start | bytes 589832 | tf_op jit(solution)/shard_map/ppermute | solution.py:367
  17.0 8.1 %collective-permute-start.6 = (bf16[384,128]{1,0:T(8,128)(2,1)S(1)}, bf16[384,128]{1,0:T(8,128)(2,1)S(1)}, u32[]{:S(2)}, u32[]{:S(2)}) collective-permute-start(bf16[384,128]{1,0:T(8,128)(2,1)S(1)} %dynamic-slice_convert_fusion), channel_id=1, source_target_pairs={{0,64},{16,80},{32,96},{48,112},{64,0},{80,16},{96,32},{112,48},{1... | collective-permute-start | bytes 294920 | tf_op jit(solution)/shard_map/ppermute | solution.py:367
  33.7 5.5 %collective-permute-start.7 = (bf16[1152,128]{1,0:T(8,128)(2,1)S(1)}, bf16[1152,128]{1,0:T(8,128)(2,1)S(1)}, u32[]{:S(2)}, u32[]{:S(2)}) collective-permute-start(bf16[1152,128]{1,0:T(8,128)(2,1)S(1)} %pad_maximum_fusion), channel_id=1, source_target_pairs={{0,16},{16,0},{32,48},{48,32},{64,80},{80,64},{96,112},{112,96},{1... | collective-permute-start | bytes 884744 | tf_op jit(solution)/shard_map/ppermute | solution.py:372
  36.4 25.5 %collective-permute-start.10 = (bf16[3072,128]{1,0:T(8,128)(2,1)S(1)}, bf16[3072,128]{1,0:T(8,128)(2,1)S(1)}, u32[]{:S(2)}, u32[]{:S(2)}) collective-permute-start(bf16[3072,128]{1,0:T(8,128)(2,1)S(1)} %select_select_fusion.1), channel_id=1, source_target_pairs={{0,1},{1,2},{2,3},{3,0},{4,5},{5,6},{6,7},{7,4},{8,9},{9,10},{10,1... | collective-permute-start | bytes 2359304 | tf_op jit(solution)/shard_map/ppermute | solution.py:359
  37.4 24.5 %collective-permute-start.9 = (bf16[3072,128]{1,0:T(8,128)(2,1)S(1)}, bf16[3072,128]{1,0:T(8,128)(2,1)S(1)}, u32[]{:S(2)}, u32[]{:S(2)}) collective-permute-start(bf16[3072,128]{1,0:T(8,128)(2,1)S(1)} %select_select_fusion.1), channel_id=1, source_target_pairs={{0,3},{1,0},{2,1},{3,2},{4,7},{5,4},{6,5},{7,6},{8,11},{9,8},{10,9... | collective-permute-start | bytes 2359304 | tf_op jit(solution)/shard_map/ppermute | solution.py:359
  44.9 16.9 %collective-permute-start.8 = (bf16[3072,128]{1,0:T(8,128)(2,1)S(1)}, bf16[3072,128]{1,0:T(8,128)(2,1)}, u32[]{:S(2)}, u32[]{:S(2)}) collective-permute-start(bf16[3072,128]{1,0:T(8,128)(2,1)S(1)} %select_select_fusion.1), channel_id=1, source_target_pairs={{0,2},{1,3},{2,0},{3,1},{4,6},{5,7},{6,4},{7,5},{8,10},{9,11},{10,... | collective-permute-start | bytes 2359304 | tf_op jit(solution)/shard_map/ppermute | solution.py:359
  45.1 16.8 %all-to-all-start = ((bf16[16,64,128]{2,1,0:T(8,128)(2,1)}), bf16[16,64,128]{2,1,0:T(8,128)(2,1)S(1)}, u32[]{:S(2)}, u32[]{:S(2)}) async-start(bf16[16,64,128]{2,1,0:T(8,128)(2,1)} %bitcast.15), calls=%async_computation | async-start | bytes 524288 | tf_op jit(solution)/shard_map/all_to_all | solution.py:418
  63.3 4.9 %collective-permute-start.15 = (bf16[1536,128]{1,0:T(8,128)(2,1)S(1)}, bf16[1536,128]{1,0:T(8,128)(2,1)S(1)}, u32[]{:S(2)}, u32[]{:S(2)}) collective-permute-start(bf16[1536,128]{1,0:T(8,128)(2,1)S(1)} %get-tuple-element.85), channel_id=1, source_target_pairs={{0,16},{16,0},{32,48},{48,32},{64,80},{80,64},{96,112},{112,96},{1... | collective-permute-start | bytes 1179656 | tf_op jit(solution)/shard_map/ppermute | solution.py:425
  63.4 8.3 %collective-permute-start.14 = (bf16[1536,128]{1,0:T(8,128)(2,1)S(1)}, bf16[1536,128]{1,0:T(8,128)(2,1)S(1)}, u32[]{:S(2)}, u32[]{:S(2)}) collective-permute-start(bf16[1536,128]{1,0:T(8,128)(2,1)S(1)} %get-tuple-element.86.refs_0_), channel_id=1, source_target_pairs={{0,4},{1,5},{2,6},{3,7},{4,8},{5,9},{6,10},{7,11},{8,12},{9,13},{1... | collective-permute-start | bytes 1179656 | tf_op jit(solution)/shard_map/ppermute | solution.py:359
  65.7 3.4 %collective-permute-start.11 = (bf16[64,128]{1,0:T(8,128)(2,1)S(1)}, bf16[64,128]{1,0:T(8,128)(2,1)S(1)}, u32[]{:S(2)}, u32[]{:S(2)}) collective-permute-start(bf16[64,128]{1,0:T(8,128)(2,1)S(1)} %constant_dynamic-slice_fusion), channel_id=1, source_target_pairs={{0,16},{16,0},{32,48},{48,32},{64,80},{80,64},{96,112},{112,96},{1... | collective-permute-start | bytes 49160 | tf_op jit(solution)/shard_map/ppermute | solution.py:431
  65.7 10.7 %collective-permute-start.13 = (bf16[1536,128]{1,0:T(8,128)(2,1)S(1)}, bf16[1536,128]{1,0:T(8,128)(2,1)S(1)}, u32[]{:S(2)}, u32[]{:S(2)}) collective-permute-start(bf16[1536,128]{1,0:T(8,128)(2,1)S(1)} %get-tuple-element.86.refs_0_), channel_id=1, source_target_pairs={{0,12},{1,13},{2,14},{3,15},{4,0},{5,1},{6,2},{7,3},{8,4},{9,5},{1... | collective-permute-start | bytes 1179656 | tf_op jit(solution)/shard_map/ppermute | solution.py:359
  67.3 13.5 %collective-permute-start.12 = (bf16[1536,128]{1,0:T(8,128)(2,1)S(1)}, bf16[1536,128]{1,0:T(8,128)(2,1)S(1)}, u32[]{:S(2)}, u32[]{:S(2)}) collective-permute-start(bf16[1536,128]{1,0:T(8,128)(2,1)S(1)} %get-tuple-element.86.refs_0_), channel_id=1, source_target_pairs={{0,8},{1,9},{2,10},{3,11},{4,12},{5,13},{6,14},{7,15},{8,0},{9,1},... | collective-permute-start | bytes 1179656 | tf_op jit(solution)/shard_map/ppermute | solution.py:359
  68.2 16.9 %collective-permute-start.18 = (bf16[1536,128]{1,0:T(8,128)(2,1)S(1)}, bf16[1536,128]{1,0:T(8,128)(2,1)S(1)}, u32[]{:S(2)}, u32[]{:S(2)}) collective-permute-start(bf16[1536,128]{1,0:T(8,128)(2,1)S(1)} %collective-permute-done.15.refs_1_), channel_id=1, source_target_pairs={{0,1},{1,2},{2,3},{3,0},{4,5},{5,6},{6,7},{7,4},{8,9},{9,10},{10,1... | collective-permute-start | bytes 1179656 | tf_op jit(solution)/shard_map/ppermute | solution.py:359
  69.1 16.0 %collective-permute-start.17 = (bf16[1536,128]{1,0:T(8,128)(2,1)S(1)}, bf16[1536,128]{1,0:T(8,128)(2,1)S(1)}, u32[]{:S(2)}, u32[]{:S(2)}) collective-permute-start(bf16[1536,128]{1,0:T(8,128)(2,1)S(1)} %collective-permute-done.15.refs_1_), channel_id=1, source_target_pairs={{0,3},{1,0},{2,1},{3,2},{4,7},{5,4},{6,5},{7,6},{8,11},{9,8},{10,9... | collective-permute-start | bytes 1179656 | tf_op jit(solution)/shard_map/ppermute | solution.py:359
  71.7 13.4 %collective-permute-start.16 = (bf16[1536,128]{1,0:T(8,128)(2,1)S(1)}, bf16[1536,128]{1,0:T(8,128)(2,1)S(1)}, u32[]{:S(2)}, u32[]{:S(2)}) collective-permute-start(bf16[1536,128]{1,0:T(8,128)(2,1)S(1)} %collective-permute-done.15.refs_1_), channel_id=1, source_target_pairs={{0,2},{1,3},{2,0},{3,1},{4,6},{5,7},{6,4},{7,5},{8,10},{9,11},{10,... | collective-permute-start | bytes 1179656 | tf_op jit(solution)/shard_map/ppermute | solution.py:359

commit v5 on v4

--- a/solution.py
+++ b/solution.py
@@ -7,8 +7,8 @@
 
 NB = 128
 LOOK = 16
-ORDER = ((1, 3, 2), (2, 3, 1), (2, 3, 1), (2, 3, 1))
-VMEM_LIMIT = 42 * 1024 * 1024
+ORDER = ((1, 3, 2), (2, 3, 1), (1, 3, 2), (1, 3, 2))
+VMEM_LIMIT = 20 * 1024 * 1024
 F32 = jnp.float32
 BF16 = jnp.bfloat16
 HI = lax.Precision.HIGHEST
@@ -62,6 +62,10 @@
     return copies
 
 
+def in_hbm(array):
+    return pltpu.with_memory_space_constraint(array, pltpu.HBM)
+
+
 def cast_half(window, half, first):
     def body(place_ref, window_ref, out_ref, buffer, sem):
         copies = read_half(place_ref, window_ref, buffer, sem)
@@ -80,7 +84,7 @@
         compiler_params=params(),
         cost_estimate=cost(2.0),
         name="cast_half",
-    )(jnp.stack([half, first]).astype(jnp.int32), window)
+    )(jnp.stack([half, first]).astype(jnp.int32), in_hbm(window))
 
 
 def pair_up(window, half, first, partners, parts):
@@ -114,7 +118,7 @@
         compiler_params=params(),
         cost_estimate=cost(1.0 + 0.4 * count),
         name="pair_up",
-    )(jnp.stack([half, first]).astype(jnp.int32), window, partners)
+    )(jnp.stack([half, first]).astype(jnp.int32), in_hbm(window), partners)
 
 
 def pick(choice, arrays, order):
@@ -122,6 +126,25 @@
     return jnp.where(
         choice < 2, jnp.where(choice == 0, arrays[0], arrays[1]), jnp.where(choice == 2, arrays[2], arrays[3])
     )
+
+
+def take(choice, arrays, order):
+    def body(choice_ref, *refs):
+        for n, s in enumerate((0,) + order):
+
+            @pl.when(choice_ref[0] == s)
+            def _():
+                refs[4][...] = refs[n][...]
+
+    return pl.pallas_call(
+        body,
+        in_specs=[SMEM] + [VMEM] * 4,
+        out_specs=VMEM,
+        out_shape=jax.ShapeDtypeStruct(arrays[0].shape, BF16),
+        compiler_params=params(),
+        cost_estimate=cost(0.5),
+        name="take",
+    )(jnp.reshape(choice, (1,)).astype(jnp.int32), *arrays)
 
 
 def factor(places, tiles):
@@ -239,7 +262,7 @@
         compiler_params=params(),
         cost_estimate=cost(5.5),
         name="keep_column",
-    )(scalars, window)
+    )(scalars, in_hbm(window))
 
 
 def write_panel(scalars, window, low, inv, out):
@@ -291,34 +314,46 @@
         compiler_params=params(),
         cost_estimate=cost(1.0),
         name="write_panel",
-    )(scalars, window, low, inv, out)
-
-
-def update(scalars, window, weights, parts, places, out):
-    n = len(parts)
+    )(scalars, in_hbm(window), low, inv, out)
+
+
+def update(scalars, window, weights, parts, places, out, ahead=(), held=None):
+    n, more = len(parts), len(ahead)
     size = PART // 2
     blocks = [(m, i) for m in range(n) for i in range(2)]
-    s_all = jnp.concatenate([scalars, jnp.stack(places).astype(jnp.int32)])
-
-    def body(s_ref, window_ref, weight_ref, *refs):
+    s_all = jnp.concatenate([scalars, jnp.stack(list(places) + list(ahead)).astype(jnp.int32)])
+
+    def body(s_ref, source_ref, weight_ref, *refs):
         panels, out_ref = refs[:n], refs[n + 1]
-        buffer, sem = refs[n + 2 :]
+        buffer, sem, ahead_sem = refs[-3:]
         p, j = s_ref[1], s_ref[4]
         lanes = pl.ds(pl.multiple_of(s_ref[3] * NB, NB), NB)
+        reads_ahead = [
+            pltpu.make_async_copy(
+                source_ref.at[pl.ds(pl.multiple_of(s_ref[5 + n + m] * PART, PART), PART), lanes],
+                refs[n + 2].at[m],
+                ahead_sem.at[m],
+            )
+            for m in range(more)
+        ]
 
         def rows(m, i):
             return pl.ds(pl.multiple_of(s_ref[5 + m] * PART + i * size, size), size)
 
         def read(m, i):
-            return pltpu.make_async_copy(window_ref.at[rows(m, i), lanes], buffer.at[m, i], sem.at[0, m, i])
+            return pltpu.make_async_copy(source_ref.at[rows(m, i), lanes], buffer.at[m, i], sem.at[0, m, i])
 
         def write(m, i):
             return pltpu.make_async_copy(buffer.at[m, i], out_ref.at[rows(m, i), lanes], sem.at[1, m, i])
 
+        if held is None:
+            for m, i in blocks:
+                read(m, i).start()
+        for copy in reads_ahead:
+            copy.start()
         for m, i in blocks:
-            read(m, i).start()
-        for m, i in blocks:
-            read(m, i).wait()
+            if held is None:
+                read(m, i).wait()
             for t in range(size // 256):
                 change = lax.dot_general(
                     panels[m][i * size + t * 256 : i * size + (t + 1) * 256, :],
@@ -329,26 +364,34 @@
                 for u in range(2):
                     at = t * 256 + u * NB
                     tile = (s_ref[5 + m] * (PART // NB) + (i * size + at) // NB) * 8 + p
-                    old = buffer[m, i, at : at + NB, :]
+                    if held is None:
+                        old = buffer[m, i, at : at + NB, :]
+                    else:
+                        old = source_ref[m, i * size + at : i * size + at + NB, :]
                     buffer[m, i, at : at + NB, :] = old - jnp.where(tile >= j, change[u * NB : (u + 1) * NB, :], 0.0)
             write(m, i).start()
         for m, i in blocks:
             write(m, i).wait()
-
-    return pl.pallas_call(
-        body,
-        in_specs=[SMEM, HBM, VMEM] + [VMEM] * n + [HBM],
-        out_specs=HBM,
-        out_shape=jax.ShapeDtypeStruct(window.shape, F32),
+        for copy in reads_ahead:
+            copy.wait()
+
+    given = pl.pallas_call(
+        body,
+        in_specs=[SMEM, HBM if held is None else VMEM, VMEM] + [VMEM] * n + [HBM],
+        out_specs=[HBM] + [VMEM] * min(more, 1),
+        out_shape=[jax.ShapeDtypeStruct(window.shape, F32)]
+        + [jax.ShapeDtypeStruct((more, PART, NB), F32)] * min(more, 1),
         scratch_shapes=[
             pltpu.VMEM((n, 2, size, NB), F32),
             pltpu.SemaphoreType.DMA((2, n, 2)),
+            pltpu.SemaphoreType.DMA((max(more, 1),)),
         ],
         input_output_aliases={3 + n: 0},
         compiler_params=params(),
         cost_estimate=cost(1.0 + 0.8 * n),
         name="update",
-    )(s_all, window, weights, *parts, out)
+    )(s_all, in_hbm(window) if held is None else held, weights, *parts, out)
+    return given if more else given[0]
 
 
 def turn(s):
@@ -404,7 +447,7 @@
     got = send_rows(own, pair)
     out = keep_column(keep_scalars, window)
     moved, got, out = lax.optimization_barrier((moved, got, out))
-    message = pick(d_along, moved, ORDER[0])
+    message = take(d_along, moved, ORDER[0])
 
     message, got = lax.optimization_barrier((message, got))
 
@@ -429,9 +472,10 @@
 
     weights = lax.dynamic_slice(weights, (k * SHARE, 0), (SHARE, NB))
     weights = side_by_side(weights, lax.ppermute(weights, "prow", core_swap()), c)
-    out = update(scalars, window, weights, [mine, other], places[::4], out)
-    first, second, out = lax.optimization_barrier((first, second, out))
-    return update(scalars, window, weights, first[1:] + second[1:], places[1:4] + places[5:], out)
+    later = places[1:4] + places[5:]
+    out, held = update(scalars, window, weights, [mine, other], places[::4], out, ahead=later)
+    first, second, out, held = lax.optimization_barrier((first, second, out, held))
+    return update(scalars, window, weights, first[1:] + second[1:], later, out, held=held)
 
 
 def solution(mesh):

time: 91.1 us -> 88.4 us (0.970)
  other arithmetic: 3.16 us -> 0.65 us
    select_n x2 -> x1, other arithmetic: 2.65 us -> 0.14 us  [pick(): jnp.where(choice < 2, jnp.where(choice == 0, arrays[0], arrays[1]), jnp.w...]
    ppermute x1, starting transfers between devices: 0.09 us -> 1.38 us  [body(): other = lax.ppermute(message[PART:], 'prow', core_swap())]
    ppermute x12, starting transfers between devices: 16.1 us -> 15 us  [stage(): lax.ppermute(arrays[s], BOTH, split_shift(s, axis))]
    pallas_call x2 -> x3, Pallas kernels: 8.51 us -> 8.54 us  [the longest x2 7.35 us: update(): pl.pallas_call(body, in_specs=[SMEM, HBM if held is None else VMEM, VMEM]...]
  transfers between devices with their start and end apart: 20 -> 20, of which waited for: 7 -> 7; matrix products, arithmetic and copies ran while one was open for 2% -> 2% of each run, Pallas kernels for 19% -> 20%
where the time goes in v5:
time: 88.4 us; the launch traced here: 88.1 us
  starting transfers between devices  30 us (34%)
  Pallas kernels  28 us (32%)
  waiting for transfers between devices  27.2 us (31%)
  local copies, waits for them, and re-layouts  1.27 us (1%)
  between operations  0.92 us (1%)
    ppermute x12, waiting for transfers between devices, stage(): lax.ppermute(arrays[s], BOTH, split_shift(s, axis))  16.5 us
    ppermute x12, starting transfers between devices, stage(): lax.ppermute(arrays[s], BOTH, split_shift(s, axis))  15 us
    all_to_all x1, waiting for transfers between devices, body(): weights = lax.all_to_all(weights, 'pcol', 0, 0, tiled=True)  9.49 us
    pallas_call x2, Pallas kernels, update(): pl.pallas_call(body, in_specs=[SMEM, HBM if held is None else VMEM, VMEM]...  7.35 us
    all_to_all x1, starting transfers between devices, body(): weights = lax.all_to_all(weights, 'pcol', 0, 0, tiled=True)  6.64 us
    pallas_call x1, Pallas kernels, keep_column(): pl.pallas_call(body, in_specs=[SMEM, HBM], out_specs=HBM, out_shape=jax.S...  5.7 us
    pallas_call x1, Pallas kernels, factor(): pl.pallas_call(body, in_specs=[SMEM] + [VMEM] * 4, out_specs=[VMEM] * 3,...  5.66 us
    pallas_call x2, Pallas kernels, pair_up(): pl.pallas_call(body, in_specs=[SMEM, HBM, VMEM], out_specs=[ANY] * count,...  5.01 us
  transfers between devices with their start and end apart: 20, of which 7 were waited for; matrix products, arithmetic and copies ran while one was open for 2% of the time, Pallas kernels for 20%

profile of v5, /device:TPU:1, one launch (start us, length us, event | category | flops | bytes accessed | tf_op | source)
XLA Modules:
  0.0 88.1 jit_solution(3670473585909768167)
XLA Ops:
  0.1 2.5 %cast_half.1 = bf16[6144,128]{1,0:T(8,128)(2,1)S(1)} custom-call(s32[2]{0:T(128)S(1)} %pad_add_fusion.1.place_ref, f32[12288,256]{1,0:T(8,128)} %source_ref.1), custom_call_target="tpu_custom_call" | custom-call | bytes 7000000 | tf_op jit(solution)/shard_map/cast_half/pallas_call | solution.py:78
  2.6 1.5 %collective-permute-start.1 = (bf16[6144,128]{1,0:T(8,128)(2,1)S(1)}, bf16[6144,128]{1,0:T(8,128)(2,1)S(1)}, u32[]{:S(2)}, u32[]{:S(2)}) collective-permute-start(bf16[6144,128]{1,0:T(8,128)(2,1)S(1)} %cast_half.1), channel_id=1, source_target_pairs={{0,16},{16,0},{32,48},{48,32},{64,80},{80,64},{96,112},{112,96},{1... | collective-permute-start | bytes 4718600 | tf_op jit(solution)/shard_map/ppermute | solution.py:437
  7.2 3.2 %pair_up.2 = (bf16[3072,128]{1,0:T(8,128)(2,1)}, bf16[3072,128]{1,0:T(8,128)(2,1)}, bf16[3072,128]{1,0:T(8,128)(2,1)}) custom-call(s32[2]{0:T(128)S(1)} %pad_add_fusion.place_ref, f32[12288,256]{1,0:T(8,128)} %source_ref.1, bf16[6144,128]{1,0:T(8,128)(2,1)S(1)} %collective-permute-done.1.partners_ref), custom_call_target="tpu_custom_call" | custom-call | bytes 7700000 | tf_op jit(solution)/shard_map/pair_up/pallas_call | solution.py:108
  10.4 1.4 %collective-permute-start.2 = (bf16[3072,128]{1,0:T(8,128)(2,1)}, bf16[3072,128]{1,0:T(8,128)(2,1)S(1)}, u32[]{:S(2)}, u32[]{:S(2)}) collective-permute-start(bf16[3072,128]{1,0:T(8,128)(2,1)} %get-tuple-element.54), channel_id=1, source_target_pairs={{0,4},{1,5},{2,6},{3,7},{4,8},{5,9},{6,10},{7,11},{8,12},{9,13},{1... | collective-permute-start | bytes 2359304 | tf_op jit(solution)/shard_map/ppermute | solution.py:402
  11.9 1.5 %collective-permute-start.3 = (bf16[3072,128]{1,0:T(8,128)(2,1)}, bf16[3072,128]{1,0:T(8,128)(2,1)S(1)}, u32[]{:S(2)}, u32[]{:S(2)}) collective-permute-start(bf16[3072,128]{1,0:T(8,128)(2,1)} %get-tuple-element.55), channel_id=1, source_target_pairs={{0,12},{1,13},{2,14},{3,15},{4,0},{5,1},{6,2},{7,3},{8,4},{9,5},{1... | collective-permute-start | bytes 2359304 | tf_op jit(solution)/shard_map/ppermute | solution.py:402
  13.4 1.6 %collective-permute-start.4 = (bf16[3072,128]{1,0:T(8,128)(2,1)}, bf16[3072,128]{1,0:T(8,128)(2,1)}, u32[]{:S(2)}, u32[]{:S(2)}) collective-permute-start(bf16[3072,128]{1,0:T(8,128)(2,1)} %get-tuple-element.56), channel_id=1, source_target_pairs={{0,8},{1,9},{2,10},{3,11},{4,12},{5,13},{6,14},{7,15},{8,0},{9,1},... | collective-permute-start | bytes 2359304 | tf_op jit(solution)/shard_map/ppermute | solution.py:402
  15.0 2.5 %collective-permute-start.5 = (bf16[768,128]{1,0:T(8,128)(2,1)S(1)}, bf16[768,128]{1,0:T(8,128)(2,1)S(1)}, u32[]{:S(2)}, u32[]{:S(2)}) collective-permute-start(bf16[768,128]{1,0:T(8,128)(2,1)S(1)} %maximum_select_fusion.refs_0_), channel_id=1, source_target_pairs={{0,32},{16,112},{32,64},{48,16},{64,96},{80,48},{96,0},{112,80},{1... | collective-permute-start | bytes 589832 | tf_op jit(solution)/shard_map/ppermute | solution.py:410
  18.1 5.7 %keep_column.1._ = f32[12288,256]{1,0:T(8,128)} custom-call(s32[5]{0:T(128)S(1)} %stack.82.s_ref, f32[12288,256]{1,0:T(8,128)} %source_ref.1), custom_call_target="tpu_custom_call" | custom-call | bytes 19250000 | tf_op jit(solution)/shard_map/keep_column/pallas_call | solution.py:256
  23.8 1.8 %pair_up.3.refs_0_ = bf16[3072,128]{1,0:T(8,128)(2,1)S(1)} custom-call(s32[2]{0:T(128)S(1)} %pad_add_fusion.place_ref, f32[12288,256]{1,0:T(8,128)} %source_ref.1, bf16[6144,128]{1,0:T(8,128)(2,1)S(1)} %collective-permute-done.1.partners_ref), custom_call_target="tpu_custom_call" | custom-call | bytes 4900000 | tf_op jit(solution)/shard_map/pair_up/pallas_call | solution.py:108
  25.7 5.4 %collective-permute-done.3.refs_2_ = bf16[3072,128]{1,0:T(8,128)(2,1)S(1)} collective-permute-done((bf16[3072,128]{1,0:T(8,128)(2,1)}, bf16[3072,128]{1,0:T(8,128)(2,1)S(1)}, u32[]{:S(2)}, u32[]{:S(2)}) %collective-permute-start.3) | collective-permute-done | bytes 786464 | tf_op jit(solution)/shard_map/ppermute | solution.py:402
  31.1 1.8 %collective-permute-done.4.refs_3_ = bf16[3072,128]{1,0:T(8,128)(2,1)} collective-permute-done((bf16[3072,128]{1,0:T(8,128)(2,1)}, bf16[3072,128]{1,0:T(8,128)(2,1)}, u32[]{:S(2)}, u32[]{:S(2)}) %collective-permute-start.4) | collective-permute-done | bytes 786464 | tf_op jit(solution)/shard_map/ppermute | solution.py:402
  34.1 2.3 %collective-permute-start.7 = (bf16[1152,128]{1,0:T(8,128)(2,1)S(1)}, bf16[1152,128]{1,0:T(8,128)(2,1)S(1)}, u32[]{:S(2)}, u32[]{:S(2)}) collective-permute-start(bf16[1152,128]{1,0:T(8,128)(2,1)S(1)} %pad_maximum_fusion), channel_id=1, source_target_pairs={{0,16},{16,0},{32,48},{48,32},{64,80},{80,64},{96,112},{112,96},{1... | collective-permute-start | bytes 884744 | tf_op jit(solution)/shard_map/ppermute | solution.py:415
  37.8 1.5 %collective-permute-start.9 = (bf16[3072,128]{1,0:T(8,128)(2,1)S(1)}, bf16[3072,128]{1,0:T(8,128)(2,1)S(1)}, u32[]{:S(2)}, u32[]{:S(2)}) collective-permute-start(bf16[3072,128]{1,0:T(8,128)(2,1)S(1)} %take.1), channel_id=1, source_target_pairs={{0,3},{1,0},{2,1},{3,2},{4,7},{5,4},{6,5},{7,6},{8,11},{9,8},{10,9... | collective-permute-start | bytes 2359304 | tf_op jit(solution)/shard_map/ppermute | solution.py:402
  39.5 5.7 %factor.1 = (f32[128,128]{1,0:T(8,128)S(1)}, f32[128,128]{1,0:T(8,128)S(1)}, bf16[1024,128]{1,0:T(8,128)(2,1)}) custom-call(s32[34]{0:T(128)S(1)} %pad_add_fusion.2.places_ref, bf16[768,128]{1,0:T(8,128)(2,1)S(1)} %maximum_select_fusion.refs_0_, bf16[768,128]{1,0:T(8,128)(2,1)S(1)} %get-tuple-element.94.refs_1_, ...), custom_call_target="tpu_custom_call" | custom-call | bytes 35000000 | tf_op jit(solution)/shard_map/factor/pallas_call | solution.py:216
  45.5 6.6 %all-to-all-start = ((bf16[16,64,128]{2,1,0:T(8,128)(2,1)}), bf16[16,64,128]{2,1,0:T(8,128)(2,1)S(1)}, u32[]{:S(2)}, u32[]{:S(2)}) async-start(bf16[16,64,128]{2,1,0:T(8,128)(2,1)} %bitcast.16), calls=%async_computation | async-start | bytes 524288 | tf_op jit(solution)/shard_map/all_to_all | solution.py:461
  52.8 9.5 %all-to-all-done = bf16[16,64,128]{2,1,0:T(8,128)(2,1)S(1)} async-done(((bf16[16,64,128]{2,1,0:T(8,128)(2,1)}), bf16[16,64,128]{2,1,0:T(8,128)(2,1)S(1)}, u32[]{:S(2)}, u32[]{:S(2)}) %all-to-all-start) | async-done | bytes 262176 | tf_op jit(solution)/shard_map/all_to_all | solution.py:461
  62.5 1.4 %collective-permute-start.14 = (bf16[1536,128]{1,0:T(8,128)(2,1)S(1)}, bf16[1536,128]{1,0:T(8,128)(2,1)S(1)}, u32[]{:S(2)}, u32[]{:S(2)}) collective-permute-start(bf16[1536,128]{1,0:T(8,128)(2,1)S(1)} %get-tuple-element.91), channel_id=1, source_target_pairs={{0,16},{16,0},{32,48},{48,32},{64,80},{80,64},{96,112},{112,96},{1... | collective-permute-start | bytes 1179656 | tf_op jit(solution)/shard_map/ppermute | solution.py:468
  65.1 1.5 %collective-permute-start.12 = (bf16[1536,128]{1,0:T(8,128)(2,1)S(1)}, bf16[1536,128]{1,0:T(8,128)(2,1)S(1)}, u32[]{:S(2)}, u32[]{:S(2)}) collective-permute-start(bf16[1536,128]{1,0:T(8,128)(2,1)S(1)} %get-tuple-element.92.refs_0_), channel_id=1, source_target_pairs={{0,12},{1,13},{2,14},{3,15},{4,0},{5,1},{6,2},{7,3},{8,4},{9,5},{1... | collective-permute-start | bytes 1179656 | tf_op jit(solution)/shard_map/ppermute | solution.py:402
  68.3 1.6 %collective-permute-start.16 = (bf16[1536,128]{1,0:T(8,128)(2,1)S(1)}, bf16[1536,128]{1,0:T(8,128)(2,1)S(1)}, u32[]{:S(2)}, u32[]{:S(2)}) collective-permute-start(bf16[1536,128]{1,0:T(8,128)(2,1)S(1)} %collective-permute-done.14.refs_1_), channel_id=1, source_target_pairs={{0,3},{1,0},{2,1},{3,2},{4,7},{5,4},{6,5},{7,6},{8,11},{9,8},{10,9... | collective-permute-start | bytes 1179656 | tf_op jit(solution)/shard_map/ppermute | solution.py:402
  70.0 2.1 %collective-permute-done.11.refs_0_ = bf16[1536,128]{1,0:T(8,128)(2,1)S(1)} collective-permute-done((bf16[1536,128]{1,0:T(8,128)(2,1)S(1)}, bf16[1536,128]{1,0:T(8,128)(2,1)S(1)}, u32[]{:S(2)}, u32[]{:S(2)}) %collective-permute-start.11) | collective-permute-done | bytes 393248 | tf_op jit(solution)/shard_map/ppermute | solution.py:402
  73.5 4.2 %update.2 = (f32[12288,256]{1,0:T(8,128)}, f32[6,1536,128]{2,1,0:T(8,128)S(1)}) custom-call(s32[13]{0:T(128)S(1)} %concatenate.39.s_ref, f32[12288,256]{1,0:T(8,128)} %source_ref.1, bf16[128,128]{1,0:T(8,128)(2,1)S(1)} %maximum_select_fusion.2.weight_ref, bf16[1536,128]{1,0:T(8,128)(2,1)S(1)} %get-tuple-element.92.refs_0_, ...), custom_call_target="tpu_custom_call", output_to_operand_aliasing={{0}: (5, {})} | custom-call | bytes 9100000 | tf_op jit(solution)/shard_map/update/pallas_call | solution.py:378
  77.7 2.6 %collective-permute-done.13.refs_2_ = bf16[1536,128]{1,0:T(8,128)(2,1)S(1)} collective-permute-done((bf16[1536,128]{1,0:T(8,128)(2,1)S(1)}, bf16[1536,128]{1,0:T(8,128)(2,1)S(1)}, u32[]{:S(2)}, u32[]{:S(2)}) %collective-permute-start.13) | collective-permute-done | bytes 393248 | tf_op jit(solution)/shard_map/ppermute | solution.py:402
  80.3 4.6 %collective-permute-done.15.refs_3_ = bf16[1536,128]{1,0:T(8,128)(2,1)S(1)} collective-permute-done((bf16[1536,128]{1,0:T(8,128)(2,1)S(1)}, bf16[1536,128]{1,0:T(8,128)(2,1)S(1)}, u32[]{:S(2)}, u32[]{:S(2)}) %collective-permute-start.15) | collective-permute-done | bytes 393248 | tf_op jit(solution)/shard_map/ppermute | solution.py:402
  84.9 3.2 %update.3 = f32[12288,256]{1,0:T(8,128)} custom-call(s32[11]{0:T(128)S(1)} %concatenate.32.s_ref, f32[6,1536,128]{2,1,0:T(8,128)S(1)} %get-tuple-element.83.source_ref, bf16[128,128]{1,0:T(8,128)(2,1)S(1)} %maximum_select_fusion.2.weight_ref, bf16[1536,128]{1,0:T(8,128)(2,1)S(1)} %collective-permute-done.11.refs_0_, ...), custom_call_target="tpu_custom_call", output_to_operand_aliasing={{}: (9, {})} | custom-call | bytes 20300000 | tf_op jit(solution)/shard_map/update/pallas_call | solution.py:378
  (45 shorter events, 11.4 us)
Async XLA Ops:
  2.6 4.7 %collective-permute-start.1 = (bf16[6144,128]{1,0:T(8,128)(2,1)S(1)}, bf16[6144,128]{1,0:T(8,128)(2,1)S(1)}, u32[]{:S(2)}, u32[]{:S(2)}) collective-permute-start(bf16[6144,128]{1,0:T(8,128)(2,1)S(1)} %cast_half.1), channel_id=1, source_target_pairs={{0,16},{16,0},{32,48},{48,32},{64,80},{80,64},{96,112},{112,96},{1... | collective-permute-start | bytes 4718600 | tf_op jit(solution)/shard_map/ppermute | solution.py:437
  5.7 1.5 %collective-permute-start = (bf16[384,128]{1,0:T(8,128)(2,1)S(1)}, bf16[384,128]{1,0:T(8,128)(2,1)S(1)}, u32[]{:S(2)}, u32[]{:S(2)}) collective-permute-start(bf16[384,128]{1,0:T(8,128)(2,1)S(1)} %dynamic-slice_convert_fusion), channel_id=1, source_target_pairs={{0,16},{16,0},{32,48},{48,32},{64,80},{80,64},{96,112},{112,96},{1... | collective-permute-start | bytes 294920 | tf_op jit(solution)/shard_map/ppermute | solution.py:439
  10.4 15.3 %collective-permute-start.2 = (bf16[3072,128]{1,0:T(8,128)(2,1)}, bf16[3072,128]{1,0:T(8,128)(2,1)S(1)}, u32[]{:S(2)}, u32[]{:S(2)}) collective-permute-start(bf16[3072,128]{1,0:T(8,128)(2,1)} %get-tuple-element.54), channel_id=1, source_target_pairs={{0,4},{1,5},{2,6},{3,7},{4,8},{5,9},{6,10},{7,11},{8,12},{9,13},{1... | collective-permute-start | bytes 2359304 | tf_op jit(solution)/shard_map/ppermute | solution.py:402
  11.9 19.2 %collective-permute-start.3 = (bf16[3072,128]{1,0:T(8,128)(2,1)}, bf16[3072,128]{1,0:T(8,128)(2,1)S(1)}, u32[]{:S(2)}, u32[]{:S(2)}) collective-permute-start(bf16[3072,128]{1,0:T(8,128)(2,1)} %get-tuple-element.55), channel_id=1, source_target_pairs={{0,12},{1,13},{2,14},{3,15},{4,0},{5,1},{6,2},{7,3},{8,4},{9,5},{1... | collective-permute-start | bytes 2359304 | tf_op jit(solution)/shard_map/ppermute | solution.py:402
  13.4 19.5 %collective-permute-start.4 = (bf16[3072,128]{1,0:T(8,128)(2,1)}, bf16[3072,128]{1,0:T(8,128)(2,1)}, u32[]{:S(2)}, u32[]{:S(2)}) collective-permute-start(bf16[3072,128]{1,0:T(8,128)(2,1)} %get-tuple-element.56), channel_id=1, source_target_pairs={{0,8},{1,9},{2,10},{3,11},{4,12},{5,13},{6,14},{7,15},{8,0},{9,1},... | collective-permute-start | bytes 2359304 | tf_op jit(solution)/shard_map/ppermute | solution.py:402
  15.0 10.6 %collective-permute-start.5 = (bf16[768,128]{1,0:T(8,128)(2,1)S(1)}, bf16[768,128]{1,0:T(8,128)(2,1)S(1)}, u32[]{:S(2)}, u32[]{:S(2)}) collective-permute-start(bf16[768,128]{1,0:T(8,128)(2,1)S(1)} %maximum_select_fusion.refs_0_), channel_id=1, source_target_pairs={{0,32},{16,112},{32,64},{48,16},{64,96},{80,48},{96,0},{112,80},{1... | collective-permute-start | bytes 589832 | tf_op jit(solution)/shard_map/ppermute | solution.py:410
  17.6 8.1 %collective-permute-start.6 = (bf16[384,128]{1,0:T(8,128)(2,1)S(1)}, bf16[384,128]{1,0:T(8,128)(2,1)S(1)}, u32[]{:S(2)}, u32[]{:S(2)}) collective-permute-start(bf16[384,128]{1,0:T(8,128)(2,1)S(1)} %dynamic-slice_convert_fusion), channel_id=1, source_target_pairs={{0,64},{16,80},{32,96},{48,112},{64,0},{80,16},{96,32},{112,48},{1... | collective-permute-start | bytes 294920 | tf_op jit(solution)/shard_map/ppermute | solution.py:410
  34.1 5.2 %collective-permute-start.7 = (bf16[1152,128]{1,0:T(8,128)(2,1)S(1)}, bf16[1152,128]{1,0:T(8,128)(2,1)S(1)}, u32[]{:S(2)}, u32[]{:S(2)}) collective-permute-start(bf16[1152,128]{1,0:T(8,128)(2,1)S(1)} %pad_maximum_fusion), channel_id=1, source_target_pairs={{0,16},{16,0},{32,48},{48,32},{64,80},{80,64},{96,112},{112,96},{1... | collective-permute-start | bytes 884744 | tf_op jit(solution)/shard_map/ppermute | solution.py:415
  36.6 25.7 %collective-permute-start.10 = (bf16[3072,128]{1,0:T(8,128)(2,1)S(1)}, bf16[3072,128]{1,0:T(8,128)(2,1)S(1)}, u32[]{:S(2)}, u32[]{:S(2)}) collective-permute-start(bf16[3072,128]{1,0:T(8,128)(2,1)S(1)} %take.1), channel_id=1, source_target_pairs={{0,1},{1,2},{2,3},{3,0},{4,5},{5,6},{6,7},{7,4},{8,9},{9,10},{10,1... | collective-permute-start | bytes 2359304 | tf_op jit(solution)/shard_map/ppermute | solution.py:402
  37.8 24.5 %collective-permute-start.9 = (bf16[3072,128]{1,0:T(8,128)(2,1)S(1)}, bf16[3072,128]{1,0:T(8,128)(2,1)S(1)}, u32[]{:S(2)}, u32[]{:S(2)}) collective-permute-start(bf16[3072,128]{1,0:T(8,128)(2,1)S(1)} %take.1), channel_id=1, source_target_pairs={{0,3},{1,0},{2,1},{3,2},{4,7},{5,4},{6,5},{7,6},{8,11},{9,8},{10,9... | collective-permute-start | bytes 2359304 | tf_op jit(solution)/shard_map/ppermute | solution.py:402
  45.1 17.1 %collective-permute-start.8 = (bf16[3072,128]{1,0:T(8,128)(2,1)S(1)}, bf16[3072,128]{1,0:T(8,128)(2,1)S(1)}, u32[]{:S(2)}, u32[]{:S(2)}) collective-permute-start(bf16[3072,128]{1,0:T(8,128)(2,1)S(1)} %take.1), channel_id=1, source_target_pairs={{0,2},{1,3},{2,0},{3,1},{4,6},{5,7},{6,4},{7,5},{8,10},{9,11},{10,... | collective-permute-start | bytes 2359304 | tf_op jit(solution)/shard_map/ppermute | solution.py:402
  45.5 16.8 %all-to-all-start = ((bf16[16,64,128]{2,1,0:T(8,128)(2,1)}), bf16[16,64,128]{2,1,0:T(8,128)(2,1)S(1)}, u32[]{:S(2)}, u32[]{:S(2)}) async-start(bf16[16,64,128]{2,1,0:T(8,128)(2,1)} %bitcast.16), calls=%async_computation | async-start | bytes 524288 | tf_op jit(solution)/shard_map/all_to_all | solution.py:461
  62.5 4.7 %collective-permute-start.14 = (bf16[1536,128]{1,0:T(8,128)(2,1)S(1)}, bf16[1536,128]{1,0:T(8,128)(2,1)S(1)}, u32[]{:S(2)}, u32[]{:S(2)}) collective-permute-start(bf16[1536,128]{1,0:T(8,128)(2,1)S(1)} %get-tuple-element.91), channel_id=1, source_target_pairs={{0,16},{16,0},{32,48},{48,32},{64,80},{80,64},{96,112},{112,96},{1... | collective-permute-start | bytes 1179656 | tf_op jit(solution)/shard_map/ppermute | solution.py:468
  63.9 8.1 %collective-permute-start.11 = (bf16[1536,128]{1,0:T(8,128)(2,1)S(1)}, bf16[1536,128]{1,0:T(8,128)(2,1)S(1)}, u32[]{:S(2)}, u32[]{:S(2)}) collective-permute-start(bf16[1536,128]{1,0:T(8,128)(2,1)S(1)} %get-tuple-element.92.refs_0_), channel_id=1, source_target_pairs={{0,4},{1,5},{2,6},{3,7},{4,8},{5,9},{6,10},{7,11},{8,12},{9,13},{1... | collective-permute-start | bytes 1179656 | tf_op jit(solution)/shard_map/ppermute | solution.py:402
  65.1 3.3 %collective-permute-start.18 = (bf16[64,128]{1,0:T(8,128)(2,1)S(1)}, bf16[64,128]{1,0:T(8,128)(2,1)S(1)}, u32[]{:S(2)}, u32[]{:S(2)}) collective-permute-start(bf16[64,128]{1,0:T(8,128)(2,1)S(1)} %constant_dynamic-slice_fusion), channel_id=1, source_target_pairs={{0,16},{16,0},{32,48},{48,32},{64,80},{80,64},{96,112},{112,96},{1... | collective-permute-start | bytes 49160 | tf_op jit(solution)/shard_map/ppermute | solution.py:474
  65.1 12.6 %collective-permute-start.12 = (bf16[1536,128]{1,0:T(8,128)(2,1)S(1)}, bf16[1536,128]{1,0:T(8,128)(2,1)S(1)}, u32[]{:S(2)}, u32[]{:S(2)}) collective-permute-start(bf16[1536,128]{1,0:T(8,128)(2,1)S(1)} %get-tuple-element.92.refs_0_), channel_id=1, source_target_pairs={{0,12},{1,13},{2,14},{3,15},{4,0},{5,1},{6,2},{7,3},{8,4},{9,5},{1... | collective-permute-start | bytes 1179656 | tf_op jit(solution)/shard_map/ppermute | solution.py:402
  66.6 13.7 %collective-permute-start.13 = (bf16[1536,128]{1,0:T(8,128)(2,1)S(1)}, bf16[1536,128]{1,0:T(8,128)(2,1)S(1)}, u32[]{:S(2)}, u32[]{:S(2)}) collective-permute-start(bf16[1536,128]{1,0:T(8,128)(2,1)S(1)} %get-tuple-element.92.refs_0_), channel_id=1, source_target_pairs={{0,8},{1,9},{2,10},{3,11},{4,12},{5,13},{6,14},{7,15},{8,0},{9,1},... | collective-permute-start | bytes 1179656 | tf_op jit(solution)/shard_map/ppermute | solution.py:402
  67.2 17.7 %collective-permute-start.15 = (bf16[1536,128]{1,0:T(8,128)(2,1)S(1)}, bf16[1536,128]{1,0:T(8,128)(2,1)S(1)}, u32[]{:S(2)}, u32[]{:S(2)}) collective-permute-start(bf16[1536,128]{1,0:T(8,128)(2,1)S(1)} %collective-permute-done.14.refs_1_), channel_id=1, source_target_pairs={{0,1},{1,2},{2,3},{3,0},{4,5},{5,6},{6,7},{7,4},{8,9},{9,10},{10,1... | collective-permute-start | bytes 1179656 | tf_op jit(solution)/shard_map/ppermute | solution.py:402
  68.3 16.6 %collective-permute-start.16 = (bf16[1536,128]{1,0:T(8,128)(2,1)S(1)}, bf16[1536,128]{1,0:T(8,128)(2,1)S(1)}, u32[]{:S(2)}, u32[]{:S(2)}) collective-permute-start(bf16[1536,128]{1,0:T(8,128)(2,1)S(1)} %collective-permute-done.14.refs_1_), channel_id=1, source_target_pairs={{0,3},{1,0},{2,1},{3,2},{4,7},{5,4},{6,5},{7,6},{8,11},{9,8},{10,9... | collective-permute-start | bytes 1179656 | tf_op jit(solution)/shard_map/ppermute | solution.py:402
  72.0 12.9 %collective-permute-start.17 = (bf16[1536,128]{1,0:T(8,128)(2,1)S(1)}, bf16[1536,128]{1,0:T(8,128)(2,1)S(1)}, u32[]{:S(2)}, u32[]{:S(2)}) collective-permute-start(bf16[1536,128]{1,0:T(8,128)(2,1)S(1)} %collective-permute-done.14.refs_1_), channel_id=1, source_target_pairs={{0,2},{1,3},{2,0},{3,1},{4,6},{5,7},{6,4},{7,5},{8,10},{9,11},{10,... | collective-permute-start | bytes 1179656 | tf_op jit(solution)/shard_map/ppermute | solution.py:402

commit v6 on v5

--- a/solution.py
+++ b/solution.py
@@ -196,8 +196,8 @@
                 done = jnp.concatenate([done_left, done_right], 1)
                 high = done.astype(BF16)
                 rest = (done - high.astype(F32)).astype(BF16)
-                change = across(high[:, :NB], high) + across(high[:, :NB], rest) + across(rest[:, :NB], high)
-                work[...] -= change
+                left_sides = jnp.concatenate([high[:, :NB], high[:, :NB], rest[:, :NB]], 0)
+                work[...] -= across(left_sides, jnp.concatenate([high, rest, high], 0))
         up = jnp.concatenate(upper, 0)
         low_ref[...] = jnp.where(row >= col, up.T, 0.0)
         inv = jnp.where(row >= col, jnp.concatenate(inverse, 0), 0.0)
@@ -209,8 +209,10 @@
             row = places_ref[n] * NB + places_ref[2 * LOOK + 1] * SHARE
             place = pl.multiple_of(places_ref[LOOK + n] * SHARE, SHARE)
             rows[pl.ds(place, SHARE), :] = stack[pl.ds(pl.multiple_of(row, SHARE), SHARE), :]
-        full = lax.dot_general(rows[...], high, (((1,), (0,)), ((), ())), preferred_element_type=F32)
-        full += lax.dot_general(rows[...], rest, (((1,), (0,)), ((), ())), preferred_element_type=F32)
+        twice = jnp.concatenate([rows[...], rows[...]], 1)
+        full = lax.dot_general(
+            twice, jnp.concatenate([high, rest], 0), (((1,), (0,)), ((), ())), preferred_element_type=F32
+        )
         weights_ref[...] = full.astype(BF16)
 
     return pl.pallas_call(

time: 88.4 us -> 88.4 us (level)
  no operation moved by 1% of the time
where the time goes in v6:
time: 88.4 us; the launch traced here: 88.1 us
  starting transfers between devices  30 us (34%)
  waiting for transfers between devices  27.7 us (31%)
  Pallas kernels  27.6 us (31%)
  local copies, waits for them, and re-layouts  1.27 us (1%)
  between operations  0.92 us (1%)
    ppermute x12, waiting for transfers between devices, stage(): lax.ppermute(arrays[s], BOTH, split_shift(s, axis))  16.5 us
    ppermute x12, starting transfers between devices, stage(): lax.ppermute(arrays[s], BOTH, split_shift(s, axis))  14.9 us
    all_to_all x1, waiting for transfers between devices, body(): weights = lax.all_to_all(weights, 'pcol', 0, 0, tiled=True)  9.92 us
    pallas_call x2, Pallas kernels, update(): pl.pallas_call(body, in_specs=[SMEM, HBM if held is None else VMEM, VMEM]...  7.35 us
    all_to_all x1, starting transfers between devices, body(): weights = lax.all_to_all(weights, 'pcol', 0, 0, tiled=True)  6.66 us
    pallas_call x1, Pallas kernels, keep_column(): pl.pallas_call(body, in_specs=[SMEM, HBM], out_specs=HBM, out_shape=jax.S...  5.7 us
    pallas_call x1, Pallas kernels, factor(): pl.pallas_call(body, in_specs=[SMEM] + [VMEM] * 4, out_specs=[VMEM] * 3,...  5.23 us
    pallas_call x2, Pallas kernels, pair_up(): pl.pallas_call(body, in_specs=[SMEM, HBM, VMEM], out_specs=[ANY] * count,...  5.01 us
  transfers between devices with their start and end apart: 20, of which 7 were waited for; matrix products, arithmetic and copies ran while one was open for 2% of the time, Pallas kernels for 20%

profile of v6, /device:TPU:1, one launch (start us, length us, event | category | flops | bytes accessed | tf_op | source)
XLA Modules:
  0.0 88.1 jit_solution(4331213206834618402)
XLA Ops:
  0.1 2.5 %cast_half.1 = bf16[6144,128]{1,0:T(8,128)(2,1)S(1)} custom-call(s32[2]{0:T(128)S(1)} %pad_add_fusion.1.place_ref, f32[12288,256]{1,0:T(8,128)} %source_ref.1), custom_call_target="tpu_custom_call" | custom-call | bytes 7000000 | tf_op jit(solution)/shard_map/cast_half/pallas_call | solution.py:78
  2.6 1.5 %collective-permute-start.1 = (bf16[6144,128]{1,0:T(8,128)(2,1)S(1)}, bf16[6144,128]{1,0:T(8,128)(2,1)S(1)}, u32[]{:S(2)}, u32[]{:S(2)}) collective-permute-start(bf16[6144,128]{1,0:T(8,128)(2,1)S(1)} %cast_half.1), channel_id=1, source_target_pairs={{0,16},{16,0},{32,48},{48,32},{64,80},{80,64},{96,112},{112,96},{1... | collective-permute-start | bytes 4718600 | tf_op jit(solution)/shard_map/ppermute | solution.py:439
  7.2 3.2 %pair_up.2 = (bf16[3072,128]{1,0:T(8,128)(2,1)}, bf16[3072,128]{1,0:T(8,128)(2,1)}, bf16[3072,128]{1,0:T(8,128)(2,1)}) custom-call(s32[2]{0:T(128)S(1)} %pad_add_fusion.place_ref, f32[12288,256]{1,0:T(8,128)} %source_ref.1, bf16[6144,128]{1,0:T(8,128)(2,1)S(1)} %collective-permute-done.1.partners_ref), custom_call_target="tpu_custom_call" | custom-call | bytes 7700000 | tf_op jit(solution)/shard_map/pair_up/pallas_call | solution.py:108
  10.4 1.4 %collective-permute-start.2 = (bf16[3072,128]{1,0:T(8,128)(2,1)}, bf16[3072,128]{1,0:T(8,128)(2,1)S(1)}, u32[]{:S(2)}, u32[]{:S(2)}) collective-permute-start(bf16[3072,128]{1,0:T(8,128)(2,1)} %get-tuple-element.54), channel_id=1, source_target_pairs={{0,4},{1,5},{2,6},{3,7},{4,8},{5,9},{6,10},{7,11},{8,12},{9,13},{1... | collective-permute-start | bytes 2359304 | tf_op jit(solution)/shard_map/ppermute | solution.py:404
  11.9 1.5 %collective-permute-start.3 = (bf16[3072,128]{1,0:T(8,128)(2,1)}, bf16[3072,128]{1,0:T(8,128)(2,1)S(1)}, u32[]{:S(2)}, u32[]{:S(2)}) collective-permute-start(bf16[3072,128]{1,0:T(8,128)(2,1)} %get-tuple-element.55), channel_id=1, source_target_pairs={{0,12},{1,13},{2,14},{3,15},{4,0},{5,1},{6,2},{7,3},{8,4},{9,5},{1... | collective-permute-start | bytes 2359304 | tf_op jit(solution)/shard_map/ppermute | solution.py:404
  13.4 1.6 %collective-permute-start.4 = (bf16[3072,128]{1,0:T(8,128)(2,1)}, bf16[3072,128]{1,0:T(8,128)(2,1)}, u32[]{:S(2)}, u32[]{:S(2)}) collective-permute-start(bf16[3072,128]{1,0:T(8,128)(2,1)} %get-tuple-element.56), channel_id=1, source_target_pairs={{0,8},{1,9},{2,10},{3,11},{4,12},{5,13},{6,14},{7,15},{8,0},{9,1},... | collective-permute-start | bytes 2359304 | tf_op jit(solution)/shard_map/ppermute | solution.py:404
  15.0 2.5 %collective-permute-start.5 = (bf16[768,128]{1,0:T(8,128)(2,1)S(1)}, bf16[768,128]{1,0:T(8,128)(2,1)S(1)}, u32[]{:S(2)}, u32[]{:S(2)}) collective-permute-start(bf16[768,128]{1,0:T(8,128)(2,1)S(1)} %maximum_select_fusion.refs_0_), channel_id=1, source_target_pairs={{0,32},{16,112},{32,64},{48,16},{64,96},{80,48},{96,0},{112,80},{1... | collective-permute-start | bytes 589832 | tf_op jit(solution)/shard_map/ppermute | solution.py:412
  18.1 5.7 %keep_column.1._ = f32[12288,256]{1,0:T(8,128)} custom-call(s32[5]{0:T(128)S(1)} %stack.82.s_ref, f32[12288,256]{1,0:T(8,128)} %source_ref.1), custom_call_target="tpu_custom_call" | custom-call | bytes 19250000 | tf_op jit(solution)/shard_map/keep_column/pallas_call | solution.py:258
  23.8 1.8 %pair_up.3.refs_0_ = bf16[3072,128]{1,0:T(8,128)(2,1)S(1)} custom-call(s32[2]{0:T(128)S(1)} %pad_add_fusion.place_ref, f32[12288,256]{1,0:T(8,128)} %source_ref.1, bf16[6144,128]{1,0:T(8,128)(2,1)S(1)} %collective-permute-done.1.partners_ref), custom_call_target="tpu_custom_call" | custom-call | bytes 4900000 | tf_op jit(solution)/shard_map/pair_up/pallas_call | solution.py:108
  25.7 5.4 %collective-permute-done.3.refs_2_ = bf16[3072,128]{1,0:T(8,128)(2,1)S(1)} collective-permute-done((bf16[3072,128]{1,0:T(8,128)(2,1)}, bf16[3072,128]{1,0:T(8,128)(2,1)S(1)}, u32[]{:S(2)}, u32[]{:S(2)}) %collective-permute-start.3) | collective-permute-done | bytes 786464 | tf_op jit(solution)/shard_map/ppermute | solution.py:404
  31.1 1.8 %collective-permute-done.4.refs_3_ = bf16[3072,128]{1,0:T(8,128)(2,1)} collective-permute-done((bf16[3072,128]{1,0:T(8,128)(2,1)}, bf16[3072,128]{1,0:T(8,128)(2,1)}, u32[]{:S(2)}, u32[]{:S(2)}) %collective-permute-start.4) | collective-permute-done | bytes 786464 | tf_op jit(solution)/shard_map/ppermute | solution.py:404
  34.1 2.3 %collective-permute-start.7 = (bf16[1152,128]{1,0:T(8,128)(2,1)S(1)}, bf16[1152,128]{1,0:T(8,128)(2,1)S(1)}, u32[]{:S(2)}, u32[]{:S(2)}) collective-permute-start(bf16[1152,128]{1,0:T(8,128)(2,1)S(1)} %pad_maximum_fusion), channel_id=1, source_target_pairs={{0,16},{16,0},{32,48},{48,32},{64,80},{80,64},{96,112},{112,96},{1... | collective-permute-start | bytes 884744 | tf_op jit(solution)/shard_map/ppermute | solution.py:417
  37.8 1.6 %collective-permute-start.9 = (bf16[3072,128]{1,0:T(8,128)(2,1)S(1)}, bf16[3072,128]{1,0:T(8,128)(2,1)S(1)}, u32[]{:S(2)}, u32[]{:S(2)}) collective-permute-start(bf16[3072,128]{1,0:T(8,128)(2,1)S(1)} %take.1), channel_id=1, source_target_pairs={{0,3},{1,0},{2,1},{3,2},{4,7},{5,4},{6,5},{7,6},{8,11},{9,8},{10,9... | collective-permute-start | bytes 2359304 | tf_op jit(solution)/shard_map/ppermute | solution.py:404
  39.5 5.2 %factor.1 = (f32[128,128]{1,0:T(8,128)S(1)}, f32[128,128]{1,0:T(8,128)S(1)}, bf16[1024,128]{1,0:T(8,128)(2,1)}) custom-call(s32[34]{0:T(128)S(1)} %pad_add_fusion.2.places_ref, bf16[768,128]{1,0:T(8,128)(2,1)S(1)} %maximum_select_fusion.refs_0_, bf16[768,128]{1,0:T(8,128)(2,1)S(1)} %get-tuple-element.94.refs_1_, ...), custom_call_target="tpu_custom_call" | custom-call | bytes 35000000 | tf_op jit(solution)/shard_map/factor/pallas_call | solution.py:218
  45.0 6.7 %all-to-all-start = ((bf16[16,64,128]{2,1,0:T(8,128)(2,1)}), bf16[16,64,128]{2,1,0:T(8,128)(2,1)S(1)}, u32[]{:S(2)}, u32[]{:S(2)}) async-start(bf16[16,64,128]{2,1,0:T(8,128)(2,1)} %bitcast.16), calls=%async_computation | async-start | bytes 524288 | tf_op jit(solution)/shard_map/all_to_all | solution.py:463
  52.4 9.9 %all-to-all-done = bf16[16,64,128]{2,1,0:T(8,128)(2,1)S(1)} async-done(((bf16[16,64,128]{2,1,0:T(8,128)(2,1)}), bf16[16,64,128]{2,1,0:T(8,128)(2,1)S(1)}, u32[]{:S(2)}, u32[]{:S(2)}) %all-to-all-start) | async-done | bytes 262176 | tf_op jit(solution)/shard_map/all_to_all | solution.py:463
  62.5 1.4 %collective-permute-start.14 = (bf16[1536,128]{1,0:T(8,128)(2,1)S(1)}, bf16[1536,128]{1,0:T(8,128)(2,1)S(1)}, u32[]{:S(2)}, u32[]{:S(2)}) collective-permute-start(bf16[1536,128]{1,0:T(8,128)(2,1)S(1)} %get-tuple-element.91), channel_id=1, source_target_pairs={{0,16},{16,0},{32,48},{48,32},{64,80},{80,64},{96,112},{112,96},{1... | collective-permute-start | bytes 1179656 | tf_op jit(solution)/shard_map/ppermute | solution.py:470
  65.1 1.5 %collective-permute-start.12 = (bf16[1536,128]{1,0:T(8,128)(2,1)S(1)}, bf16[1536,128]{1,0:T(8,128)(2,1)S(1)}, u32[]{:S(2)}, u32[]{:S(2)}) collective-permute-start(bf16[1536,128]{1,0:T(8,128)(2,1)S(1)} %get-tuple-element.92.refs_0_), channel_id=1, source_target_pairs={{0,12},{1,13},{2,14},{3,15},{4,0},{5,1},{6,2},{7,3},{8,4},{9,5},{1... | collective-permute-start | bytes 1179656 | tf_op jit(solution)/shard_map/ppermute | solution.py:404
  68.3 1.6 %collective-permute-start.16 = (bf16[1536,128]{1,0:T(8,128)(2,1)S(1)}, bf16[1536,128]{1,0:T(8,128)(2,1)S(1)}, u32[]{:S(2)}, u32[]{:S(2)}) collective-permute-start(bf16[1536,128]{1,0:T(8,128)(2,1)S(1)} %collective-permute-done.14.refs_1_), channel_id=1, source_target_pairs={{0,3},{1,0},{2,1},{3,2},{4,7},{5,4},{6,5},{7,6},{8,11},{9,8},{10,9... | collective-permute-start | bytes 1179656 | tf_op jit(solution)/shard_map/ppermute | solution.py:404
  70.0 2.1 %collective-permute-done.11.refs_0_ = bf16[1536,128]{1,0:T(8,128)(2,1)S(1)} collective-permute-done((bf16[1536,128]{1,0:T(8,128)(2,1)S(1)}, bf16[1536,128]{1,0:T(8,128)(2,1)S(1)}, u32[]{:S(2)}, u32[]{:S(2)}) %collective-permute-start.11) | collective-permute-done | bytes 393248 | tf_op jit(solution)/shard_map/ppermute | solution.py:404
  73.5 4.2 %update.2 = (f32[12288,256]{1,0:T(8,128)}, f32[6,1536,128]{2,1,0:T(8,128)S(1)}) custom-call(s32[13]{0:T(128)S(1)} %concatenate.39.s_ref, f32[12288,256]{1,0:T(8,128)} %source_ref.1, bf16[128,128]{1,0:T(8,128)(2,1)S(1)} %maximum_select_fusion.2.weight_ref, bf16[1536,128]{1,0:T(8,128)(2,1)S(1)} %get-tuple-element.92.refs_0_, ...), custom_call_target="tpu_custom_call", output_to_operand_aliasing={{0}: (5, {})} | custom-call | bytes 9100000 | tf_op jit(solution)/shard_map/update/pallas_call | solution.py:380
  77.7 2.6 %collective-permute-done.13.refs_2_ = bf16[1536,128]{1,0:T(8,128)(2,1)S(1)} collective-permute-done((bf16[1536,128]{1,0:T(8,128)(2,1)S(1)}, bf16[1536,128]{1,0:T(8,128)(2,1)S(1)}, u32[]{:S(2)}, u32[]{:S(2)}) %collective-permute-start.13) | collective-permute-done | bytes 393248 | tf_op jit(solution)/shard_map/ppermute | solution.py:404
  80.3 4.6 %collective-permute-done.15.refs_3_ = bf16[1536,128]{1,0:T(8,128)(2,1)S(1)} collective-permute-done((bf16[1536,128]{1,0:T(8,128)(2,1)S(1)}, bf16[1536,128]{1,0:T(8,128)(2,1)S(1)}, u32[]{:S(2)}, u32[]{:S(2)}) %collective-permute-start.15) | collective-permute-done | bytes 393248 | tf_op jit(solution)/shard_map/ppermute | solution.py:404
  84.9 3.2 %update.3 = f32[12288,256]{1,0:T(8,128)} custom-call(s32[11]{0:T(128)S(1)} %concatenate.32.s_ref, f32[6,1536,128]{2,1,0:T(8,128)S(1)} %get-tuple-element.83.source_ref, bf16[128,128]{1,0:T(8,128)(2,1)S(1)} %maximum_select_fusion.2.weight_ref, bf16[1536,128]{1,0:T(8,128)(2,1)S(1)} %collective-permute-done.11.refs_0_, ...), custom_call_target="tpu_custom_call", output_to_operand_aliasing={{}: (9, {})} | custom-call | bytes 20300000 | tf_op jit(solution)/shard_map/update/pallas_call | solution.py:380
  (45 shorter events, 11.3 us)
Async XLA Ops:
  2.6 4.7 %collective-permute-start.1 = (bf16[6144,128]{1,0:T(8,128)(2,1)S(1)}, bf16[6144,128]{1,0:T(8,128)(2,1)S(1)}, u32[]{:S(2)}, u32[]{:S(2)}) collective-permute-start(bf16[6144,128]{1,0:T(8,128)(2,1)S(1)} %cast_half.1), channel_id=1, source_target_pairs={{0,16},{16,0},{32,48},{48,32},{64,80},{80,64},{96,112},{112,96},{1... | collective-permute-start | bytes 4718600 | tf_op jit(solution)/shard_map/ppermute | solution.py:439
  5.7 1.5 %collective-permute-start = (bf16[384,128]{1,0:T(8,128)(2,1)S(1)}, bf16[384,128]{1,0:T(8,128)(2,1)S(1)}, u32[]{:S(2)}, u32[]{:S(2)}) collective-permute-start(bf16[384,128]{1,0:T(8,128)(2,1)S(1)} %dynamic-slice_convert_fusion), channel_id=1, source_target_pairs={{0,16},{16,0},{32,48},{48,32},{64,80},{80,64},{96,112},{112,96},{1... | collective-permute-start | bytes 294920 | tf_op jit(solution)/shard_map/ppermute | solution.py:441
  10.4 15.3 %collective-permute-start.2 = (bf16[3072,128]{1,0:T(8,128)(2,1)}, bf16[3072,128]{1,0:T(8,128)(2,1)S(1)}, u32[]{:S(2)}, u32[]{:S(2)}) collective-permute-start(bf16[3072,128]{1,0:T(8,128)(2,1)} %get-tuple-element.54), channel_id=1, source_target_pairs={{0,4},{1,5},{2,6},{3,7},{4,8},{5,9},{6,10},{7,11},{8,12},{9,13},{1... | collective-permute-start | bytes 2359304 | tf_op jit(solution)/shard_map/ppermute | solution.py:404
  11.9 19.2 %collective-permute-start.3 = (bf16[3072,128]{1,0:T(8,128)(2,1)}, bf16[3072,128]{1,0:T(8,128)(2,1)S(1)}, u32[]{:S(2)}, u32[]{:S(2)}) collective-permute-start(bf16[3072,128]{1,0:T(8,128)(2,1)} %get-tuple-element.55), channel_id=1, source_target_pairs={{0,12},{1,13},{2,14},{3,15},{4,0},{5,1},{6,2},{7,3},{8,4},{9,5},{1... | collective-permute-start | bytes 2359304 | tf_op jit(solution)/shard_map/ppermute | solution.py:404
  13.4 19.5 %collective-permute-start.4 = (bf16[3072,128]{1,0:T(8,128)(2,1)}, bf16[3072,128]{1,0:T(8,128)(2,1)}, u32[]{:S(2)}, u32[]{:S(2)}) collective-permute-start(bf16[3072,128]{1,0:T(8,128)(2,1)} %get-tuple-element.56), channel_id=1, source_target_pairs={{0,8},{1,9},{2,10},{3,11},{4,12},{5,13},{6,14},{7,15},{8,0},{9,1},... | collective-permute-start | bytes 2359304 | tf_op jit(solution)/shard_map/ppermute | solution.py:404
  15.0 10.6 %collective-permute-start.5 = (bf16[768,128]{1,0:T(8,128)(2,1)S(1)}, bf16[768,128]{1,0:T(8,128)(2,1)S(1)}, u32[]{:S(2)}, u32[]{:S(2)}) collective-permute-start(bf16[768,128]{1,0:T(8,128)(2,1)S(1)} %maximum_select_fusion.refs_0_), channel_id=1, source_target_pairs={{0,32},{16,112},{32,64},{48,16},{64,96},{80,48},{96,0},{112,80},{1... | collective-permute-start | bytes 589832 | tf_op jit(solution)/shard_map/ppermute | solution.py:412
  17.6 8.1 %collective-permute-start.6 = (bf16[384,128]{1,0:T(8,128)(2,1)S(1)}, bf16[384,128]{1,0:T(8,128)(2,1)S(1)}, u32[]{:S(2)}, u32[]{:S(2)}) collective-permute-start(bf16[384,128]{1,0:T(8,128)(2,1)S(1)} %dynamic-slice_convert_fusion), channel_id=1, source_target_pairs={{0,64},{16,80},{32,96},{48,112},{64,0},{80,16},{96,32},{112,48},{1... | collective-permute-start | bytes 294920 | tf_op jit(solution)/shard_map/ppermute | solution.py:412
  34.1 5.3 %collective-permute-start.7 = (bf16[1152,128]{1,0:T(8,128)(2,1)S(1)}, bf16[1152,128]{1,0:T(8,128)(2,1)S(1)}, u32[]{:S(2)}, u32[]{:S(2)}) collective-permute-start(bf16[1152,128]{1,0:T(8,128)(2,1)S(1)} %pad_maximum_fusion), channel_id=1, source_target_pairs={{0,16},{16,0},{32,48},{48,32},{64,80},{80,64},{96,112},{112,96},{1... | collective-permute-start | bytes 884744 | tf_op jit(solution)/shard_map/ppermute | solution.py:417
  36.6 25.6 %collective-permute-start.10 = (bf16[3072,128]{1,0:T(8,128)(2,1)S(1)}, bf16[3072,128]{1,0:T(8,128)(2,1)S(1)}, u32[]{:S(2)}, u32[]{:S(2)}) collective-permute-start(bf16[3072,128]{1,0:T(8,128)(2,1)S(1)} %take.1), channel_id=1, source_target_pairs={{0,1},{1,2},{2,3},{3,0},{4,5},{5,6},{6,7},{7,4},{8,9},{9,10},{10,1... | collective-permute-start | bytes 2359304 | tf_op jit(solution)/shard_map/ppermute | solution.py:404
  37.8 24.5 %collective-permute-start.9 = (bf16[3072,128]{1,0:T(8,128)(2,1)S(1)}, bf16[3072,128]{1,0:T(8,128)(2,1)S(1)}, u32[]{:S(2)}, u32[]{:S(2)}) collective-permute-start(bf16[3072,128]{1,0:T(8,128)(2,1)S(1)} %take.1), channel_id=1, source_target_pairs={{0,3},{1,0},{2,1},{3,2},{4,7},{5,4},{6,5},{7,6},{8,11},{9,8},{10,9... | collective-permute-start | bytes 2359304 | tf_op jit(solution)/shard_map/ppermute | solution.py:404
  44.7 17.6 %collective-permute-start.8 = (bf16[3072,128]{1,0:T(8,128)(2,1)S(1)}, bf16[3072,128]{1,0:T(8,128)(2,1)S(1)}, u32[]{:S(2)}, u32[]{:S(2)}) collective-permute-start(bf16[3072,128]{1,0:T(8,128)(2,1)S(1)} %take.1), channel_id=1, source_target_pairs={{0,2},{1,3},{2,0},{3,1},{4,6},{5,7},{6,4},{7,5},{8,10},{9,11},{10,... | collective-permute-start | bytes 2359304 | tf_op jit(solution)/shard_map/ppermute | solution.py:404
  45.0 17.2 %all-to-all-start = ((bf16[16,64,128]{2,1,0:T(8,128)(2,1)}), bf16[16,64,128]{2,1,0:T(8,128)(2,1)S(1)}, u32[]{:S(2)}, u32[]{:S(2)}) async-start(bf16[16,64,128]{2,1,0:T(8,128)(2,1)} %bitcast.16), calls=%async_computation | async-start | bytes 524288 | tf_op jit(solution)/shard_map/all_to_all | solution.py:463
  62.5 4.7 %collective-permute-start.14 = (bf16[1536,128]{1,0:T(8,128)(2,1)S(1)}, bf16[1536,128]{1,0:T(8,128)(2,1)S(1)}, u32[]{:S(2)}, u32[]{:S(2)}) collective-permute-start(bf16[1536,128]{1,0:T(8,128)(2,1)S(1)} %get-tuple-element.91), channel_id=1, source_target_pairs={{0,16},{16,0},{32,48},{48,32},{64,80},{80,64},{96,112},{112,96},{1... | collective-permute-start | bytes 1179656 | tf_op jit(solution)/shard_map/ppermute | solution.py:470
  63.9 8.1 %collective-permute-start.11 = (bf16[1536,128]{1,0:T(8,128)(2,1)S(1)}, bf16[1536,128]{1,0:T(8,128)(2,1)S(1)}, u32[]{:S(2)}, u32[]{:S(2)}) collective-permute-start(bf16[1536,128]{1,0:T(8,128)(2,1)S(1)} %get-tuple-element.92.refs_0_), channel_id=1, source_target_pairs={{0,4},{1,5},{2,6},{3,7},{4,8},{5,9},{6,10},{7,11},{8,12},{9,13},{1... | collective-permute-start | bytes 1179656 | tf_op jit(solution)/shard_map/ppermute | solution.py:404
  65.1 3.3 %collective-permute-start.18 = (bf16[64,128]{1,0:T(8,128)(2,1)S(1)}, bf16[64,128]{1,0:T(8,128)(2,1)S(1)}, u32[]{:S(2)}, u32[]{:S(2)}) collective-permute-start(bf16[64,128]{1,0:T(8,128)(2,1)S(1)} %constant_dynamic-slice_fusion), channel_id=1, source_target_pairs={{0,16},{16,0},{32,48},{48,32},{64,80},{80,64},{96,112},{112,96},{1... | collective-permute-start | bytes 49160 | tf_op jit(solution)/shard_map/ppermute | solution.py:476
  65.1 12.6 %collective-permute-start.12 = (bf16[1536,128]{1,0:T(8,128)(2,1)S(1)}, bf16[1536,128]{1,0:T(8,128)(2,1)S(1)}, u32[]{:S(2)}, u32[]{:S(2)}) collective-permute-start(bf16[1536,128]{1,0:T(8,128)(2,1)S(1)} %get-tuple-element.92.refs_0_), channel_id=1, source_target_pairs={{0,12},{1,13},{2,14},{3,15},{4,0},{5,1},{6,2},{7,3},{8,4},{9,5},{1... | collective-permute-start | bytes 1179656 | tf_op jit(solution)/shard_map/ppermute | solution.py:404
  66.6 13.7 %collective-permute-start.13 = (bf16[1536,128]{1,0:T(8,128)(2,1)S(1)}, bf16[1536,128]{1,0:T(8,128)(2,1)S(1)}, u32[]{:S(2)}, u32[]{:S(2)}) collective-permute-start(bf16[1536,128]{1,0:T(8,128)(2,1)S(1)} %get-tuple-element.92.refs_0_), channel_id=1, source_target_pairs={{0,8},{1,9},{2,10},{3,11},{4,12},{5,13},{6,14},{7,15},{8,0},{9,1},... | collective-permute-start | bytes 1179656 | tf_op jit(solution)/shard_map/ppermute | solution.py:404
  67.2 17.7 %collective-permute-start.15 = (bf16[1536,128]{1,0:T(8,128)(2,1)S(1)}, bf16[1536,128]{1,0:T(8,128)(2,1)S(1)}, u32[]{:S(2)}, u32[]{:S(2)}) collective-permute-start(bf16[1536,128]{1,0:T(8,128)(2,1)S(1)} %collective-permute-done.14.refs_1_), channel_id=1, source_target_pairs={{0,1},{1,2},{2,3},{3,0},{4,5},{5,6},{6,7},{7,4},{8,9},{9,10},{10,1... | collective-permute-start | bytes 1179656 | tf_op jit(solution)/shard_map/ppermute | solution.py:404
  68.3 16.6 %collective-permute-start.16 = (bf16[1536,128]{1,0:T(8,128)(2,1)S(1)}, bf16[1536,128]{1,0:T(8,128)(2,1)S(1)}, u32[]{:S(2)}, u32[]{:S(2)}) collective-permute-start(bf16[1536,128]{1,0:T(8,128)(2,1)S(1)} %collective-permute-done.14.refs_1_), channel_id=1, source_target_pairs={{0,3},{1,0},{2,1},{3,2},{4,7},{5,4},{6,5},{7,6},{8,11},{9,8},{10,9... | collective-permute-start | bytes 1179656 | tf_op jit(solution)/shard_map/ppermute | solution.py:404
  72.0 12.9 %collective-permute-start.17 = (bf16[1536,128]{1,0:T(8,128)(2,1)S(1)}, bf16[1536,128]{1,0:T(8,128)(2,1)S(1)}, u32[]{:S(2)}, u32[]{:S(2)}) collective-permute-start(bf16[1536,128]{1,0:T(8,128)(2,1)S(1)} %collective-permute-done.14.refs_1_), channel_id=1, source_target_pairs={{0,2},{1,3},{2,0},{3,1},{4,6},{5,7},{6,4},{7,5},{8,10},{9,11},{10,... | collective-permute-start | bytes 1179656 | tf_op jit(solution)/shard_map/ppermute | solution.py:404
